TPU v7x, 256 devices: a whole 4x4x8 slice. The times are simulated.
256 devices in a mesh: rep: 16 (over z, core), tp: 16 (over x, y).
Axes of the slice: x: 4, y: 4, z: 8, core: 2. Of those that a mesh axis runs over, the one named last changes fastest.
Arguments:
- tokens: bfloat16 [16, 3072, 4096], P('rep', 'tp'), may hold values from -6 to 6
- out_grad: bfloat16 [16, 3072, 2048], P('rep', None, 'tp'), may hold values from -0.109375 to 0.109375
- weights: float32 [2048, 4096], P('tp'), may hold values from -6 to 6
- moment_one: bfloat16 [16, 2048, 4096], P('rep', 'tp'), may hold values from -3 to 3
- moment_two: bfloat16 [16, 2048, 4096], P('rep', 'tp'), may hold values from 0.0019989014 to 0.019897461
- error_buf: bfloat16 [16, 2048, 4096], P('rep', 'tp'), may hold values from -6 to 6
- momentum: bfloat16 [2048, 4096], P('tp'), may hold values from -6 to 6
- tile_lists: int32 [16, 16, 4], P('rep', 'tp'), may hold values from -1 to 31, as said below
Outputs:
- weights_new: float32 [2048, 4096], P('tp')
- error_new: bfloat16 [16, 2048, 4096], P('rep', 'tp')
- momentum_new: bfloat16 [2048, 4096], P('tp')
Inputs may be any that keep to these rules, and one draw needn't show every extreme that they name: Each list tile_lists[r, j] holds between 0 and 4 distinct tile numbers below 32 in its first slots and -1 in the rest; in every replica some list holds exactly 4; the number of listed tiles may differ from list to list.
All inputs are finite; a program needn't handle non-finite values.
Results may differ from a plain program's by a relative error of at most 0.0065.
Values may be sent and summed in bfloat16 or wider, within the bound.
No kernel may reach another device: no remote copies, remote signals or barrier semaphores. Data moves between devices by JAX's collectives and lax.ppermute only.
A program may use at most 128 MiB of HBM per device.

v0:
```python
import jax
import jax.numpy as jnp
from jax import lax
from jax.sharding import PartitionSpec as P

TILE = 128


def per_device(tokens, out_grad, weights, moment_one, moment_two, error_buf, momentum, tile_lists):
    local_rows = tokens[0]
    local_grad = out_grad[0]
    columns = weights.shape[0]
    features = weights.shape[1]
    col_blocks = columns // TILE
    feat_blocks = features // TILE
    tiles_here = col_blocks * feat_blocks
    contract = (((0,), (0,)), ((), ()))
    gradient = lax.dot_general(
        local_grad,
        lax.all_gather(local_rows, "tp", axis=0, tiled=True),
        contract,
        preferred_element_type=jnp.float32,
    )
    corr_one = 1.0 - 0.8**20
    corr_two = 1.0 - 0.99**20
    first = 0.8 * moment_one[0].astype(jnp.float32) + 0.2 * gradient
    second = 0.99 * moment_two[0].astype(jnp.float32) + 0.01 * gradient * gradient
    delta = 0.5 * (first / corr_one / (jnp.sqrt(second / corr_two) + 1e-08) + 0.1 * weights)
    accrued = 0.95 * error_buf[0].astype(jnp.float32) + delta
    tile_ids = tile_lists[0, 0]
    tile_grid = jnp.arange(tiles_here, dtype=jnp.int32)
    chosen = jnp.any(tile_ids[:, None] == tile_grid[None, :], axis=0).reshape(
        col_blocks, 1, feat_blocks, 1
    )
    tile_mask = jnp.broadcast_to(chosen, (col_blocks, TILE, feat_blocks, TILE)).reshape(
        columns, features
    )
    rounded = accrued.astype(jnp.bfloat16)
    error_new = jnp.where(tile_mask, 0.0, accrued).astype(jnp.bfloat16)
    contrib = jnp.where(tile_mask, rounded.astype(jnp.float32), 0.0)
    summed = lax.psum(contrib.astype(jnp.bfloat16), "rep").astype(jnp.float32)
    aggregate = summed / lax.axis_size("rep")
    velocity = 0.9 * momentum.astype(jnp.float32) + aggregate
    weights_new = weights - 0.7 * (aggregate + 0.9 * velocity)
    return (weights_new, error_new[None], velocity.astype(jnp.bfloat16))


def solution(mesh):
    return jax.shard_map(
        per_device,
        mesh=mesh,
        in_specs=(
            P("rep", "tp", None),
            P("rep", None, "tp"),
            P("tp", None),
            P("rep", "tp", None),
            P("rep", "tp", None),
            P("rep", "tp", None),
            P("tp", None),
            P("rep", "tp", None),
        ),
        out_specs=(P("tp", None), P("rep", "tp", None), P("tp", None)),
        check_vma=False,
    )
```

profile of v0, /device:TPU:1, one launch (start us, length us, event | category | flops | bytes accessed | tf_op | source)
XLA Modules:
  0.0 311.9 jit_solution(2641603119455546966)
XLA Ops:
  7.2 0.0 copy-start
  7.2 0.0 all-gather.3.cloned.1.call-start
  7.2 0.7 all-gather.3.cloned.1.call-update
  7.9 0.0 all-reduce.2.cloned.1.call-start
  8.0 0.7 fusion.14
  8.7 0.1 broadcast_bitcast_fusion
  8.8 164.7 %all-gather.3.cloned.1.call-done = bf16[1,3072,4096]{2,1,0:T(8,128)(2,1)} async-done(((bf16[1,192,4096]{2,1,0:T(8,128)(2,1)}), bf16[1,3072,4096]{2,1,0:T(8,128)(2,1)}) %all-gather.3.cloned.1.call-update) | async-done | bytes 25165840 | tf_op jit(solution)/shard_map/all_gather | solution.py:20
  173.5 0.0 copy-done
  173.5 16.3 %select_convert_fusion.1 = (bf16[128,4096]{1,0:T(8,128)(2,1)}, bf16[128,4096]{1,0:T(8,128)(2,1)}) fusion(pred[4096]{0:T(1024)(128)(4,1)S(1)} %broadcast_bitcast_fusion, f32[128,4096]{1,0:T(8,128)} %param.10, bf16[1,128,4096]{2,1,0:T(8,128)(2,1)} %param.12, bf16[1,3072,4096]{2,1,0:T(8,128)(2,1)} %all-gather.3.cloned.1.call-done, ...), kind=kOutput, calls=%fused_computation.17 | convolution fusion | flops 3233284096 | bytes 33296384 | tf_op jit(solution)/shard_map/dot_general | solution.py:18
  189.8 0.0 copy-start.1
  189.8 0.0 all-reduce.2.cloned.1.call-update
  189.9 2.6 fusion.12
  192.4 108.8 %all-reduce.2.cloned.1.call-done = bf16[128,4096]{1,0:T(8,128)(2,1)} async-done(((bf16[128,4096]{1,0:T(8,128)(2,1)}), bf16[128,4096]{1,0:T(8,128)(2,1)}) %all-reduce.2.cloned.1.call-update) | async-done | bytes 1048592 | tf_op jit(solution)/shard_map/psum | solution.py:41
  301.2 0.0 copy-done.1
  301.2 3.9 %fusion.9 = (bf16[128,4096]{1,0:T(8,128)(2,1)}, f32[128,4096]{1,0:T(8,128)}) fusion(bf16[128,4096]{1,0:T(8,128)(2,1)} %param.14, bf16[128,4096]{1,0:T(8,128)(2,1)} %all-reduce.2.cloned.1.call-done, f32[128,4096]{1,0:T(8,128)S(1)} %copy-done.1), kind=kLoop, calls=%fused_computation.15 | loop fusion | flops 5242880 | bytes 7340032 | tf_op jit(solution)/shard_map/convert_element_type | solution.py:45
Async XLA Ops:
  7.2 166.4 %copy-start = (bf16[1,3072,128]{2,1,0:T(8,128)(2,1)S(1)}, bf16[1,3072,128]{2,1,0:T(8,128)(2,1)}, u32[]{:S(2)}) copy-start(bf16[1,3072,128]{2,1,0:T(8,128)(2,1)} %param.9) | copy-start | bytes 2359300
  7.2 166.3 %all-gather.3.cloned.1.call-start = ((), (), s32[]{:S(2)}) async-start(), calls=%async_computation.1 | async-start | bytes 26738688 | tf_op jit(solution)/shard_map/all_gather | solution.py:20
  7.9 293.3 %all-reduce.2.cloned.1.call-start = ((), (), s32[]{:S(2)}) async-start(), calls=%async_computation | async-start | bytes 2097152 | tf_op jit(solution)/shard_map/psum | solution.py:41
  189.8 111.4 %copy-start.1 = (f32[128,4096]{1,0:T(8,128)S(1)}, f32[128,4096]{1,0:T(8,128)}, u32[]{:S(2)}) copy-start(f32[128,4096]{1,0:T(8,128)} %param.10) | copy-start | bytes 6291460
Sparse Core Ops, SparseCore 0:
  10.5 162.9 all-gather.2
  190.0 111.1 all-reduce.1
where the time goes:
time: 312 us
  waiting for transfers between devices  274 us (88%)
  matrix products  16.3 us (5%)
  between operations  14 us (4%)
  other arithmetic  7.17 us (2%)
    all_gather x1, waiting for transfers between devices, per_device(): lax.all_gather(local_rows, 'tp', axis=0, tiled=True)  165 us
    psum x1, waiting for transfers between devices, per_device(): summed = lax.psum(contrib.astype(jnp.bfloat16), 'rep').astype(jnp.float32)  109 us
    dot_general x1, matrix products, per_device(): lax.dot_general(local_grad, lax.all_gather(local_rows, 'tp', axis=0, tile...  16.3 us
  transfers between devices with their start and end apart: 2, of which 2 were waited for; matrix products, arithmetic and copies ran while one was open for 1% of the time, Pallas kernels for 0%

commit v1 on v0

v1 whole, which is shorter than its diff:
```python
import functools

import jax
import jax.numpy as jnp
from jax import lax
from jax.experimental import pallas as pl
from jax.experimental.pallas import tpu as pltpu
from jax.sharding import PartitionSpec as P

N = 4
ROWS = 192
HALF = 2048
COLS = 128
TILE = 128
FEATS = 4096
SLOTS = 4
PIECE = SLOTS * 64 + 16
BF = jnp.bfloat16
F32 = jnp.float32
VMEM_CAP = 40 * 1024 * 1024


def along_x(v, s):
    return lax.ppermute(v, "tp", [(N * a + b, N * ((a + s) % N) + b) for a in range(N) for b in range(N)])


def along_y(v, s):
    return lax.ppermute(v, "tp", [(N * a + b, N * a + (b + s) % N) for a in range(N) for b in range(N)])


def along_z(v, s):
    return lax.ppermute(v, "rep", [(2 * a + c, 2 * ((a + s) % 8) + c) for a in range(8) for c in range(2)])


def across(v):
    return lax.ppermute(v, "rep", [(2 * a + c, 2 * a + 1 - c) for a in range(8) for c in range(2)])


def pack(pos, tokens, og4, part, shift):
    alone = part >= 2
    base = 0 if alone else HALF
    by_y = part % 2 == 0

    def kernel(pos_ref, og_ref, *refs):
        out_ref = refs[-1]
        if not alone:
            out_ref[:, 0:HALF] = refs[0][...]
        for i in range(N):
            out_ref[:, base + COLS * i : base + COLS * (i + 1)] = og_ref[i, 0] if by_y else og_ref[0, i]

    if by_y:
        og_spec = pl.BlockSpec((N, 1, ROWS, COLS), lambda i, p: (0, lax.rem(p[1] + shift, N), 0, 0))
    else:
        og_spec = pl.BlockSpec((1, N, ROWS, COLS), lambda i, p: (lax.rem(p[0] + shift, N), 0, 0, 0))
    tok_spec = pl.BlockSpec((ROWS, HALF), lambda i, p: (0, part))
    width = base + N * COLS
    return pl.pallas_call(
        kernel,
        out_shape=jax.ShapeDtypeStruct((ROWS, width), BF),
        grid_spec=pltpu.PrefetchScalarGridSpec(
            num_scalar_prefetch=1,
            grid=(1,),
            in_specs=[og_spec] if alone else [og_spec, tok_spec],
            out_specs=pl.BlockSpec((ROWS, width), lambda i, p: (0, 0)),
        ),
        cost_estimate=pl.CostEstimate(flops=0, bytes_accessed=4 * ROWS * width, transcendentals=0),
        compiler_params=pltpu.CompilerParams(vmem_limit_bytes=VMEM_CAP),
        name="pack",
    )(pos, og4, *([] if alone else [tokens]))


def partials(pos, og4, o_from, tokens, t_from, part):
    near_o, far_o, op_o = o_from
    near_t, far_t, op1, op2 = t_from
    width = 512
    first = part * (HALF // width)

    def kernel(pos_ref, own_o, n_o, f_o, p_o, t, l, r, a, b, out0, out1, out3, out2, lhs, rhs):
        @pl.when(pl.program_id(0) == 0)
        def _():
            here = pos_ref[1 - part]
            for s, d in enumerate((0, N - 1, 1, 2)):
                k = lax.rem(here + d, N)
                rows = pl.ds(ROWS * s, ROWS)
                lhs[rows, 0:COLS] = own_o[0, k] if part == 0 else own_o[k, 0]
                lanes = pl.ds(pl.multiple_of(k * COLS, COLS), COLS)
                lhs[rows, COLS : 2 * COLS] = n_o[:, lanes]
                lhs[rows, 2 * COLS : 3 * COLS] = f_o[:, lanes]
                lhs[rows, 3 * COLS : 4 * COLS] = p_o[:, lanes]

        rhs[0:192] = t[...]
        rhs[192:384] = l[...]
        rhs[384:576] = r[...]
        rhs[576:672] = a[...]
        rhs[672:768] = b[...]
        res = lax.dot_general(lhs[...], rhs[...], (((0,), (0,)), ((), ())), preferred_element_type=F32)
        out0[...] = res[0:COLS]
        out1[...] = res[COLS : 2 * COLS].astype(BF)
        out3[...] = res[2 * COLS : 3 * COLS].astype(BF)
        out2[...] = res[3 * COLS : 4 * COLS].astype(BF)

    own_spec = (
        pl.BlockSpec((1, N, ROWS, COLS), lambda i, p: (p[0], 0, 0, 0))
        if part == 0
        else pl.BlockSpec((N, 1, ROWS, COLS), lambda i, p: (0, p[1], 0, 0))
    )
    tail = pl.BlockSpec((ROWS, 512), lambda i, p: (0, HALF // 512))
    piece = pl.BlockSpec((ROWS, 512), lambda i, p: (0, 0))
    lanes = lambda rows, off=0: pl.BlockSpec((rows, width), lambda i, p: (0, i + off))
    outs = [jax.ShapeDtypeStruct((COLS, HALF), d) for d in (F32, BF, BF, BF)]
    return pl.pallas_call(
        kernel,
        out_shape=outs,
        grid_spec=pltpu.PrefetchScalarGridSpec(
            num_scalar_prefetch=1,
            grid=(HALF // width,),
            in_specs=[own_spec, tail, tail, piece, lanes(ROWS, first), lanes(ROWS), lanes(ROWS), lanes(ROWS // 2), lanes(ROWS // 2)],
            out_specs=[lanes(COLS)] * 4,
            scratch_shapes=[pltpu.VMEM((N * ROWS, N * COLS), BF), pltpu.VMEM((N * ROWS, width), BF)],
        ),
        compiler_params=pltpu.CompilerParams(vmem_limit_bytes=VMEM_CAP),
        cost_estimate=pl.CostEstimate(flops=2 * 768 * 512 * HALF, bytes_accessed=8 << 20, transcendentals=0),
        name="partials",
    )(pos, og4, near_o, far_o, op_o, tokens, near_t, far_t, op1, op2)


def epilogue(ids, pos, grads, m1, m2, err, weights):
    width = 512
    steps = FEATS // width
    half = steps // 2
    corr_one = 1.0 - 0.8**20
    corr_two = 1.0 - 0.99**20

    def kernel(ids_ref, pos_ref, a0, a1, a2, a3, b0, b1, b2, b3, m1_ref, m2_ref, e_ref, w_ref, out, mine, other, grad):
        i = pl.program_id(0)

        @pl.when(i == 0)
        def _():
            row = lax.broadcasted_iota(jnp.int32, (16, TILE), 0)
            v = jnp.full((16, TILE), -1, jnp.int32)
            for k in range(SLOTS):
                v = jnp.where(row == k, ids_ref[k], v)
            v = v.astype(F32).astype(BF)
            for ref in (mine, other):
                ref[0 : SLOTS * 64] = jnp.zeros((SLOTS * 64, TILE), BF)
                ref[SLOTS * 64 :] = v

        @pl.when(i < half)
        def _():
            grad[...] = a0[...] + (a1[...].astype(F32) + a2[...].astype(F32)) + a3[...].astype(F32)

        @pl.when(i >= half)
        def _():
            grad[...] = b0[...] + (b1[...].astype(F32) + b2[...].astype(F32)) + b3[...].astype(F32)

        core = pos_ref[2]
        for j in range(width // TILE):
            at = slice(j * TILE, (j + 1) * TILE)
            g = grad[:, at]
            first = 0.8 * m1_ref[:, at].astype(F32) + 0.2 * g
            second = 0.99 * m2_ref[:, at].astype(F32) + 0.01 * g * g
            delta = 0.5 * (first / corr_one / (jnp.sqrt(second / corr_two) + 1e-08) + 0.1 * w_ref[:, at])
            acc = (0.95 * e_ref[:, at].astype(F32) + delta).astype(BF)
            t = i * (width // TILE) + j
            hit = (ids_ref[0] == t) | (ids_ref[1] == t) | (ids_ref[2] == t) | (ids_ref[3] == t)
            out[:, at] = acc

            @pl.when(hit)
            def _():
                out[:, at] = jnp.zeros((COLS, TILE), BF)
                for k in range(SLOTS):

                    @pl.when(ids_ref[k] == t)
                    def _():
                        top, bottom = acc[0:64], acc[64:128]

                        @pl.when(core == 0)
                        def _():
                            mine[64 * k : 64 * k + 64] = top
                            other[64 * k : 64 * k + 64] = bottom

                        @pl.when(core == 1)
                        def _():
                            mine[64 * k : 64 * k + 64] = bottom
                            other[64 * k : 64 * k + 64] = top

    blk = lambda f: pl.BlockSpec((COLS, width), f)
    a_spec = blk(lambda i, *_: (0, jnp.minimum(i, half - 1)))
    b_spec = blk(lambda i, *_: (0, jnp.maximum(i - half, 0)))
    full = blk(lambda i, *_: (0, i))
    keep = pl.BlockSpec((PIECE, TILE), lambda i, *_: (0, 0))
    return pl.pallas_call(
        kernel,
        out_shape=[
            jax.ShapeDtypeStruct((COLS, FEATS), BF),
            jax.ShapeDtypeStruct((PIECE, TILE), BF),
            jax.ShapeDtypeStruct((PIECE, TILE), BF),
        ],
        grid_spec=pltpu.PrefetchScalarGridSpec(
            num_scalar_prefetch=2,
            grid=(steps,),
            in_specs=[a_spec] * 4 + [b_spec] * 4 + [full] * 4,
            out_specs=[full, keep, keep],
            scratch_shapes=[pltpu.VMEM((COLS, width), F32)],
        ),
        compiler_params=pltpu.CompilerParams(vmem_limit_bytes=VMEM_CAP),
        cost_estimate=pl.CostEstimate(flops=20 * COLS * FEATS, bytes_accessed=10 << 20, transcendentals=0),
        name="epilogue",
    )(ids, pos, *grads, m1, m2, err, weights)


def add_tiles(ids, pieces):
    n = len(pieces)

    def kernel(ids_ref, *refs):
        ins, out, acc = refs[:n], refs[n], refs[n + 1]
        acc[...] = jnp.zeros_like(acc)
        at = 0
        for ref in ins:
            for h in range(ref.shape[0] // PIECE):
                for k in range(SLOTS):
                    t = ids_ref[at]
                    at += 1

                    @pl.when(t >= 0)
                    def _():
                        lanes = pl.ds(pl.multiple_of(t * TILE, TILE), TILE)
                        row = h * PIECE + 64 * k
                        acc[:, lanes] = acc[:, lanes] + ref[row : row + 64].astype(F32)

        out[...] = (acc[...] * (1.0 / 16.0)).astype(BF)

    whole = lambda p: pl.BlockSpec(p.shape, lambda i, *_: (0, 0))
    return pl.pallas_call(
        kernel,
        out_shape=jax.ShapeDtypeStruct((64, FEATS), BF),
        grid_spec=pltpu.PrefetchScalarGridSpec(
            num_scalar_prefetch=1,
            grid=(1,),
            in_specs=[whole(p) for p in pieces],
            out_specs=pl.BlockSpec((64, FEATS), lambda i, *_: (0, 0)),
            scratch_shapes=[pltpu.VMEM((64, FEATS), F32)],
        ),
        compiler_params=pltpu.CompilerParams(vmem_limit_bytes=VMEM_CAP),
        cost_estimate=pl.CostEstimate(flops=64 * 64 * 128, bytes_accessed=3 << 20, transcendentals=0),
        name="add_tiles",
    )(ids, *pieces)


def outer(pos, mine, other, weights, momentum):
    width = 1024

    def kernel(pos_ref, m_ref, o_ref, w_ref, v_ref, w_out, v_out):
        core = pos_ref[2]
        for h in range(2):
            rows = slice(64 * h, 64 * h + 64)
            agg = jnp.where(core == h, m_ref[...].astype(F32), o_ref[...].astype(F32))
            vel = 0.9 * v_ref[rows].astype(F32) + agg
            w_out[rows] = w_ref[rows] - 0.7 * (agg + 0.9 * vel)
            v_out[rows] = vel.astype(BF)

    part = pl.BlockSpec((64, width), lambda i, *_: (0, i))
    full = pl.BlockSpec((COLS, width), lambda i, *_: (0, i))
    return pl.pallas_call(
        kernel,
        out_shape=[jax.ShapeDtypeStruct((COLS, FEATS), F32), jax.ShapeDtypeStruct((COLS, FEATS), BF)],
        grid_spec=pltpu.PrefetchScalarGridSpec(
            num_scalar_prefetch=1,
            grid=(FEATS // width,),
            in_specs=[part, part, full, full],
            out_specs=[full, full],
        ),
        compiler_params=pltpu.CompilerParams(vmem_limit_bytes=VMEM_CAP),
        cost_estimate=pl.CostEstimate(flops=6 * COLS * FEATS, bytes_accessed=8 << 20, transcendentals=0),
        name="outer",
    )(pos, mine, other, weights, momentum)


def per_device(tokens, out_grad, weights, moment_one, moment_two, error_buf, momentum, tile_lists):
    tp = lax.axis_index("tp")
    core = lax.rem(lax.axis_index("rep"), 2)
    pos = jnp.stack([tp // N, lax.rem(tp, N), core]).astype(jnp.int32)
    tok = tokens[0]
    og4 = out_grad[0].reshape(N, N, ROWS, COLS)
    ids = tile_lists[0, 0]

    yp = along_y(pack(pos, tok, og4, 0, 1), 1)
    ym = along_y(pack(pos, tok, og4, 0, 3), 3)
    xp = along_x(pack(pos, tok, og4, 1, 1), 1)
    xm = along_x(pack(pos, tok, og4, 1, 3), 3)
    ox = along_x(pack(pos, tok, og4, 3, 2), 2)
    oy = along_y(pack(pos, tok, og4, 2, 2), 2)
    half = ROWS // 2
    y1 = along_y(yp[:half, :HALF], 1)
    y2 = along_y(ym[half:, :HALF], 3)
    x1 = along_x(xp[:half, :HALF], 1)
    x2 = along_x(xm[half:, :HALF], 3)

    pa = partials(pos, og4, (xp, xm, ox), tok, (yp, ym, y1, y2), 0)
    pb = partials(pos, og4, (yp, ym, oy), tok, (xp, xm, x1, x2), 1)
    ga = [pa[0], along_x(pa[1], 3), along_x(pa[2], 1), along_x(pa[3], 2)]
    gb = [pb[0], along_y(pb[1], 3), along_y(pb[2], 1), along_y(pb[3], 2)]

    error_new, mine, other = epilogue(ids, pos, ga + gb, moment_one[0], moment_two[0], error_buf[0], weights)

    own = jnp.concatenate([mine, across(other)])
    u1, d1 = along_z(own, 1), along_z(own, 7)
    u2, d2 = along_z(u1, 1), along_z(d1, 7)
    u3, d3 = along_z(u2, 1), along_z(d2, 7)
    u4, d4 = along_z(u3[:PIECE], 1), along_z(d3[PIECE:], 7)
    pieces = [own, u1, d1, u2, d2, u3, d3, u4, d4]
    got = [p.reshape(-1, PIECE, TILE)[:, SLOTS * 64 : SLOTS * 64 + SLOTS, 0] for p in pieces]
    got = jnp.concatenate(got).astype(jnp.int32).reshape(-1)
    agg = add_tiles(got, pieces)
    weights_new, momentum_new = outer(pos, agg, across(agg), weights, momentum)
    return (weights_new, error_new[None], momentum_new)


def solution(mesh):
    return jax.shard_map(
        per_device,
        mesh=mesh,
        in_specs=(
            P("rep", "tp", None),
            P("rep", None, "tp"),
            P("tp", None),
            P("rep", "tp", None),
            P("rep", "tp", None),
            P("rep", "tp", None),
            P("tp", None),
            P("rep", "tp", None),
        ),
        out_specs=(P("tp", None), P("rep", "tp", None), P("tp", None)),
        check_vma=False,
    )
```

time: 312 us -> 142 us (0.46)
  waiting for transfers between devices: 274 us -> 51.2 us
  starting transfers between devices: 0.08 us -> 54 us
  Pallas kernels: 0 us -> 22.6 us
  matrix products: 16.3 us -> 0 us
  between operations: 14 us -> 0.88 us
  local copies, waits for them, and re-layouts: 0.09 us -> 12.9 us
  other arithmetic: 7.17 us -> 0.08 us
    all_gather x1 -> x0, waiting for transfers between devices: 165 us -> none  [per_device(): lax.all_gather(local_rows, 'tp', axis=0, tiled=True)]
    psum x1 -> x0, waiting for transfers between devices: 109 us -> none  [per_device(): summed = lax.psum(contrib.astype(jnp.bfloat16), 'rep').astype(jnp.float32)]
    ppermute x0 -> x26, starting transfers between devices: none -> 54 us  [the longest x8 15.2 us: along_z(): lax.ppermute(v, 'rep', [(2 * a + c, 2 * ((a + s) % 8) + c) for a in range...]
    ppermute x0 -> x26, waiting for transfers between devices: none -> 51.2 us  [the longest x8 30.6 us: along_x(): lax.ppermute(v, 'tp', [(N * a + b, N * ((a + s) % N) + b) for a in range(...]
    pallas_call x0 -> x11, Pallas kernels: none -> 22.6 us  [the longest x2 7.53 us: partials(): pl.pallas_call(kernel, out_shape=outs, grid_spec=pltpu.PrefetchScalarGrid...]
    dot_general x1 -> x0, matrix products: 16.3 us -> none  [per_device(): lax.dot_general(local_grad, lax.all_gather(local_rows, 'tp', axis=0, tile...]
    unnamed x4 -> x42, local copies, waits for them, and re-layouts: 0.01 us -> 7.02 us
    slice x0 -> x13, local copies, waits for them, and re-layouts: none -> 4.14 us  [the longest x7 2.79 us: per_device(): p.reshape(-1, PIECE, TILE)[:, SLOTS * 64:SLOTS * 64 + SLOTS, 0]]
  transfers between devices with their start and end apart: 2 -> 26, of which waited for: 2 -> 15; matrix products, arithmetic and copies ran while one was open for 1% -> 4% of each run, Pallas kernels for 0% -> 7%
where the time goes in v1:
time: 142 us
  starting transfers between devices  54 us (38%)
  waiting for transfers between devices  51.2 us (36%)
  Pallas kernels  22.6 us (16%)
  local copies, waits for them, and re-layouts  12.9 us (9%)
    ppermute x8, waiting for transfers between devices, along_x(): lax.ppermute(v, 'tp', [(N * a + b, N * ((a + s) % N) + b) for a in range(...  30.6 us
    ppermute x8, starting transfers between devices, along_z(): lax.ppermute(v, 'rep', [(2 * a + c, 2 * ((a + s) % 8) + c) for a in range...  15.2 us
    ppermute x8, starting transfers between devices, along_y(): lax.ppermute(v, 'tp', [(N * a + b, N * a + (b + s) % N) for a in range(N)...  14.4 us
    ppermute x8, starting transfers between devices, along_x(): lax.ppermute(v, 'tp', [(N * a + b, N * ((a + s) % N) + b) for a in range(...  12.5 us
    ppermute x2, starting transfers between devices, across(): lax.ppermute(v, 'rep', [(2 * a + c, 2 * a + 1 - c) for a in range(8) for...  11.9 us
    ppermute x8, waiting for transfers between devices, along_z(): lax.ppermute(v, 'rep', [(2 * a + c, 2 * ((a + s) % 8) + c) for a in range...  10.9 us
    pallas_call x2, Pallas kernels, partials(): pl.pallas_call(kernel, out_shape=outs, grid_spec=pltpu.PrefetchScalarGrid...  7.53 us
    ppermute x8, waiting for transfers between devices, along_y(): lax.ppermute(v, 'tp', [(N * a + b, N * a + (b + s) % N) for a in range(N)...  7.3 us
  transfers between devices with their start and end apart: 26, of which 15 were waited for; matrix products, arithmetic and copies ran while one was open for 4% of the time, Pallas kernels for 7%

profile of v1, /device:TPU:1, one launch (start us, length us, event | category | flops | bytes accessed | tf_op | source)
XLA Modules:
  0.0 141.7 jit_solution(15522045063656548463)
XLA Ops:
  0.7 1.4 copy-done
  3.9 2.1 %collective-permute-start = (bf16[192,2560]{1,0:T(8,128)(2,1)S(1)}, bf16[192,2560]{1,0:T(8,128)(2,1)S(1)}, u32[]{:S(2)}, u32[]{:S(2)}) collective-permute-start(bf16[192,2560]{1,0:T(8,128)(2,1)S(1)} %pack.6), channel_id=1, source_target_pairs={{0,4},{1,5},{2,6},{3,7},{4,8},{5,9},{6,10},{7,11},{8,12},{9,13},{1... | collective-permute-start | bytes 2949128 | tf_op jit(solution)/shard_map/ppermute | solution.py:24
  8.7 1.6 %collective-permute-start.3 = (bf16[192,2560]{1,0:T(8,128)(2,1)S(1)}, bf16[192,2560]{1,0:T(8,128)(2,1)S(1)}, u32[]{:S(2)}, u32[]{:S(2)}) collective-permute-start(bf16[192,2560]{1,0:T(8,128)(2,1)S(1)} %pack.9), channel_id=1, source_target_pairs={{0,1},{1,2},{2,3},{3,0},{4,5},{5,6},{6,7},{7,4},{8,9},{9,10},{10,1... | collective-permute-start | bytes 2949128 | tf_op jit(solution)/shard_map/ppermute | solution.py:28
  10.9 1.5 %collective-permute-start.4 = (bf16[192,2560]{1,0:T(8,128)(2,1)S(1)}, bf16[192,2560]{1,0:T(8,128)(2,1)S(1)}, u32[]{:S(2)}, u32[]{:S(2)}) collective-permute-start(bf16[192,2560]{1,0:T(8,128)(2,1)S(1)} %pack.10), channel_id=1, source_target_pairs={{0,3},{1,0},{2,1},{3,2},{4,7},{5,4},{6,5},{7,6},{8,11},{9,8},{10,9... | collective-permute-start | bytes 2949128 | tf_op jit(solution)/shard_map/ppermute | solution.py:28
  12.4 14.1 %collective-permute-done.n_o.l = bf16[192,2560]{1,0:T(8,128)(2,1)S(1)} collective-permute-done((bf16[192,2560]{1,0:T(8,128)(2,1)S(1)}, bf16[192,2560]{1,0:T(8,128)(2,1)S(1)}, u32[]{:S(2)}, u32[]{:S(2)}) %collective-permute-start) | collective-permute-done | bytes 983072 | tf_op jit(solution)/shard_map/ppermute | solution.py:24
  26.5 2.0 %collective-permute-start.11 = (bf16[96,2048]{1,0:T(8,128)(2,1)S(1)}, bf16[96,2048]{1,0:T(8,128)(2,1)S(1)}, u32[]{:S(2)}, u32[]{:S(2)}) collective-permute-start(bf16[96,2048]{1,0:T(8,128)(2,1)S(1)} %slice.62), channel_id=1, source_target_pairs={{0,4},{1,5},{2,6},{3,7},{4,8},{5,9},{6,10},{7,11},{8,12},{9,13},{1... | collective-permute-start | bytes 1179656 | tf_op jit(solution)/shard_map/ppermute | solution.py:24
  28.8 1.4 collective-permute-start.12
  30.8 4.7 %collective-permute-start.10 = (bf16[192,512]{1,0:T(8,128)(2,1)S(1)}, bf16[192,512]{1,0:T(8,128)(2,1)S(1)}, u32[]{:S(2)}, u32[]{:S(2)}) collective-permute-start(bf16[192,512]{1,0:T(8,128)(2,1)S(1)} %pack.11), channel_id=1, source_target_pairs={{0,2},{1,3},{2,0},{3,1},{4,6},{5,7},{6,4},{7,5},{8,10},{9,11},{10,... | collective-permute-start | bytes 589832 | tf_op jit(solution)/shard_map/ppermute | solution.py:28
  36.0 2.4 %collective-permute-start.6 = (bf16[96,2048]{1,0:T(8,128)(2,1)S(1)}, bf16[96,2048]{1,0:T(8,128)(2,1)S(1)}, u32[]{:S(2)}, u32[]{:S(2)}) collective-permute-start(bf16[96,2048]{1,0:T(8,128)(2,1)S(1)} %slice.61), channel_id=1, source_target_pairs={{0,3},{1,0},{2,1},{3,2},{4,7},{5,4},{6,5},{7,6},{8,11},{9,8},{10,9... | collective-permute-start | bytes 1179656 | tf_op jit(solution)/shard_map/ppermute | solution.py:28
  38.5 3.8 %partials.3 = (f32[128,2048]{1,0:T(8,128)S(1)}, bf16[128,2048]{1,0:T(8,128)(2,1)S(1)}, bf16[128,2048]{1,0:T(8,128)(2,1)S(1)}, bf16[128,2048]{1,0:T(8,128)(2,1)S(1)}) custom-call(s32[3]{0:T(128)S(1)} %pad_add_fusion.pos_ref, bf16[4,4,192,128]{3,2,1,0:T(8,128)(2,1)S(1)} %bitcast.41, bf16[192,2560]{1,0:T(8,128)(2,1)S(1)} %collective-permute-done.3.l.n_o, ...), custom_call_target="tpu_custom_call" | custom-call | flops 1610612736 | bytes 8388608 | tf_op jit(solution)/shard_map/partials/pallas_call | solution.py:111
  42.3 3.3 %collective-permute-start.13 = (bf16[128,2048]{1,0:T(8,128)(2,1)S(1)}, bf16[128,2048]{1,0:T(8,128)(2,1)S(1)}, u32[]{:S(2)}, u32[]{:S(2)}) collective-permute-start(bf16[128,2048]{1,0:T(8,128)(2,1)S(1)} %get-tuple-element.21), channel_id=1, source_target_pairs={{0,3},{1,0},{2,1},{3,2},{4,7},{5,4},{6,5},{7,6},{8,11},{9,8},{10,9... | collective-permute-start | bytes 1572872 | tf_op jit(solution)/shard_map/ppermute | solution.py:28
  46.2 1.4 collective-permute-start.2
  47.6 4.7 %collective-permute-done.2.p_o = bf16[192,512]{1,0:T(8,128)(2,1)S(1)} collective-permute-done((bf16[192,512]{1,0:T(8,128)(2,1)S(1)}, bf16[192,512]{1,0:T(8,128)(2,1)S(1)}, u32[]{:S(2)}, u32[]{:S(2)}) %collective-permute-start.2) | collective-permute-done | bytes 196640 | tf_op jit(solution)/shard_map/ppermute | solution.py:24
  52.8 3.7 %partials.2 = (f32[128,2048]{1,0:T(8,128)S(1)}, bf16[128,2048]{1,0:T(8,128)(2,1)S(1)}, bf16[128,2048]{1,0:T(8,128)(2,1)S(1)}, bf16[128,2048]{1,0:T(8,128)(2,1)S(1)}) custom-call(s32[3]{0:T(128)S(1)} %pad_add_fusion.pos_ref, bf16[4,4,192,128]{3,2,1,0:T(8,128)(2,1)S(1)} %bitcast.43, bf16[192,2560]{1,0:T(8,128)(2,1)S(1)} %collective-permute-done.n_o.l, ...), custom_call_target="tpu_custom_call" | custom-call | flops 1610612736 | bytes 8388608 | tf_op jit(solution)/shard_map/partials/pallas_call | solution.py:111
  56.5 3.0 %collective-permute-start.7 = (bf16[128,2048]{1,0:T(8,128)(2,1)S(1)}, bf16[128,2048]{1,0:T(8,128)(2,1)S(1)}, u32[]{:S(2)}, u32[]{:S(2)}) collective-permute-start(bf16[128,2048]{1,0:T(8,128)(2,1)S(1)} %get-tuple-element.17), channel_id=1, source_target_pairs={{0,12},{1,13},{2,14},{3,15},{4,0},{5,1},{6,2},{7,3},{8,4},{9,5},{1... | collective-permute-start | bytes 1572872 | tf_op jit(solution)/shard_map/ppermute | solution.py:24
  60.8 7.1 %collective-permute-done.15.b3 = bf16[128,2048]{1,0:T(8,128)(2,1)S(1)} collective-permute-done((bf16[128,2048]{1,0:T(8,128)(2,1)S(1)}, bf16[128,2048]{1,0:T(8,128)(2,1)S(1)}, u32[]{:S(2)}, u32[]{:S(2)}) %collective-permute-start.15) | collective-permute-done | bytes 524320 | tf_op jit(solution)/shard_map/ppermute | solution.py:28
  68.0 3.0 %collective-permute-done.7.a1 = bf16[128,2048]{1,0:T(8,128)(2,1)S(1)} collective-permute-done((bf16[128,2048]{1,0:T(8,128)(2,1)S(1)}, bf16[128,2048]{1,0:T(8,128)(2,1)S(1)}, u32[]{:S(2)}, u32[]{:S(2)}) %collective-permute-start.7) | collective-permute-done | bytes 524320 | tf_op jit(solution)/shard_map/ppermute | solution.py:24
  71.2 8.3 %collective-permute-done.9.a3 = bf16[128,2048]{1,0:T(8,128)(2,1)S(1)} collective-permute-done((bf16[128,2048]{1,0:T(8,128)(2,1)S(1)}, bf16[128,2048]{1,0:T(8,128)(2,1)S(1)}, u32[]{:S(2)}, u32[]{:S(2)}) %collective-permute-start.9) | collective-permute-done | bytes 524320 | tf_op jit(solution)/shard_map/ppermute | solution.py:24
  79.5 5.8 %epilogue.1 = (bf16[128,4096]{1,0:T(8,128)(2,1)}, bf16[272,128]{1,0:T(8,128)(2,1)S(1)}, bf16[272,128]{1,0:T(8,128)(2,1)S(1)}) custom-call(s32[4]{0:T(128)S(1)} %bitcast.54, s32[3]{0:T(128)S(1)} %pad_add_fusion.pos_ref, f32[128,2048]{1,0:T(8,128)S(1)} %get-tuple-element.16.a0, bf16[128,2048]{1,0:T(8,128)(2,1)S(1)} %collective-permute-done.7.a1, ...), custom_call_target="tpu_custom_call" | custom-call | flops 10485760 | bytes 10485760 | tf_op jit(solution)/shard_map/epilogue/pallas_call | solution.py:192
  85.3 6.9 %collective-permute-start.16 = (bf16[272,128]{1,0:T(8,128)(2,1)S(1)}, bf16[272,128]{1,0:T(8,128)(2,1)S(1)}, u32[]{:S(2)}, u32[]{:S(2)}) collective-permute-start(bf16[272,128]{1,0:T(8,128)(2,1)S(1)} %get-tuple-element.25), channel_id=1, source_target_pairs={{0,16},{16,0},{32,48},{48,32},{64,80},{80,64},{96,112},{112,96},{1... | collective-permute-start | bytes 208904 | tf_op jit(solution)/shard_map/ppermute | solution.py:36
  93.2 5.6 %collective-permute-start.18 = (bf16[544,128]{1,0:T(8,128)(2,1)S(1)}, bf16[544,128]{1,0:T(8,128)(2,1)S(1)}, u32[]{:S(2)}, u32[]{:S(2)}) collective-permute-start(bf16[544,128]{1,0:T(8,128)(2,1)S(1)} %constant_dynamic-update-slice_fusion.refs_0_), channel_id=1, source_target_pairs={{0,224},{16,240},{32,0},{48,16},{64,32},{80,48},{96,64},{112,80},{... | collective-permute-start | bytes 417800 | tf_op jit(solution)/shard_map/ppermute | solution.py:32
  98.8 2.7 %collective-permute-done.18.refs_2_ = bf16[544,128]{1,0:T(8,128)(2,1)S(1)} collective-permute-done((bf16[544,128]{1,0:T(8,128)(2,1)S(1)}, bf16[544,128]{1,0:T(8,128)(2,1)S(1)}, u32[]{:S(2)}, u32[]{:S(2)}) %collective-permute-start.18) | collective-permute-done | bytes 139296 | tf_op jit(solution)/shard_map/ppermute | solution.py:32
  101.5 3.4 %collective-permute-start.20 = (bf16[544,128]{1,0:T(8,128)(2,1)S(1)}, bf16[544,128]{1,0:T(8,128)(2,1)S(1)}, u32[]{:S(2)}, u32[]{:S(2)}) collective-permute-start(bf16[544,128]{1,0:T(8,128)(2,1)S(1)} %collective-permute-done.18.refs_2_), channel_id=1, source_target_pairs={{0,224},{16,240},{32,0},{48,16},{64,32},{80,48},{96,64},{112,80},{... | collective-permute-start | bytes 417800 | tf_op jit(solution)/shard_map/ppermute | solution.py:32
  105.0 2.0 %collective-permute-done.20.refs_4_ = bf16[544,128]{1,0:T(8,128)(2,1)S(1)} collective-permute-done((bf16[544,128]{1,0:T(8,128)(2,1)S(1)}, bf16[544,128]{1,0:T(8,128)(2,1)S(1)}, u32[]{:S(2)}, u32[]{:S(2)}) %collective-permute-start.20) | collective-permute-done | bytes 139296 | tf_op jit(solution)/shard_map/ppermute | solution.py:32
  107.0 3.1 %collective-permute-start.22 = (bf16[544,128]{1,0:T(8,128)(2,1)S(1)}, bf16[544,128]{1,0:T(8,128)(2,1)S(1)}, u32[]{:S(2)}, u32[]{:S(2)}) collective-permute-start(bf16[544,128]{1,0:T(8,128)(2,1)S(1)} %collective-permute-done.20.refs_4_), channel_id=1, source_target_pairs={{0,224},{16,240},{32,0},{48,16},{64,32},{80,48},{96,64},{112,80},{... | collective-permute-start | bytes 417800 | tf_op jit(solution)/shard_map/ppermute | solution.py:32
  110.2 1.9 %collective-permute-done.22.refs_6_ = bf16[544,128]{1,0:T(8,128)(2,1)S(1)} collective-permute-done((bf16[544,128]{1,0:T(8,128)(2,1)S(1)}, bf16[544,128]{1,0:T(8,128)(2,1)S(1)}, u32[]{:S(2)}, u32[]{:S(2)}) %collective-permute-start.22) | collective-permute-done | bytes 139296 | tf_op jit(solution)/shard_map/ppermute | solution.py:32
  112.7 3.1 %collective-permute-start.24 = (bf16[272,128]{1,0:T(8,128)(2,1)}, bf16[272,128]{1,0:T(8,128)(2,1)S(1)}, u32[]{:S(2)}, u32[]{:S(2)}) collective-permute-start(bf16[272,128]{1,0:T(8,128)(2,1)} %slice.73), channel_id=1, source_target_pairs={{0,224},{16,240},{32,0},{48,16},{64,32},{80,48},{96,64},{112,80},{... | collective-permute-start | bytes 208904 | tf_op jit(solution)/shard_map/ppermute | solution.py:32
  120.8 4.2 %collective-permute-done.23.refs_7_ = bf16[272,128]{1,0:T(8,128)(2,1)} collective-permute-done((bf16[272,128]{1,0:T(8,128)(2,1)}, bf16[272,128]{1,0:T(8,128)(2,1)}, u32[]{:S(2)}, u32[]{:S(2)}) %collective-permute-start.23) | collective-permute-done | bytes 69664 | tf_op jit(solution)/shard_map/ppermute | solution.py:32
  129.6 2.4 %add_tiles.1.m_ref = bf16[64,4096]{1,0:T(8,128)(2,1)S(1)} custom-call(s32[64]{0:T(128)S(1)} %reshape.46.ids_ref, bf16[544,128]{1,0:T(8,128)(2,1)S(1)} %copy-done.9, bf16[544,128]{1,0:T(8,128)(2,1)S(1)} %copy-done.13, bf16[544,128]{1,0:T(8,128)(2,1)S(1)} %copy-done.11, bf16[544,128]{1,0:T(8,128)(2,1)} %collective-permute-done.19.refs_3_, ...), custom_call_target="tpu_custom_call" | custom-call | flops 524288 | bytes 3145728 | tf_op jit(solution)/shard_map/add_tiles/pallas_call | solution.py:234
  132.0 5.0 %collective-permute-start.25 = (bf16[64,4096]{1,0:T(8,128)(2,1)S(1)}, bf16[64,4096]{1,0:T(8,128)(2,1)S(1)}, u32[]{:S(2)}, u32[]{:S(2)}) collective-permute-start(bf16[64,4096]{1,0:T(8,128)(2,1)S(1)} %add_tiles.1.m_ref), channel_id=1, source_target_pairs={{0,16},{16,0},{32,48},{48,32},{64,80},{80,64},{96,112},{112,96},{1... | collective-permute-start | bytes 1572872 | tf_op jit(solution)/shard_map/ppermute | solution.py:36
  137.0 1.5 %collective-permute-done.25.o_ref = bf16[64,4096]{1,0:T(8,128)(2,1)S(1)} collective-permute-done((bf16[64,4096]{1,0:T(8,128)(2,1)S(1)}, bf16[64,4096]{1,0:T(8,128)(2,1)S(1)}, u32[]{:S(2)}, u32[]{:S(2)}) %collective-permute-start.25) | collective-permute-done | bytes 524320 | tf_op jit(solution)/shard_map/ppermute | solution.py:36
  138.5 3.2 %outer.1 = (f32[128,4096]{1,0:T(8,128)}, bf16[128,4096]{1,0:T(8,128)(2,1)}) custom-call(s32[3]{0:T(128)S(1)} %pad_add_fusion.pos_ref, bf16[64,4096]{1,0:T(8,128)(2,1)S(1)} %add_tiles.1.m_ref, bf16[64,4096]{1,0:T(8,128)(2,1)S(1)} %collective-permute-done.25.o_ref, f32[128,4096]{1,0:T(8,128)S(1)} %copy-done.3, bf16[128,4096]{1,0:T(8,128)(2,1)S(1)} %copy-done.4), custom_call_target="tpu_custom_call" | custom-call | flops 3145728 | bytes 8388608 | tf_op jit(solution)/shard_map/outer/pallas_call | solution.py:264
  (101 shorter events, 20.5 us)
Async XLA Ops:
  3.9 22.6 %collective-permute-start = (bf16[192,2560]{1,0:T(8,128)(2,1)S(1)}, bf16[192,2560]{1,0:T(8,128)(2,1)S(1)}, u32[]{:S(2)}, u32[]{:S(2)}) collective-permute-start(bf16[192,2560]{1,0:T(8,128)(2,1)S(1)} %pack.6), channel_id=1, source_target_pairs={{0,4},{1,5},{2,6},{3,7},{4,8},{5,9},{6,10},{7,11},{8,12},{9,13},{1... | collective-permute-start | bytes 2949128 | tf_op jit(solution)/shard_map/ppermute | solution.py:24
  6.6 22.1 %collective-permute-start.1 = (bf16[192,2560]{1,0:T(8,128)(2,1)S(1)}, bf16[192,2560]{1,0:T(8,128)(2,1)S(1)}, u32[]{:S(2)}, u32[]{:S(2)}) collective-permute-start(bf16[192,2560]{1,0:T(8,128)(2,1)S(1)} %pack.7), channel_id=1, source_target_pairs={{0,12},{1,13},{2,14},{3,15},{4,0},{5,1},{6,2},{7,3},{8,4},{9,5},{1... | collective-permute-start | bytes 2949128 | tf_op jit(solution)/shard_map/ppermute | solution.py:24
  8.7 26.8 %collective-permute-start.3 = (bf16[192,2560]{1,0:T(8,128)(2,1)S(1)}, bf16[192,2560]{1,0:T(8,128)(2,1)S(1)}, u32[]{:S(2)}, u32[]{:S(2)}) collective-permute-start(bf16[192,2560]{1,0:T(8,128)(2,1)S(1)} %pack.9), channel_id=1, source_target_pairs={{0,1},{1,2},{2,3},{3,0},{4,5},{5,6},{6,7},{7,4},{8,9},{9,10},{10,1... | collective-permute-start | bytes 2949128 | tf_op jit(solution)/shard_map/ppermute | solution.py:28
  10.9 27.6 %copy-start.1 = (bf16[1,192,4096]{2,1,0:T(8,128)(2,1)S(1)}, bf16[1,192,4096]{2,1,0:T(8,128)(2,1)}, u32[]{:S(2)}) copy-start(bf16[1,192,4096]{2,1,0:T(8,128)(2,1)} %param.8) | copy-start | bytes 4718596
  10.9 25.1 %collective-permute-start.4 = (bf16[192,2560]{1,0:T(8,128)(2,1)S(1)}, bf16[192,2560]{1,0:T(8,128)(2,1)S(1)}, u32[]{:S(2)}, u32[]{:S(2)}) collective-permute-start(bf16[192,2560]{1,0:T(8,128)(2,1)S(1)} %pack.10), channel_id=1, source_target_pairs={{0,3},{1,0},{2,1},{3,2},{4,7},{5,4},{6,5},{7,6},{8,11},{9,8},{10,9... | collective-permute-start | bytes 2949128 | tf_op jit(solution)/shard_map/ppermute | solution.py:28
  26.5 12.0 %collective-permute-start.11 = (bf16[96,2048]{1,0:T(8,128)(2,1)S(1)}, bf16[96,2048]{1,0:T(8,128)(2,1)S(1)}, u32[]{:S(2)}, u32[]{:S(2)}) collective-permute-start(bf16[96,2048]{1,0:T(8,128)(2,1)S(1)} %slice.62), channel_id=1, source_target_pairs={{0,4},{1,5},{2,6},{3,7},{4,8},{5,9},{6,10},{7,11},{8,12},{9,13},{1... | collective-permute-start | bytes 1179656 | tf_op jit(solution)/shard_map/ppermute | solution.py:24
  28.8 9.7 %collective-permute-start.12 = (bf16[96,2048]{1,0:T(8,128)(2,1)S(1)}, bf16[96,2048]{1,0:T(8,128)(2,1)S(1)}, u32[]{:S(2)}, u32[]{:S(2)}) collective-permute-start(bf16[96,2048]{1,0:T(8,128)(2,1)S(1)} %slice.63), channel_id=1, source_target_pairs={{0,12},{1,13},{2,14},{3,15},{4,0},{5,1},{6,2},{7,3},{8,4},{9,5},{1... | collective-permute-start | bytes 1179656 | tf_op jit(solution)/shard_map/ppermute | solution.py:24
  30.8 7.7 %collective-permute-start.10 = (bf16[192,512]{1,0:T(8,128)(2,1)S(1)}, bf16[192,512]{1,0:T(8,128)(2,1)S(1)}, u32[]{:S(2)}, u32[]{:S(2)}) collective-permute-start(bf16[192,512]{1,0:T(8,128)(2,1)S(1)} %pack.11), channel_id=1, source_target_pairs={{0,2},{1,3},{2,0},{3,1},{4,6},{5,7},{6,4},{7,5},{8,10},{9,11},{10,... | collective-permute-start | bytes 589832 | tf_op jit(solution)/shard_map/ppermute | solution.py:28
  35.5 17.4 %collective-permute-start.5 = (bf16[96,2048]{1,0:T(8,128)(2,1)S(1)}, bf16[96,2048]{1,0:T(8,128)(2,1)S(1)}, u32[]{:S(2)}, u32[]{:S(2)}) collective-permute-start(bf16[96,2048]{1,0:T(8,128)(2,1)S(1)} %slice.60), channel_id=1, source_target_pairs={{0,1},{1,2},{2,3},{3,0},{4,5},{5,6},{6,7},{7,4},{8,9},{9,10},{10,1... | collective-permute-start | bytes 1179656 | tf_op jit(solution)/shard_map/ppermute | solution.py:28
  36.0 16.8 %collective-permute-start.6 = (bf16[96,2048]{1,0:T(8,128)(2,1)S(1)}, bf16[96,2048]{1,0:T(8,128)(2,1)S(1)}, u32[]{:S(2)}, u32[]{:S(2)}) collective-permute-start(bf16[96,2048]{1,0:T(8,128)(2,1)S(1)} %slice.61), channel_id=1, source_target_pairs={{0,3},{1,0},{2,1},{3,2},{4,7},{5,4},{6,5},{7,6},{8,11},{9,8},{10,9... | collective-permute-start | bytes 1179656 | tf_op jit(solution)/shard_map/ppermute | solution.py:28
  42.3 17.3 %collective-permute-start.13 = (bf16[128,2048]{1,0:T(8,128)(2,1)S(1)}, bf16[128,2048]{1,0:T(8,128)(2,1)S(1)}, u32[]{:S(2)}, u32[]{:S(2)}) collective-permute-start(bf16[128,2048]{1,0:T(8,128)(2,1)S(1)} %get-tuple-element.21), channel_id=1, source_target_pairs={{0,3},{1,0},{2,1},{3,2},{4,7},{5,4},{6,5},{7,6},{8,11},{9,8},{10,9... | collective-permute-start | bytes 1572872 | tf_op jit(solution)/shard_map/ppermute | solution.py:28
  46.2 6.1 %collective-permute-start.2 = (bf16[192,512]{1,0:T(8,128)(2,1)S(1)}, bf16[192,512]{1,0:T(8,128)(2,1)S(1)}, u32[]{:S(2)}, u32[]{:S(2)}) collective-permute-start(bf16[192,512]{1,0:T(8,128)(2,1)S(1)} %pack.8), channel_id=1, source_target_pairs={{0,8},{1,9},{2,10},{3,11},{4,12},{5,13},{6,14},{7,15},{8,0},{9,1},... | collective-permute-start | bytes 589832 | tf_op jit(solution)/shard_map/ppermute | solution.py:24
  47.6 13.2 %collective-permute-start.14 = (bf16[128,2048]{1,0:T(8,128)(2,1)S(1)}, bf16[128,2048]{1,0:T(8,128)(2,1)S(1)}, u32[]{:S(2)}, u32[]{:S(2)}) collective-permute-start(bf16[128,2048]{1,0:T(8,128)(2,1)S(1)} %get-tuple-element.22), channel_id=1, source_target_pairs={{0,1},{1,2},{2,3},{3,0},{4,5},{5,6},{6,7},{7,4},{8,9},{9,10},{10,1... | collective-permute-start | bytes 1572872 | tf_op jit(solution)/shard_map/ppermute | solution.py:28
  52.4 27.1 %copy-start.5 = (bf16[1,128,4096]{2,1,0:T(8,128)(2,1)S(1)}, bf16[1,128,4096]{2,1,0:T(8,128)(2,1)}, u32[]{:S(2)}) copy-start(bf16[1,128,4096]{2,1,0:T(8,128)(2,1)} %param.11) | copy-start | bytes 3145732
  52.4 27.1 %copy-start.6 = (bf16[1,128,4096]{2,1,0:T(8,128)(2,1)S(1)}, bf16[1,128,4096]{2,1,0:T(8,128)(2,1)}, u32[]{:S(2)}) copy-start(bf16[1,128,4096]{2,1,0:T(8,128)(2,1)} %param.12) | copy-start | bytes 3145732
  52.4 27.1 %copy-start.7 = (bf16[1,128,4096]{2,1,0:T(8,128)(2,1)S(1)}, bf16[1,128,4096]{2,1,0:T(8,128)(2,1)}, u32[]{:S(2)}) copy-start(bf16[1,128,4096]{2,1,0:T(8,128)(2,1)} %param.13) | copy-start | bytes 3145732
  52.4 27.1 %copy-start.16 = (s32[1,1,4]{2,1,0:T(1,128)S(1)}, s32[1,1,4]{2,1,0:T(1,128)}, u32[]{:S(2)}) copy-start(s32[1,1,4]{2,1,0:T(1,128)} %param.15) | copy-start | bytes 52
  52.4 15.6 %collective-permute-start.15 = (bf16[128,2048]{1,0:T(8,128)(2,1)S(1)}, bf16[128,2048]{1,0:T(8,128)(2,1)S(1)}, u32[]{:S(2)}, u32[]{:S(2)}) collective-permute-start(bf16[128,2048]{1,0:T(8,128)(2,1)S(1)} %get-tuple-element.23), channel_id=1, source_target_pairs={{0,2},{1,3},{2,0},{3,1},{4,6},{5,7},{6,4},{7,5},{8,10},{9,11},{10,... | collective-permute-start | bytes 1572872 | tf_op jit(solution)/shard_map/ppermute | solution.py:28
  56.5 14.4 %collective-permute-start.7 = (bf16[128,2048]{1,0:T(8,128)(2,1)S(1)}, bf16[128,2048]{1,0:T(8,128)(2,1)S(1)}, u32[]{:S(2)}, u32[]{:S(2)}) collective-permute-start(bf16[128,2048]{1,0:T(8,128)(2,1)S(1)} %get-tuple-element.17), channel_id=1, source_target_pairs={{0,12},{1,13},{2,14},{3,15},{4,0},{5,1},{6,2},{7,3},{8,4},{9,5},{1... | collective-permute-start | bytes 1572872 | tf_op jit(solution)/shard_map/ppermute | solution.py:24
  59.6 11.6 %collective-permute-start.8 = (bf16[128,2048]{1,0:T(8,128)(2,1)S(1)}, bf16[128,2048]{1,0:T(8,128)(2,1)S(1)}, u32[]{:S(2)}, u32[]{:S(2)}) collective-permute-start(bf16[128,2048]{1,0:T(8,128)(2,1)S(1)} %get-tuple-element.18), channel_id=1, source_target_pairs={{0,4},{1,5},{2,6},{3,7},{4,8},{5,9},{6,10},{7,11},{8,12},{9,13},{1... | collective-permute-start | bytes 1572872 | tf_op jit(solution)/shard_map/ppermute | solution.py:24
  59.6 19.9 %collective-permute-start.9 = (bf16[128,2048]{1,0:T(8,128)(2,1)S(1)}, bf16[128,2048]{1,0:T(8,128)(2,1)S(1)}, u32[]{:S(2)}, u32[]{:S(2)}) collective-permute-start(bf16[128,2048]{1,0:T(8,128)(2,1)S(1)} %get-tuple-element.19), channel_id=1, source_target_pairs={{0,8},{1,9},{2,10},{3,11},{4,12},{5,13},{6,14},{7,15},{8,0},{9,1},... | collective-permute-start | bytes 1572872 | tf_op jit(solution)/shard_map/ppermute | solution.py:24
  85.3 53.2 %copy-start.4 = (bf16[128,4096]{1,0:T(8,128)(2,1)S(1)}, bf16[128,4096]{1,0:T(8,128)(2,1)}, u32[]{:S(2)}) copy-start(bf16[128,4096]{1,0:T(8,128)(2,1)} %v_ref.1) | copy-start | bytes 3145732
  85.3 7.8 %collective-permute-start.16 = (bf16[272,128]{1,0:T(8,128)(2,1)S(1)}, bf16[272,128]{1,0:T(8,128)(2,1)S(1)}, u32[]{:S(2)}, u32[]{:S(2)}) collective-permute-start(bf16[272,128]{1,0:T(8,128)(2,1)S(1)} %get-tuple-element.25), channel_id=1, source_target_pairs={{0,16},{16,0},{32,48},{48,32},{64,80},{80,64},{96,112},{112,96},{1... | collective-permute-start | bytes 208904 | tf_op jit(solution)/shard_map/ppermute | solution.py:36
  93.2 8.3 %collective-permute-start.18 = (bf16[544,128]{1,0:T(8,128)(2,1)S(1)}, bf16[544,128]{1,0:T(8,128)(2,1)S(1)}, u32[]{:S(2)}, u32[]{:S(2)}) collective-permute-start(bf16[544,128]{1,0:T(8,128)(2,1)S(1)} %constant_dynamic-update-slice_fusion.refs_0_), channel_id=1, source_target_pairs={{0,224},{16,240},{32,0},{48,16},{64,32},{80,48},{96,64},{112,80},{... | collective-permute-start | bytes 417800 | tf_op jit(solution)/shard_map/ppermute | solution.py:32
  98.8 6.1 %collective-permute-start.17 = (bf16[544,128]{1,0:T(8,128)(2,1)S(1)}, bf16[544,128]{1,0:T(8,128)(2,1)S(1)}, u32[]{:S(2)}, u32[]{:S(2)}) collective-permute-start(bf16[544,128]{1,0:T(8,128)(2,1)S(1)} %constant_dynamic-update-slice_fusion.refs_0_), channel_id=1, source_target_pairs={{0,32},{16,48},{32,64},{48,80},{64,96},{80,112},{96,128},{112,144}... | collective-permute-start | bytes 417800 | tf_op jit(solution)/shard_map/ppermute | solution.py:32
  101.5 5.4 %collective-permute-start.20 = (bf16[544,128]{1,0:T(8,128)(2,1)S(1)}, bf16[544,128]{1,0:T(8,128)(2,1)S(1)}, u32[]{:S(2)}, u32[]{:S(2)}) collective-permute-start(bf16[544,128]{1,0:T(8,128)(2,1)S(1)} %collective-permute-done.18.refs_2_), channel_id=1, source_target_pairs={{0,224},{16,240},{32,0},{48,16},{64,32},{80,48},{96,64},{112,80},{... | collective-permute-start | bytes 417800 | tf_op jit(solution)/shard_map/ppermute | solution.py:32
  105.0 5.2 %collective-permute-start.19 = (bf16[544,128]{1,0:T(8,128)(2,1)S(1)}, bf16[544,128]{1,0:T(8,128)(2,1)}, u32[]{:S(2)}, u32[]{:S(2)}) collective-permute-start(bf16[544,128]{1,0:T(8,128)(2,1)S(1)} %collective-permute-done.17.refs_1_), channel_id=1, source_target_pairs={{0,32},{16,48},{32,64},{48,80},{64,96},{80,112},{96,128},{112,144}... | collective-permute-start | bytes 417800 | tf_op jit(solution)/shard_map/ppermute | solution.py:32
  107.0 5.1 %collective-permute-start.22 = (bf16[544,128]{1,0:T(8,128)(2,1)S(1)}, bf16[544,128]{1,0:T(8,128)(2,1)S(1)}, u32[]{:S(2)}, u32[]{:S(2)}) collective-permute-start(bf16[544,128]{1,0:T(8,128)(2,1)S(1)} %collective-permute-done.20.refs_4_), channel_id=1, source_target_pairs={{0,224},{16,240},{32,0},{48,16},{64,32},{80,48},{96,64},{112,80},{... | collective-permute-start | bytes 417800 | tf_op jit(solution)/shard_map/ppermute | solution.py:32
  110.2 9.5 %collective-permute-start.21 = (bf16[544,128]{1,0:T(8,128)(2,1)}, bf16[544,128]{1,0:T(8,128)(2,1)S(1)}, u32[]{:S(2)}, u32[]{:S(2)}) collective-permute-start(bf16[544,128]{1,0:T(8,128)(2,1)} %collective-permute-done.19.refs_3_), channel_id=1, source_target_pairs={{0,32},{16,48},{32,64},{48,80},{64,96},{80,112},{96,128},{112,144}... | collective-permute-start | bytes 417800 | tf_op jit(solution)/shard_map/ppermute | solution.py:32
  112.7 8.1 %collective-permute-start.24 = (bf16[272,128]{1,0:T(8,128)(2,1)}, bf16[272,128]{1,0:T(8,128)(2,1)S(1)}, u32[]{:S(2)}, u32[]{:S(2)}) collective-permute-start(bf16[272,128]{1,0:T(8,128)(2,1)} %slice.73), channel_id=1, source_target_pairs={{0,224},{16,240},{32,0},{48,16},{64,32},{80,48},{96,64},{112,80},{... | collective-permute-start | bytes 208904 | tf_op jit(solution)/shard_map/ppermute | solution.py:32
  120.4 4.7 %collective-permute-start.23 = (bf16[272,128]{1,0:T(8,128)(2,1)}, bf16[272,128]{1,0:T(8,128)(2,1)}, u32[]{:S(2)}, u32[]{:S(2)}) collective-permute-start(bf16[272,128]{1,0:T(8,128)(2,1)} %slice.71), channel_id=1, source_target_pairs={{0,32},{16,48},{32,64},{48,80},{64,96},{80,112},{96,128},{112,144}... | collective-permute-start | bytes 208904 | tf_op jit(solution)/shard_map/ppermute | solution.py:32
  132.0 6.5 %collective-permute-start.25 = (bf16[64,4096]{1,0:T(8,128)(2,1)S(1)}, bf16[64,4096]{1,0:T(8,128)(2,1)S(1)}, u32[]{:S(2)}, u32[]{:S(2)}) collective-permute-start(bf16[64,4096]{1,0:T(8,128)(2,1)S(1)} %add_tiles.1.m_ref), channel_id=1, source_target_pairs={{0,16},{16,0},{32,48},{48,32},{64,80},{80,64},{96,112},{112,96},{1... | collective-permute-start | bytes 1572872 | tf_op jit(solution)/shard_map/ppermute | solution.py:36
  (11 other events, 73.0 us)

commit v2 on v0

v2 whole, which is shorter than its diff:
```python
import functools

import jax
import jax.numpy as jnp
from jax import lax
from jax.experimental import pallas as pl
from jax.experimental.pallas import tpu as pltpu
from jax.sharding import PartitionSpec as P

N = 4
ROWS = 192
HALF = 2048
COLS = 128
TILE = 128
FEATS = 4096
SLOTS = 4
PIECE = SLOTS * COLS + 16
T_ROWS = HALF // TILE * ROWS
O_ROWS = N * ROWS
IDS = 16
FIRST = T_ROWS + O_ROWS + O_ROWS // 2 + IDS
RELAY = T_ROWS // 2 + O_ROWS // 2 + IDS
BF = jnp.bfloat16
F32 = jnp.float32
SMALL_CAP = 8 * 1024 * 1024
PACK_CAP = 50 * 1024 * 1024
VMEM = pl.BlockSpec(memory_space=pltpu.VMEM)


def along_x(v, s):
    return lax.ppermute(v, "tp", [(N * a + b, N * ((a + s) % N) + b) for a in range(N) for b in range(N)])


def along_y(v, s):
    return lax.ppermute(v, "tp", [(N * a + b, N * a + (b + s) % N) for a in range(N) for b in range(N)])


def onward(v):
    pairs = [(2 * a, 2 * ((a + 1) % 8)) for a in range(8)] + [(2 * a + 1, 2 * ((a + 7) % 8) + 1) for a in range(8)]
    return lax.ppermute(v, "rep", pairs)


def across(v):
    return lax.ppermute(v, "rep", [(2 * a + c, 2 * a + 1 - c) for a in range(8) for c in range(2)])


def put_ids(ref, row, read):
    at = lax.broadcasted_iota(jnp.int32, (IDS, TILE), 0)
    v = jnp.zeros((IDS, TILE), jnp.int32)
    for k in range(SLOTS):
        v = jnp.where(at == k, read(k) + 1, v)
    ref[row : row + IDS] = v.astype(F32).astype(BF)


def get_ids(block):
    at = lax.broadcasted_iota(jnp.int32, (IDS, TILE), 0)
    lane = lax.broadcasted_iota(jnp.int32, (IDS, TILE), 1)
    scale = jnp.where(at == 0, 1.0, jnp.where(at == 1, 64.0, jnp.where(at == 2, 4096.0, 262144.0)))
    scale = jnp.where((lane == 0) & (at < SLOTS), scale, 0.0)
    code = jnp.sum(block.astype(F32) * scale).astype(jnp.int32)
    return [((code >> (6 * k)) & 63) - 1 for k in range(SLOTS)]


def pack(pos, lists, tokens, og4):
    def kernel(pos_ref, ids_hbm, tok_hbm, og_hbm, *rest):
        outs, (ids, tok, near, far, sems) = rest[:4], rest[4:]
        x, y = pos_ref[0], pos_ref[1]
        copies = [
            pltpu.make_async_copy(ids_hbm, ids, sems.at[0]),
            pltpu.make_async_copy(tok_hbm.at[:, pl.ds(0, HALF)], tok.at[0], sems.at[1]),
            pltpu.make_async_copy(og_hbm.at[:, lax.rem(y + 1, N)], near.at[0], sems.at[2]),
            pltpu.make_async_copy(og_hbm.at[:, lax.rem(y + 3, N)], near.at[1], sems.at[3]),
            pltpu.make_async_copy(og_hbm.at[:, lax.rem(y + 2, N)], far.at[0], sems.at[4]),
            pltpu.make_async_copy(tok_hbm.at[:, pl.ds(HALF, HALF)], tok.at[1], sems.at[5]),
            pltpu.make_async_copy(og_hbm.at[lax.rem(x + 1, N)], near.at[2], sems.at[6]),
            pltpu.make_async_copy(og_hbm.at[lax.rem(x + 3, N)], near.at[3], sems.at[7]),
            pltpu.make_async_copy(og_hbm.at[lax.rem(x + 2, N)], far.at[1], sems.at[8]),
        ]
        for c in copies:
            c.start()
        copies[0].wait()
        for out in outs:
            put_ids(out, FIRST - IDS, lambda k: ids[0, k])
        for part in range(2):
            for c in copies[1 + 4 * part : 5 + 4 * part]:
                c.wait()
            for way in range(2):
                out = outs[2 * part + way]
                for j in range(HALF // TILE):
                    out[ROWS * j : ROWS * (j + 1)] = tok[part, :, TILE * j : TILE * (j + 1)]
                for i in range(N):
                    row = T_ROWS + ROWS * i
                    out[row : row + ROWS] = near[2 * part + way, i]
                for i in range(2):
                    row = T_ROWS + O_ROWS + ROWS * i
                    out[row : row + ROWS] = far[part, 2 * way + i]

    hbm = pl.BlockSpec(memory_space=pltpu.HBM)
    return pl.pallas_call(
        kernel,
        out_shape=[jax.ShapeDtypeStruct((FIRST, TILE), BF)] * 4,
        in_specs=[pl.BlockSpec(memory_space=pltpu.SMEM), hbm, hbm, hbm],
        out_specs=[VMEM] * 4,
        scratch_shapes=[
            pltpu.SMEM((1, SLOTS), jnp.int32),
            pltpu.VMEM((2, ROWS, HALF), BF),
            pltpu.VMEM((4, N, ROWS, COLS), BF),
            pltpu.VMEM((2, N, ROWS, COLS), BF),
            pltpu.SemaphoreType.DMA((9,)),
        ],
        cost_estimate=pl.CostEstimate(flops=0, bytes_accessed=16 * FIRST * TILE, transcendentals=0),
        compiler_params=pltpu.CompilerParams(vmem_limit_bytes=PACK_CAP),
        name="pack",
    )(pos, lists, tokens, og4)


def relay(message, shift):
    lo = 0 if shift == 1 else ROWS // 2
    hi = lo + ROWS // 2

    def kernel(ref, out):
        for j in range(HALF // TILE):
            out[ROWS // 2 * j : ROWS // 2 * (j + 1)] = ref[ROWS * j + lo : ROWS * j + hi]
        out[T_ROWS // 2 :] = ref[T_ROWS + O_ROWS :]

    return pl.pallas_call(
        kernel,
        out_shape=jax.ShapeDtypeStruct((RELAY, TILE), BF),
        in_specs=[VMEM],
        out_specs=VMEM,
        compiler_params=pltpu.CompilerParams(vmem_limit_bytes=SMALL_CAP),
        cost_estimate=pl.CostEstimate(flops=0, bytes_accessed=4 * RELAY * TILE, transcendentals=0),
        name="relay",
    )(message)


def gather(pos, ids, og4, near_o, far_o, tokens, near_t, far_t, part):
    def kernel(pos_ref, ids_ref, own_o, n_o, f_o, t, l, r, rhs, turned, listed, lhs):
        x, y = pos_ref[0], pos_ref[1]
        here = pos_ref[1 - part]
        for s, d in enumerate((0, N - 1, 1, 2)):
            k = lax.rem(here + d, N)
            rows = slice(ROWS * s, ROWS * (s + 1))
            their = pl.ds(pl.multiple_of(T_ROWS + k * ROWS, ROWS), ROWS)
            lhs[rows, 0:COLS] = own_o[x, k] if part == 0 else own_o[k, y]
            lhs[rows, COLS : 2 * COLS] = n_o[their]
            lhs[rows, 2 * COLS : 3 * COLS] = f_o[their]
        for p in range(3):
            at = slice(COLS * p, COLS * (p + 1))
            turned[at] = lhs[:, at].T
        for p, ref in enumerate((None, n_o, f_o)):
            found = [ids_ref[k] for k in range(SLOTS)] if ref is None else get_ids(ref[FIRST - IDS :])
            for k in range(SLOTS):
                listed[SLOTS * p + k] = found[k] - part * (HALF // TILE)
        rhs[0:ROWS] = t[:, HALF * part : HALF * (part + 1)]
        for j in range(HALF // TILE):
            at = slice(TILE * j, TILE * (j + 1))
            rows = slice(ROWS * j, ROWS * (j + 1))
            rhs[ROWS : 2 * ROWS, at] = l[rows]
            rhs[2 * ROWS : 3 * ROWS, at] = r[rows]

    smem = pl.BlockSpec(memory_space=pltpu.SMEM)
    return pl.pallas_call(
        kernel,
        out_shape=[
            jax.ShapeDtypeStruct((N * ROWS, HALF), BF),
            jax.ShapeDtypeStruct((N * COLS, N * ROWS), BF),
            jax.ShapeDtypeStruct((N * SLOTS,), jnp.int32),
        ],
        in_specs=[smem, smem] + [VMEM] * 6,
        out_specs=[VMEM, VMEM, smem],
        scratch_shapes=[pltpu.VMEM((N * ROWS, 3 * COLS), BF)],
        compiler_params=pltpu.CompilerParams(vmem_limit_bytes=SMALL_CAP),
        cost_estimate=pl.CostEstimate(flops=0, bytes_accessed=8 << 20, transcendentals=0),
        name="gather",
    )(pos, ids, og4, near_o, far_o, tokens, near_t, far_t)


def partials(pos, ready, lo_o, hi_o, op1, op2, part, *after):
    width = 512
    half = ROWS // 2
    tiles = HALF // TILE

    def kernel(pos_ref, listed, lo, hi, a, b, rhs_in, turned_in, *rest):
        own, near, far, own_sel, to_near, to_far, op_sel, rhs, turned, lhs, op, beyond, found = rest[len(after) :]
        op[0 : O_ROWS // 2] = lo[T_ROWS // 2 : T_ROWS // 2 + O_ROWS // 2]
        op[O_ROWS // 2 :] = hi[T_ROWS // 2 : T_ROWS // 2 + O_ROWS // 2]
        here = pos_ref[1 - part]
        for s, d in enumerate((0, N - 1, 1, 2)):
            k = lax.rem(here + d, N)
            lhs[ROWS * s : ROWS * (s + 1)] = op[pl.ds(pl.multiple_of(k * ROWS, ROWS), ROWS)]
        turned[3 * COLS :] = lhs[...].T
        for k in range(3 * SLOTS):
            found[k] = listed[k]
        for k, t in enumerate(get_ids(lo[RELAY - IDS :])):
            found[3 * SLOTS + k] = t - part * tiles
        for j in range(tiles):
            at = slice(TILE * j, TILE * (j + 1))
            rhs[3 * ROWS : 3 * ROWS + half, at] = a[half * j : half * (j + 1)]
            rhs[3 * ROWS + half :, at] = b[half * j : half * (j + 1)]
        for i in range(HALF // width):
            at = slice(width * i, width * (i + 1))
            res = jnp.dot(turned[...], rhs[:, at], preferred_element_type=F32)
            own[:, at] = res[0:COLS]
            near[:, at] = res[COLS : 2 * COLS].astype(BF)
            far[:, at] = res[2 * COLS : 3 * COLS].astype(BF)
            beyond[:, at] = res[3 * COLS :].astype(BF)
        for j in range(tiles):
            out = to_far if j < tiles // 2 else to_near
            row = SLOTS * COLS + COLS * (j % (tiles // 2))
            out[row : row + COLS] = beyond[:, TILE * j : TILE * (j + 1)]
        for p, (out, sel) in enumerate(((own, own_sel), (near, to_near), (far, to_far), (beyond, op_sel))):
            for k in range(SLOTS):
                t = found[SLOTS * p + k]

                @pl.when((t >= 0) & (t < tiles))
                def _():
                    sel[COLS * k : COLS * (k + 1)] = out[:, pl.ds(pl.multiple_of(t * TILE, TILE), TILE)]

    smem = pl.BlockSpec(memory_space=pltpu.SMEM)
    rhs, turned, listed = ready
    shape = jax.ShapeDtypeStruct
    wide, message, few = (COLS, HALF), (SLOTS * COLS + COLS * tiles // 2, TILE), (SLOTS * COLS, TILE)
    return pl.pallas_call(
        kernel,
        out_shape=[shape(wide, F32), shape(wide, BF), shape(wide, BF), shape(few, F32), shape(message, BF), shape(message, BF), shape(few, BF)]
        + [shape(v.shape, v.dtype) for v in (rhs, turned)],
        in_specs=[smem, smem] + [VMEM] * 6 + [pl.BlockSpec(memory_space=pl.ANY)] * len(after),
        out_specs=[VMEM] * 9,
        input_output_aliases={6: 7, 7: 8},
        scratch_shapes=[
            pltpu.VMEM((N * ROWS, COLS), BF),
            pltpu.VMEM((O_ROWS, TILE), BF),
            pltpu.VMEM(wide, BF),
            pltpu.SMEM((N * SLOTS,), jnp.int32),
        ],
        compiler_params=pltpu.CompilerParams(vmem_limit_bytes=SMALL_CAP),
        cost_estimate=pl.CostEstimate(flops=2 * 768 * 512 * HALF, bytes_accessed=8 << 20, transcendentals=0),
        name="partials",
    )(pos, listed, lo_o, hi_o, op1, op2, rhs, turned, *after)


def add_beyond(near, far, from_near, from_far):
    tiles = HALF // TILE // 2

    def kernel(near_in, far_in, a, b, near_ref, far_ref):
        for j in range(tiles):
            rows = slice(SLOTS * COLS + COLS * j, SLOTS * COLS + COLS * (j + 1))
            lo = slice(TILE * j, TILE * (j + 1))
            hi = slice(HALF // 2 + TILE * j, HALF // 2 + TILE * (j + 1))
            far_ref[:, lo] = (far_in[:, lo].astype(F32) + a[rows].astype(F32)).astype(BF)
            near_ref[:, hi] = (near_in[:, hi].astype(F32) + b[rows].astype(F32)).astype(BF)

    return pl.pallas_call(
        kernel,
        out_shape=[jax.ShapeDtypeStruct((COLS, HALF), BF)] * 2,
        in_specs=[VMEM] * 4,
        out_specs=[VMEM] * 2,
        input_output_aliases={0: 0, 1: 1},
        compiler_params=pltpu.CompilerParams(vmem_limit_bytes=SMALL_CAP),
        cost_estimate=pl.CostEstimate(flops=COLS * HALF, bytes_accessed=3 << 20, transcendentals=0),
        name="add_beyond",
    )(near, far, from_near, from_far)


CORR_ONE = 1.0 - 0.8**20
CORR_TWO = 1.0 - 0.99**20


def accrue(g, m1, m2, e, w):
    top = (0.4 / CORR_ONE) * m1.astype(F32) + (0.1 / CORR_ONE) * g
    v = (0.99 / CORR_TWO) * m2.astype(F32) + (0.01 / CORR_TWO) * (g * g)
    low = v * lax.rsqrt(v) + 1e-08
    near = pltpu.reciprocal(low, approx=True)
    delta = top * (near * (2.0 - low * near)) + 0.05 * w
    return (0.95 * e.astype(F32) + delta).astype(BF)


def total(refs):
    return refs[0][...] + functools.reduce(jnp.add, [r[...].astype(F32) for r in refs[1:]])


def sent_tiles(ids, sels, m1, m2, err, weights):
    def kernel(ids_ref, *refs):
        a, b = refs[0:4], refs[4:8]
        m1_ref, m2_ref, e_ref, w_ref, out, grad = refs[8:]
        put_ids(out, SLOTS * COLS, lambda s: ids_ref[s])
        for k in range(SLOTS):
            t = ids_ref[k]
            rows = slice(COLS * k, COLS * (k + 1))

            @pl.when(t < 0)
            def _():
                out[rows] = jnp.zeros((COLS, TILE), BF)

            @pl.when(t >= 0)
            def _():
                @pl.when(t < HALF // TILE)
                def _():
                    grad[...] = total([r.at[rows] for r in a])

                @pl.when(t >= HALF // TILE)
                def _():
                    grad[...] = total([r.at[rows] for r in b])

                at = pl.ds(pl.multiple_of(t * TILE, TILE), TILE)
                out[rows] = accrue(grad[...], m1_ref[:, at], m2_ref[:, at], e_ref[:, at], w_ref[:, at])

    return pl.pallas_call(
        kernel,
        out_shape=jax.ShapeDtypeStruct((PIECE, TILE), BF),
        in_specs=[pl.BlockSpec(memory_space=pltpu.SMEM)] + [VMEM] * 12,
        out_specs=VMEM,
        scratch_shapes=[pltpu.VMEM((COLS, TILE), F32)],
        compiler_params=pltpu.CompilerParams(vmem_limit_bytes=SMALL_CAP),
        cost_estimate=pl.CostEstimate(flops=20 * SLOTS * COLS * TILE, bytes_accessed=2 << 20, transcendentals=0),
        name="sent_tiles",
    )(ids, *sels, m1, m2, err, weights)


def tied(vs, after):
    n = len(vs)
    return pl.pallas_call(
        lambda *refs: None,
        out_shape=[jax.ShapeDtypeStruct(v.shape, v.dtype) for v in vs],
        in_specs=[pl.BlockSpec(memory_space=pl.ANY)] * (n + len(after)),
        out_specs=[pl.BlockSpec(memory_space=pl.ANY)] * n,
        input_output_aliases={i: i for i in range(n)},
        compiler_params=pltpu.CompilerParams(vmem_limit_bytes=SMALL_CAP),
        cost_estimate=pl.CostEstimate(flops=0, bytes_accessed=0, transcendentals=0),
        name="tied",
    )(*vs, *after)


def pair(mine, other, *after):
    def kernel(a, b, *rest):
        rest[-1][0:PIECE] = a[...]
        rest[-1][PIECE:] = b[...]

    return pl.pallas_call(
        kernel,
        out_shape=jax.ShapeDtypeStruct((2 * PIECE, TILE), BF),
        in_specs=[VMEM] * 2 + [pl.BlockSpec(memory_space=pl.ANY)] * len(after),
        out_specs=VMEM,
        compiler_params=pltpu.CompilerParams(vmem_limit_bytes=SMALL_CAP),
        cost_estimate=pl.CostEstimate(flops=0, bytes_accessed=8 * PIECE * TILE, transcendentals=0),
        name="pair",
    )(mine, other, *after)


def own_half(both, *after):
    def kernel(ref, *rest):
        rest[-1][...] = ref[0:PIECE]

    return pl.pallas_call(
        kernel,
        out_shape=jax.ShapeDtypeStruct((PIECE, TILE), BF),
        in_specs=[VMEM] + [pl.BlockSpec(memory_space=pl.ANY)] * len(after),
        out_specs=VMEM,
        compiler_params=pltpu.CompilerParams(vmem_limit_bytes=SMALL_CAP),
        cost_estimate=pl.CostEstimate(flops=0, bytes_accessed=4 * PIECE * TILE, transcendentals=0),
        name="own_half",
    )(both, *after)


def keep_error(ids, grads, m1, m2, err, weights, part, before=None):
    width = 512
    tiles = width // TILE
    steps = HALF // width

    def kernel(ids_ref, g0, g1, g2, m1_ref, m2_ref, e_ref, w_ref, *rest):
        out, flag, kept, sems = rest[-4:]
        flag[...] = jnp.zeros_like(flag)
        copies = []
        for i in range(steps):
            for j in range(tiles):
                at = slice(width * i + TILE * j, width * i + TILE * (j + 1))
                to = slice(part * HALF + at.start, part * HALF + at.stop)
                g = total([r.at[:, at] for r in (g0, g1, g2)])
                kept[:, at] = accrue(g, m1_ref[:, to], m2_ref[:, to], e_ref[:, to], w_ref[:, to])
            for k in range(SLOTS):
                j = ids_ref[k] - part * (HALF // TILE) - i * tiles

                @pl.when((j >= 0) & (j < tiles))
                def _():
                    kept[:, pl.ds(pl.multiple_of(width * i + j * TILE, TILE), TILE)] = jnp.zeros((COLS, TILE), BF)

            copies.append(
                pltpu.make_async_copy(
                    kept.at[:, pl.ds(width * i, width)],
                    out.at[:, pl.ds(part * HALF + width * i, width)],
                    sems.at[i],
                )
            )
            copies[-1].start()
        for c in copies:
            c.wait()

    hbm = pl.BlockSpec(memory_space=pltpu.HBM)
    more = [] if before is None else [before]
    return pl.pallas_call(
        kernel,
        out_shape=[jax.ShapeDtypeStruct((COLS, FEATS), BF), jax.ShapeDtypeStruct((8, TILE), F32)],
        in_specs=[pl.BlockSpec(memory_space=pltpu.SMEM)] + [VMEM] * 7 + [hbm] * len(more),
        out_specs=[hbm, VMEM],
        input_output_aliases={8: 0} if more else {},
        scratch_shapes=[pltpu.VMEM((COLS, HALF), BF), pltpu.SemaphoreType.DMA((steps,))],
        compiler_params=pltpu.CompilerParams(vmem_limit_bytes=SMALL_CAP),
        cost_estimate=pl.CostEstimate(flops=20 * COLS * HALF, bytes_accessed=5 << 20, transcendentals=0),
        name="keep_error",
    )(ids, *grads, m1, m2, err, weights, *more)


def add_tiles(pieces, after):
    n = len(pieces)
    halves = sum(p.shape[0] // PIECE for p in pieces)

    def kernel(*refs):
        ins, (out, acc, listed) = refs[:n], refs[-3:]
        where = [(ref, h * PIECE) for ref in ins for h in range(ref.shape[0] // PIECE)]
        for at, (ref, row) in enumerate(where):
            for k, t in enumerate(get_ids(ref[row + SLOTS * COLS : row + PIECE])):
                listed[SLOTS * at + k] = t
        acc[...] = jnp.zeros_like(acc)
        for at, (ref, row) in enumerate(where):
            for k in range(SLOTS):
                t = listed[SLOTS * at + k]

                @pl.when(t >= 0)
                def _():
                    lanes = pl.ds(pl.multiple_of(t * TILE, TILE), TILE)
                    begin = row + COLS * k
                    acc[:, lanes] = acc[:, lanes] + ref[begin : begin + COLS].astype(F32)

        out[...] = (acc[...] * (1.0 / 16.0)).astype(BF)

    return pl.pallas_call(
        kernel,
        out_shape=jax.ShapeDtypeStruct((COLS, FEATS), BF),
        in_specs=[VMEM] * n + [pl.BlockSpec(memory_space=pl.ANY)] * len(after),
        scratch_shapes=[pltpu.VMEM((COLS, FEATS), F32), pltpu.SMEM((halves * SLOTS,), jnp.int32)],
        compiler_params=pltpu.CompilerParams(vmem_limit_bytes=SMALL_CAP),
        cost_estimate=pl.CostEstimate(flops=64 * 64 * 128, bytes_accessed=3 << 20, transcendentals=0),
        name="add_tiles",
    )(*pieces, *after)


def outer(mine, other, weights, momentum):
    width = 512
    steps = FEATS // width

    def kernel(m_ref, o_ref, w_ref, v_ref, w_out, v_out, w_new, v_new, sems):
        copies = []
        for i in range(steps):
            at = slice(width * i, width * (i + 1))
            agg = m_ref[:, at].astype(F32) + o_ref[:, at].astype(F32)
            vel = 0.9 * v_ref[:, at].astype(F32) + agg
            w_new[:, at] = w_ref[:, at] - 0.7 * (agg + 0.9 * vel)
            v_new[:, at] = vel.astype(BF)
            lanes = pl.ds(width * i, width)
            copies.append(pltpu.make_async_copy(w_new.at[:, lanes], w_out.at[:, lanes], sems.at[0, i]))
            copies.append(pltpu.make_async_copy(v_new.at[:, lanes], v_out.at[:, lanes], sems.at[1, i]))
            copies[-2].start()
            copies[-1].start()
        for c in copies:
            c.wait()

    hbm = pl.BlockSpec(memory_space=pltpu.HBM)
    return pl.pallas_call(
        kernel,
        out_shape=[jax.ShapeDtypeStruct((COLS, FEATS), F32), jax.ShapeDtypeStruct((COLS, FEATS), BF)],
        in_specs=[VMEM] * 4,
        out_specs=[hbm, hbm],
        scratch_shapes=[pltpu.VMEM((COLS, FEATS), F32), pltpu.VMEM((COLS, FEATS), BF), pltpu.SemaphoreType.DMA((2, steps))],
        compiler_params=pltpu.CompilerParams(vmem_limit_bytes=SMALL_CAP),
        cost_estimate=pl.CostEstimate(flops=6 * COLS * FEATS, bytes_accessed=8 << 20, transcendentals=0),
        name="outer",
    )(mine, other, weights, momentum)


def per_device(tokens, out_grad, weights, moment_one, moment_two, error_buf, momentum, tile_lists):
    tp = lax.axis_index("tp")
    pos = jnp.stack([tp // N, lax.rem(tp, N)]).astype(jnp.int32)
    tok = tokens[0]
    og4 = out_grad[0].reshape(N, N, ROWS, COLS)
    ids = tile_lists[0, 0]
    state = (moment_one[0], moment_two[0], error_buf[0], weights)

    m = pack(pos, tile_lists[0], tok, og4)
    yp, ym, xp, xm = along_y(m[0], 1), along_y(m[1], 3), along_x(m[2], 1), along_x(m[3], 3)
    y1, y2 = along_y(relay(yp, 1), 1), along_y(relay(ym, 3), 3)
    x1, x2 = along_x(relay(xp, 1), 1), along_x(relay(xm, 3), 3)

    ra = gather(pos, ids, og4, xp, xm, tok, yp, ym, 0)
    rb = gather(pos, ids, og4, yp, ym, tok, xp, xm, 1)
    pa = partials(pos, ra, x1, x2, y1, y2, 0, rb[1])
    sa = [pa[3], along_x(pa[5], 1), along_x(pa[4], 3), along_x(pa[6], 2)]
    pb = partials(pos, rb, y1, y2, x1, x2, 1, pa[3])
    sb = [pb[3], along_y(pb[5], 1), along_y(pb[4], 3), along_y(pb[6], 2)]
    near_a, far_a = add_beyond(pa[1], pa[2], sa[1], sa[2])
    near_b, far_b = add_beyond(pb[1], pb[2], sb[1], sb[2])
    ga = [pa[0], along_x(far_a, 1), along_x(near_a, 3)]
    gb = [pb[0], along_y(far_b, 1), along_y(near_b, 3)]

    mine = sent_tiles(ids, sa + sb, *state)
    own = pair(mine, across(mine))
    (z1,) = tied([onward(own)], ga[1:] + gb[1:])
    z2 = onward(z1)
    z3 = onward(z2)
    error_new, flag = keep_error(ids, ga, *state, 0)
    z4 = onward(own_half(z3, flag))
    error_new, flag = keep_error(ids, gb, *state, 1, error_new)
    agg = add_tiles([mine, z1, z2, z3, z4], [flag])
    weights_new, momentum_new = outer(agg, across(agg), weights, momentum)

    return (weights_new, error_new[None], momentum_new)


def solution(mesh):
    return jax.shard_map(
        per_device,
        mesh=mesh,
        in_specs=(
            P("rep", "tp", None),
            P("rep", None, "tp"),
            P("tp", None),
            P("rep", "tp", None),
            P("rep", "tp", None),
            P("rep", "tp", None),
            P("tp", None),
            P("rep", "tp", None),
        ),
        out_specs=(P("tp", None), P("rep", "tp", None), P("tp", None)),
        check_vma=False,
    )
```

time: 312 us -> 115 us (0.37)
  waiting for transfers between devices: 274 us -> 39.7 us
  starting transfers between devices: 0.08 us -> 51.7 us
  Pallas kernels: 0 us -> 20.5 us
  matrix products: 16.3 us -> 0 us
  between operations: 14 us -> 1.04 us
  other arithmetic: 7.17 us -> 0.08 us
    all_gather x1 -> x0, waiting for transfers between devices: 165 us -> none  [per_device(): lax.all_gather(local_rows, 'tp', axis=0, tiled=True)]
    psum x1 -> x0, waiting for transfers between devices: 109 us -> none  [per_device(): summed = lax.psum(contrib.astype(jnp.bfloat16), 'rep').astype(jnp.float32)]
    ppermute x0 -> x24, starting transfers between devices: none -> 51.7 us  [the longest x9 15.7 us: along_y(): lax.ppermute(v, 'tp', [(N * a + b, N * a + (b + s) % N) for a in range(N)...]
    ppermute x0 -> x24, waiting for transfers between devices: none -> 39.7 us  [the longest x9 21.4 us: along_x(): lax.ppermute(v, 'tp', [(N * a + b, N * ((a + s) % N) + b) for a in range(...]
    pallas_call x0 -> x19, Pallas kernels: none -> 20.5 us  [the longest x2 5.45 us: partials(): pl.pallas_call(kernel, out_shape=[shape(wide, F32), shape(wide, BF), shap...]
    dot_general x1 -> x0, matrix products: 16.3 us -> none  [per_device(): lax.dot_general(local_grad, lax.all_gather(local_rows, 'tp', axis=0, tile...]
    convert_element_type x1 -> x0, other arithmetic: 3.87 us -> none  [per_device(): return (weights_new, error_new[None], velocity.astype(jnp.bfloat16))]
  transfers between devices with their start and end apart: 2 -> 24, of which waited for: 2 -> 12; matrix products, arithmetic and copies ran while one was open for 1% -> 0% of each run, Pallas kernels for 0% -> 10%
where the time goes in v2:
time: 115 us
  starting transfers between devices  51.7 us (45%)
  waiting for transfers between devices  39.7 us (35%)
  Pallas kernels  20.5 us (18%)
  local copies, waits for them, and re-layouts  1.82 us (2%)
    ppermute x9, waiting for transfers between devices, along_x(): lax.ppermute(v, 'tp', [(N * a + b, N * ((a + s) % N) + b) for a in range(...  21.4 us
    ppermute x9, starting transfers between devices, along_y(): lax.ppermute(v, 'tp', [(N * a + b, N * a + (b + s) % N) for a in range(N)...  15.7 us
    ppermute x4, starting transfers between devices, onward(): return lax.ppermute(v, 'rep', pairs)  15.5 us
    ppermute x9, starting transfers between devices, along_x(): lax.ppermute(v, 'tp', [(N * a + b, N * ((a + s) % N) + b) for a in range(...  10.3 us
    ppermute x2, starting transfers between devices, across(): lax.ppermute(v, 'rep', [(2 * a + c, 2 * a + 1 - c) for a in range(8) for...  10.2 us
    ppermute x4, waiting for transfers between devices, onward(): return lax.ppermute(v, 'rep', pairs)  7.66 us
    ppermute x9, waiting for transfers between devices, along_y(): lax.ppermute(v, 'tp', [(N * a + b, N * a + (b + s) % N) for a in range(N)...  7.42 us
    pallas_call x2, Pallas kernels, partials(): pl.pallas_call(kernel, out_shape=[shape(wide, F32), shape(wide, BF), shap...  5.45 us
  transfers between devices with their start and end apart: 24, of which 12 were waited for; matrix products, arithmetic and copies ran while one was open for 0% of the time, Pallas kernels for 10%

profile of v2, /device:TPU:1, one launch (start us, length us, event | category | flops | bytes accessed | tf_op | source)
XLA Modules:
  0.0 114.9 jit_solution(17112663634011349853)
XLA Ops:
  2.5 3.4 %pack.1 = (bf16[4240,128]{1,0:T(8,128)(2,1)S(1)}, bf16[4240,128]{1,0:T(8,128)(2,1)S(1)}, bf16[4240,128]{1,0:T(8,128)(2,1)S(1)}, bf16[4240,128]{1,0:T(8,128)(2,1)}) custom-call(s32[2]{0:T(128)S(1)} %pad_add_fusion.pos_ref, s32[1,4]{1,0:T(1,128)S(1)} %bitcast.25, bf16[192,4096]{1,0:T(8,128)(2,1)} %bitcast.10, bf16[4,4,192,128]{3,2,1,0:T(8,128)(2,1)S(1)} %bitcast.22), custom_call_target="tpu_custom_call" | custom-call | bytes 8683520 | tf_op jit(solution)/shard_map/pack/pallas_call | solution.py:99
  5.9 2.1 %collective-permute-start = (bf16[4240,128]{1,0:T(8,128)(2,1)S(1)}, bf16[4240,128]{1,0:T(8,128)(2,1)S(1)}, u32[]{:S(2)}, u32[]{:S(2)}) collective-permute-start(bf16[4240,128]{1,0:T(8,128)(2,1)S(1)} %get-tuple-element.37), channel_id=1, source_target_pairs={{0,4},{1,5},{2,6},{3,7},{4,8},{5,9},{6,10},{7,11},{8,12},{9,13},{1... | collective-permute-start | bytes 3256328 | tf_op jit(solution)/shard_map/ppermute | solution.py:31
  8.0 1.4 %collective-permute-start.1 = (bf16[4240,128]{1,0:T(8,128)(2,1)}, bf16[4240,128]{1,0:T(8,128)(2,1)S(1)}, u32[]{:S(2)}, u32[]{:S(2)}) collective-permute-start(bf16[4240,128]{1,0:T(8,128)(2,1)} %get-tuple-element.38), channel_id=1, source_target_pairs={{0,12},{1,13},{2,14},{3,15},{4,0},{5,1},{6,2},{7,3},{8,4},{9,5},{1... | collective-permute-start | bytes 3256328 | tf_op jit(solution)/shard_map/ppermute | solution.py:31
  9.3 1.4 %collective-permute-start.2 = (bf16[4240,128]{1,0:T(8,128)(2,1)S(1)}, bf16[4240,128]{1,0:T(8,128)(2,1)S(1)}, u32[]{:S(2)}, u32[]{:S(2)}) collective-permute-start(bf16[4240,128]{1,0:T(8,128)(2,1)S(1)} %get-tuple-element.39), channel_id=1, source_target_pairs={{0,1},{1,2},{2,3},{3,0},{4,5},{5,6},{6,7},{7,4},{8,9},{9,10},{10,1... | collective-permute-start | bytes 3256328 | tf_op jit(solution)/shard_map/ppermute | solution.py:35
  10.8 1.4 %collective-permute-start.3 = (bf16[4240,128]{1,0:T(8,128)(2,1)S(1)}, bf16[4240,128]{1,0:T(8,128)(2,1)S(1)}, u32[]{:S(2)}, u32[]{:S(2)}) collective-permute-start(bf16[4240,128]{1,0:T(8,128)(2,1)S(1)} %get-tuple-element.40), channel_id=1, source_target_pairs={{0,3},{1,0},{2,1},{3,2},{4,7},{5,4},{6,5},{7,6},{8,11},{9,8},{10,9... | collective-permute-start | bytes 3256328 | tf_op jit(solution)/shard_map/ppermute | solution.py:35
  12.2 18.4 %collective-permute-done.n_o.ref.l = bf16[4240,128]{1,0:T(8,128)(2,1)S(1)} collective-permute-done((bf16[4240,128]{1,0:T(8,128)(2,1)S(1)}, bf16[4240,128]{1,0:T(8,128)(2,1)S(1)}, u32[]{:S(2)}, u32[]{:S(2)}) %collective-permute-start) | collective-permute-done | bytes 1085472 | tf_op jit(solution)/shard_map/ppermute | solution.py:31
  30.7 2.0 %collective-permute-start.4 = (bf16[1936,128]{1,0:T(8,128)(2,1)S(1)}, bf16[1936,128]{1,0:T(8,128)(2,1)S(1)}, u32[]{:S(2)}, u32[]{:S(2)}) collective-permute-start(bf16[1936,128]{1,0:T(8,128)(2,1)S(1)} %relay.4), channel_id=1, source_target_pairs={{0,4},{1,5},{2,6},{3,7},{4,8},{5,9},{6,10},{7,11},{8,12},{9,13},{1... | collective-permute-start | bytes 1486856 | tf_op jit(solution)/shard_map/ppermute | solution.py:31
  32.7 1.7 %collective-permute-start.5 = (bf16[1936,128]{1,0:T(8,128)(2,1)S(1)}, bf16[1936,128]{1,0:T(8,128)(2,1)S(1)}, u32[]{:S(2)}, u32[]{:S(2)}) collective-permute-start(bf16[1936,128]{1,0:T(8,128)(2,1)S(1)} %relay.5), channel_id=1, source_target_pairs={{0,12},{1,13},{2,14},{3,15},{4,0},{5,1},{6,2},{7,3},{8,4},{9,5},{1... | collective-permute-start | bytes 1486856 | tf_op jit(solution)/shard_map/ppermute | solution.py:31
  34.4 2.8 %collective-permute-start.6 = (bf16[1936,128]{1,0:T(8,128)(2,1)S(1)}, bf16[1936,128]{1,0:T(8,128)(2,1)S(1)}, u32[]{:S(2)}, u32[]{:S(2)}) collective-permute-start(bf16[1936,128]{1,0:T(8,128)(2,1)S(1)} %relay.6), channel_id=1, source_target_pairs={{0,1},{1,2},{2,3},{3,0},{4,5},{5,6},{6,7},{7,4},{8,9},{9,10},{10,1... | collective-permute-start | bytes 1486856 | tf_op jit(solution)/shard_map/ppermute | solution.py:35
  37.2 1.5 %collective-permute-start.7 = (bf16[1936,128]{1,0:T(8,128)(2,1)S(1)}, bf16[1936,128]{1,0:T(8,128)(2,1)S(1)}, u32[]{:S(2)}, u32[]{:S(2)}) collective-permute-start(bf16[1936,128]{1,0:T(8,128)(2,1)S(1)} %relay.7), channel_id=1, source_target_pairs={{0,3},{1,0},{2,1},{3,2},{4,7},{5,4},{6,5},{7,6},{8,11},{9,8},{10,9... | collective-permute-start | bytes 1486856 | tf_op jit(solution)/shard_map/ppermute | solution.py:35
  40.0 1.3 %gather.2 = (bf16[768,2048]{1,0:T(8,128)(2,1)S(1)}, bf16[512,768]{1,0:T(8,128)(2,1)S(1)}, s32[16]{0:T(128)S(1)}) custom-call(s32[2]{0:T(128)S(1)} %pad_add_fusion.pos_ref, s32[4]{0:T(128)S(1)} %bitcast.27, bf16[4,4,192,128]{3,2,1,0:T(8,128)(2,1)S(1)} %bitcast.24, bf16[4240,128]{1,0:T(8,128)(2,1)S(1)} %collective-permute-done.n_o.ref.l, ...), custom_call_target="tpu_custom_call" | custom-call | bytes 8388608 | tf_op jit(solution)/shard_map/gather/pallas_call | solution.py:163
  41.3 1.4 %collective-permute-done.4.lo.a = bf16[1936,128]{1,0:T(8,128)(2,1)S(1)} collective-permute-done((bf16[1936,128]{1,0:T(8,128)(2,1)S(1)}, bf16[1936,128]{1,0:T(8,128)(2,1)S(1)}, u32[]{:S(2)}, u32[]{:S(2)}) %collective-permute-start.4) | collective-permute-done | bytes 495648 | tf_op jit(solution)/shard_map/ppermute | solution.py:31
  43.5 4.6 %collective-permute-done.6.a.lo = bf16[1936,128]{1,0:T(8,128)(2,1)S(1)} collective-permute-done((bf16[1936,128]{1,0:T(8,128)(2,1)S(1)}, bf16[1936,128]{1,0:T(8,128)(2,1)S(1)}, u32[]{:S(2)}, u32[]{:S(2)}) %collective-permute-start.6) | collective-permute-done | bytes 495648 | tf_op jit(solution)/shard_map/ppermute | solution.py:35
  48.1 2.7 %partials.2 = (f32[128,2048]{1,0:T(8,128)S(1)}, bf16[128,2048]{1,0:T(8,128)(2,1)S(1)}, bf16[128,2048]{1,0:T(8,128)(2,1)S(1)}, f32[512,128]{1,0:T(8,128)S(1)}, bf...) custom-call(s32[2]{0:T(128)S(1)} %pad_add_fusion.pos_ref, ...), custom_call_target="tpu_custom_call", output_to_operand_aliasing={{7}: (6, {}), {8}: (7, {})} | custom-call | flops 1610612736 | bytes 8388608 | tf_op jit(solution)/shard_map/partials/pallas_call | solution.py:224
  50.9 2.7 %collective-permute-start.9 = (bf16[1536,128]{1,0:T(8,128)(2,1)S(1)}, bf16[1536,128]{1,0:T(8,128)(2,1)S(1)}, u32[]{:S(2)}, u32[]{:S(2)}) collective-permute-start(bf16[1536,128]{1,0:T(8,128)(2,1)S(1)} %get-tuple-element.47), channel_id=1, source_target_pairs={{0,12},{1,13},{2,14},{3,15},{4,0},{5,1},{6,2},{7,3},{8,4},{9,5},{1... | collective-permute-start | bytes 1179656 | tf_op jit(solution)/shard_map/ppermute | solution.py:31
  53.6 2.7 %partials.3 = (f32[128,2048]{1,0:T(8,128)S(1)}, bf16[128,2048]{1,0:T(8,128)(2,1)S(1)}, bf16[128,2048]{1,0:T(8,128)(2,1)S(1)}, f32[512,128]{1,0:T(8,128)S(1)}, bf...) custom-call(s32[2]{0:T(128)S(1)} %pad_add_fusion.pos_ref, ...), custom_call_target="tpu_custom_call", output_to_operand_aliasing={{7}: (6, {}), {8}: (7, {})} | custom-call | flops 1610612736 | bytes 8388608 | tf_op jit(solution)/shard_map/partials/pallas_call | solution.py:224
  57.3 1.8 %collective-permute-start.12 = (bf16[1536,128]{1,0:T(8,128)(2,1)S(1)}, bf16[1536,128]{1,0:T(8,128)(2,1)S(1)}, u32[]{:S(2)}, u32[]{:S(2)}) collective-permute-start(bf16[1536,128]{1,0:T(8,128)(2,1)S(1)} %get-tuple-element.53), channel_id=1, source_target_pairs={{0,3},{1,0},{2,1},{3,2},{4,7},{5,4},{6,5},{7,6},{8,11},{9,8},{10,9... | collective-permute-start | bytes 1179656 | tf_op jit(solution)/shard_map/ppermute | solution.py:35
  59.8 1.8 %collective-permute-start.13 = (bf16[512,128]{1,0:T(8,128)(2,1)S(1)}, bf16[512,128]{1,0:T(8,128)(2,1)S(1)}, u32[]{:S(2)}, u32[]{:S(2)}) collective-permute-start(bf16[512,128]{1,0:T(8,128)(2,1)S(1)} %get-tuple-element.54), channel_id=1, source_target_pairs={{0,2},{1,3},{2,0},{3,1},{4,6},{5,7},{6,4},{7,5},{8,10},{9,11},{10,... | collective-permute-start | bytes 393224 | tf_op jit(solution)/shard_map/ppermute | solution.py:35
  62.0 2.7 %collective-permute-done.11.refs_5_.a = bf16[1536,128]{1,0:T(8,128)(2,1)S(1)} collective-permute-done((bf16[1536,128]{1,0:T(8,128)(2,1)S(1)}, bf16[1536,128]{1,0:T(8,128)(2,1)S(1)}, u32[]{:S(2)}, u32[]{:S(2)}) %collective-permute-start.11) | collective-permute-done | bytes 393248 | tf_op jit(solution)/shard_map/ppermute | solution.py:35
  66.2 3.2 %collective-permute-start.19 = (bf16[128,2048]{1,0:T(8,128)(2,1)S(1)}, bf16[128,2048]{1,0:T(8,128)(2,1)S(1)}, u32[]{:S(2)}, u32[]{:S(2)}) collective-permute-start(bf16[128,2048]{1,0:T(8,128)(2,1)S(1)} %get-tuple-element.62), channel_id=1, source_target_pairs={{0,3},{1,0},{2,1},{3,2},{4,7},{5,4},{6,5},{7,6},{8,11},{9,8},{10,9... | collective-permute-start | bytes 1572872 | tf_op jit(solution)/shard_map/ppermute | solution.py:35
  70.4 5.4 %collective-permute-start.14 = (bf16[528,128]{1,0:T(8,128)(2,1)S(1)}, bf16[528,128]{1,0:T(8,128)(2,1)S(1)}, u32[]{:S(2)}, u32[]{:S(2)}) collective-permute-start(bf16[528,128]{1,0:T(8,128)(2,1)S(1)} %sent_tiles.1.a.refs_0_), channel_id=1, source_target_pairs={{0,16},{16,0},{32,48},{48,32},{64,80},{80,64},{96,112},{112,96},{1... | collective-permute-start | bytes 405512 | tf_op jit(solution)/shard_map/ppermute | solution.py:44
  76.8 6.0 %collective-permute-start.15 = (bf16[1056,128]{1,0:T(8,128)(2,1)S(1)}, bf16[1056,128]{1,0:T(8,128)(2,1)S(1)}, u32[]{:S(2)}, u32[]{:S(2)}) collective-permute-start(bf16[1056,128]{1,0:T(8,128)(2,1)S(1)} %pair.1), channel_id=1, source_target_pairs={{0,32},{32,64},{64,96},{96,128},{128,160},{160,192},{192,224},{224... | collective-permute-start | bytes 811016 | tf_op jit(solution)/shard_map/ppermute | solution.py:40
  82.8 3.4 %collective-permute-done.15.refs_0_ = bf16[1056,128]{1,0:T(8,128)(2,1)S(1)} collective-permute-done((bf16[1056,128]{1,0:T(8,128)(2,1)S(1)}, bf16[1056,128]{1,0:T(8,128)(2,1)S(1)}, u32[]{:S(2)}, u32[]{:S(2)}) %collective-permute-start.15) | collective-permute-done | bytes 270368 | tf_op jit(solution)/shard_map/ppermute | solution.py:40
  86.2 3.2 %collective-permute-start.20 = (bf16[1056,128]{1,0:T(8,128)(2,1)S(1)}, bf16[1056,128]{1,0:T(8,128)(2,1)S(1)}, u32[]{:S(2)}, u32[]{:S(2)}) collective-permute-start(bf16[1056,128]{1,0:T(8,128)(2,1)S(1)} %tied.1.refs_1_), channel_id=1, source_target_pairs={{0,32},{32,64},{64,96},{96,128},{128,160},{160,192},{192,224},{224... | collective-permute-start | bytes 811016 | tf_op jit(solution)/shard_map/ppermute | solution.py:40
  89.4 3.4 %collective-permute-done.20.refs_2_ = bf16[1056,128]{1,0:T(8,128)(2,1)S(1)} collective-permute-done((bf16[1056,128]{1,0:T(8,128)(2,1)S(1)}, bf16[1056,128]{1,0:T(8,128)(2,1)S(1)}, u32[]{:S(2)}, u32[]{:S(2)}) %collective-permute-start.20) | collective-permute-done | bytes 270368 | tf_op jit(solution)/shard_map/ppermute | solution.py:40
  92.8 3.1 %collective-permute-start.21 = (bf16[1056,128]{1,0:T(8,128)(2,1)S(1)}, bf16[1056,128]{1,0:T(8,128)(2,1)S(1)}, u32[]{:S(2)}, u32[]{:S(2)}) collective-permute-start(bf16[1056,128]{1,0:T(8,128)(2,1)S(1)} %collective-permute-done.20.refs_2_), channel_id=1, source_target_pairs={{0,32},{32,64},{64,96},{96,128},{128,160},{160,192},{192,224},{224... | collective-permute-start | bytes 811016 | tf_op jit(solution)/shard_map/ppermute | solution.py:40
  95.9 2.5 %keep_error.2 = (bf16[128,4096]{1,0:T(8,128)(2,1)}, f32[8,128]{1,0:T(8,128)S(1)}) custom-call(s32[4]{0:T(128)S(1)} %bitcast.29, f32[128,2048]{1,0:T(8,128)S(1)} %get-tuple-element.63.g0, bf16[128,2048]{1,0:T(8,128)(2,1)S(1)} %collective-permute-done.16.refs_1_.g1, bf16[128,2048]{1,0:T(8,128)(2,1)S(1)} %collective-permute-done.17.refs_2_.g2, ...), custom_call_target="tpu_custom_call" | custom-call | flops 5242880 | bytes 5242880 | tf_op jit(solution)/shard_map/keep_error/pallas_call | solution.py:401
  99.3 3.2 %collective-permute-start.22 = (bf16[528,128]{1,0:T(8,128)(2,1)S(1)}, bf16[528,128]{1,0:T(8,128)(2,1)S(1)}, u32[]{:S(2)}, u32[]{:S(2)}) collective-permute-start(bf16[528,128]{1,0:T(8,128)(2,1)S(1)} %own_half.1), channel_id=1, source_target_pairs={{0,32},{32,64},{64,96},{96,128},{128,160},{160,192},{192,224},{224... | collective-permute-start | bytes 405512 | tf_op jit(solution)/shard_map/ppermute | solution.py:40
  102.5 2.3 %keep_error.3 = (bf16[128,4096]{1,0:T(8,128)(2,1)}, f32[8,128]{1,0:T(8,128)S(1)}) custom-call(s32[4]{0:T(128)S(1)} %bitcast.30, f32[128,2048]{1,0:T(8,128)S(1)} %get-tuple-element.65.g0, bf16[128,2048]{1,0:T(8,128)(2,1)S(1)} %collective-permute-done.18.refs_3_.g1, ...), custom_call_target="tpu_custom_call", output_to_operand_aliasing={{0}: (8, {})} | custom-call | flops 5242880 | bytes 5242880 | tf_op jit(solution)/shard_map/keep_error/pallas_call | solution.py:401
  105.6 4.9 %collective-permute-start.23 = (bf16[128,4096]{1,0:T(8,128)(2,1)S(1)}, bf16[128,4096]{1,0:T(8,128)(2,1)S(1)}, u32[]{:S(2)}, u32[]{:S(2)}) collective-permute-start(bf16[128,4096]{1,0:T(8,128)(2,1)S(1)} %add_tiles.1.m_ref), channel_id=1, source_target_pairs={{0,16},{16,0},{32,48},{48,32},{64,80},{80,64},{96,112},{112,96},{1... | collective-permute-start | bytes 3145736 | tf_op jit(solution)/shard_map/ppermute | solution.py:44
  110.5 2.3 %collective-permute-done.23.o_ref = bf16[128,4096]{1,0:T(8,128)(2,1)S(1)} collective-permute-done((bf16[128,4096]{1,0:T(8,128)(2,1)S(1)}, bf16[128,4096]{1,0:T(8,128)(2,1)S(1)}, u32[]{:S(2)}, u32[]{:S(2)}) %collective-permute-start.23) | collective-permute-done | bytes 1048608 | tf_op jit(solution)/shard_map/ppermute | solution.py:44
  112.8 1.9 %outer.1 = (f32[128,4096]{1,0:T(8,128)}, bf16[128,4096]{1,0:T(8,128)(2,1)}) custom-call(bf16[128,4096]{1,0:T(8,128)(2,1)S(1)} %add_tiles.1.m_ref, bf16[128,4096]{1,0:T(8,128)(2,1)S(1)} %collective-permute-done.23.o_ref, f32[128,4096]{1,0:T(8,128)S(1)} %copy-done, bf16[128,4096]{1,0:T(8,128)(2,1)S(1)} %copy-done.6), custom_call_target="tpu_custom_call" | custom-call | flops 3145728 | bytes 8388608 | tf_op jit(solution)/shard_map/outer/pallas_call | solution.py:469
  (52 shorter events, 11.3 us)
Async XLA Ops:
  0.7 1.1 copy-start.5
  1.9 0.7 copy-start.7
  5.9 24.8 %collective-permute-start = (bf16[4240,128]{1,0:T(8,128)(2,1)S(1)}, bf16[4240,128]{1,0:T(8,128)(2,1)S(1)}, u32[]{:S(2)}, u32[]{:S(2)}) collective-permute-start(bf16[4240,128]{1,0:T(8,128)(2,1)S(1)} %get-tuple-element.37), channel_id=1, source_target_pairs={{0,4},{1,5},{2,6},{3,7},{4,8},{5,9},{6,10},{7,11},{8,12},{9,13},{1... | collective-permute-start | bytes 3256328 | tf_op jit(solution)/shard_map/ppermute | solution.py:31
  8.0 24.6 %collective-permute-start.1 = (bf16[4240,128]{1,0:T(8,128)(2,1)}, bf16[4240,128]{1,0:T(8,128)(2,1)S(1)}, u32[]{:S(2)}, u32[]{:S(2)}) collective-permute-start(bf16[4240,128]{1,0:T(8,128)(2,1)} %get-tuple-element.38), channel_id=1, source_target_pairs={{0,12},{1,13},{2,14},{3,15},{4,0},{5,1},{6,2},{7,3},{8,4},{9,5},{1... | collective-permute-start | bytes 3256328 | tf_op jit(solution)/shard_map/ppermute | solution.py:31
  9.3 25.0 %collective-permute-start.2 = (bf16[4240,128]{1,0:T(8,128)(2,1)S(1)}, bf16[4240,128]{1,0:T(8,128)(2,1)S(1)}, u32[]{:S(2)}, u32[]{:S(2)}) collective-permute-start(bf16[4240,128]{1,0:T(8,128)(2,1)S(1)} %get-tuple-element.39), channel_id=1, source_target_pairs={{0,1},{1,2},{2,3},{3,0},{4,5},{5,6},{6,7},{7,4},{8,9},{9,10},{10,1... | collective-permute-start | bytes 3256328 | tf_op jit(solution)/shard_map/ppermute | solution.py:35
  10.8 26.4 %collective-permute-start.3 = (bf16[4240,128]{1,0:T(8,128)(2,1)S(1)}, bf16[4240,128]{1,0:T(8,128)(2,1)S(1)}, u32[]{:S(2)}, u32[]{:S(2)}) collective-permute-start(bf16[4240,128]{1,0:T(8,128)(2,1)S(1)} %get-tuple-element.40), channel_id=1, source_target_pairs={{0,3},{1,0},{2,1},{3,2},{4,7},{5,4},{6,5},{7,6},{8,11},{9,8},{10,9... | collective-permute-start | bytes 3256328 | tf_op jit(solution)/shard_map/ppermute | solution.py:35
  30.7 12.1 %collective-permute-start.4 = (bf16[1936,128]{1,0:T(8,128)(2,1)S(1)}, bf16[1936,128]{1,0:T(8,128)(2,1)S(1)}, u32[]{:S(2)}, u32[]{:S(2)}) collective-permute-start(bf16[1936,128]{1,0:T(8,128)(2,1)S(1)} %relay.4), channel_id=1, source_target_pairs={{0,4},{1,5},{2,6},{3,7},{4,8},{5,9},{6,10},{7,11},{8,12},{9,13},{1... | collective-permute-start | bytes 1486856 | tf_op jit(solution)/shard_map/ppermute | solution.py:31
  32.7 10.8 %collective-permute-start.5 = (bf16[1936,128]{1,0:T(8,128)(2,1)S(1)}, bf16[1936,128]{1,0:T(8,128)(2,1)S(1)}, u32[]{:S(2)}, u32[]{:S(2)}) collective-permute-start(bf16[1936,128]{1,0:T(8,128)(2,1)S(1)} %relay.5), channel_id=1, source_target_pairs={{0,12},{1,13},{2,14},{3,15},{4,0},{5,1},{6,2},{7,3},{8,4},{9,5},{1... | collective-permute-start | bytes 1486856 | tf_op jit(solution)/shard_map/ppermute | solution.py:31
  34.4 4.4 %copy-start.1 = (bf16[1,192,4096]{2,1,0:T(8,128)(2,1)S(1)}, bf16[1,192,4096]{2,1,0:T(8,128)(2,1)}, u32[]{:S(2)}) copy-start(bf16[1,192,4096]{2,1,0:T(8,128)(2,1)} %param.8) | copy-start | bytes 4718596
  34.4 13.7 %collective-permute-start.6 = (bf16[1936,128]{1,0:T(8,128)(2,1)S(1)}, bf16[1936,128]{1,0:T(8,128)(2,1)S(1)}, u32[]{:S(2)}, u32[]{:S(2)}) collective-permute-start(bf16[1936,128]{1,0:T(8,128)(2,1)S(1)} %relay.6), channel_id=1, source_target_pairs={{0,1},{1,2},{2,3},{3,0},{4,5},{5,6},{6,7},{7,4},{8,9},{9,10},{10,1... | collective-permute-start | bytes 1486856 | tf_op jit(solution)/shard_map/ppermute | solution.py:35
  37.2 10.9 %collective-permute-start.7 = (bf16[1936,128]{1,0:T(8,128)(2,1)S(1)}, bf16[1936,128]{1,0:T(8,128)(2,1)S(1)}, u32[]{:S(2)}, u32[]{:S(2)}) collective-permute-start(bf16[1936,128]{1,0:T(8,128)(2,1)S(1)} %relay.7), channel_id=1, source_target_pairs={{0,3},{1,0},{2,1},{3,2},{4,7},{5,4},{6,5},{7,6},{8,11},{9,8},{10,9... | collective-permute-start | bytes 1486856 | tf_op jit(solution)/shard_map/ppermute | solution.py:35
  50.8 9.0 %collective-permute-start.8 = (bf16[1536,128]{1,0:T(8,128)(2,1)S(1)}, bf16[1536,128]{1,0:T(8,128)(2,1)S(1)}, u32[]{:S(2)}, u32[]{:S(2)}) collective-permute-start(bf16[1536,128]{1,0:T(8,128)(2,1)S(1)} %get-tuple-element.46), channel_id=1, source_target_pairs={{0,4},{1,5},{2,6},{3,7},{4,8},{5,9},{6,10},{7,11},{8,12},{9,13},{1... | collective-permute-start | bytes 1179656 | tf_op jit(solution)/shard_map/ppermute | solution.py:31
  50.9 10.7 %collective-permute-start.9 = (bf16[1536,128]{1,0:T(8,128)(2,1)S(1)}, bf16[1536,128]{1,0:T(8,128)(2,1)S(1)}, u32[]{:S(2)}, u32[]{:S(2)}) collective-permute-start(bf16[1536,128]{1,0:T(8,128)(2,1)S(1)} %get-tuple-element.47), channel_id=1, source_target_pairs={{0,12},{1,13},{2,14},{3,15},{4,0},{5,1},{6,2},{7,3},{8,4},{9,5},{1... | collective-permute-start | bytes 1179656 | tf_op jit(solution)/shard_map/ppermute | solution.py:31
  53.6 15.9 %copy-start.3 = (bf16[1,128,4096]{2,1,0:T(8,128)(2,1)S(1)}, bf16[1,128,4096]{2,1,0:T(8,128)(2,1)}, u32[]{:S(2)}) copy-start(bf16[1,128,4096]{2,1,0:T(8,128)(2,1)} %param.12) | copy-start | bytes 3145732
  53.6 15.9 %copy-start.4 = (bf16[1,128,4096]{2,1,0:T(8,128)(2,1)S(1)}, bf16[1,128,4096]{2,1,0:T(8,128)(2,1)}, u32[]{:S(2)}) copy-start(bf16[1,128,4096]{2,1,0:T(8,128)(2,1)} %param.13) | copy-start | bytes 3145732
  56.3 8.4 %collective-permute-start.11 = (bf16[1536,128]{1,0:T(8,128)(2,1)S(1)}, bf16[1536,128]{1,0:T(8,128)(2,1)S(1)}, u32[]{:S(2)}, u32[]{:S(2)}) collective-permute-start(bf16[1536,128]{1,0:T(8,128)(2,1)S(1)} %get-tuple-element.52), channel_id=1, source_target_pairs={{0,1},{1,2},{2,3},{3,0},{4,5},{5,6},{6,7},{7,4},{8,9},{9,10},{10,1... | collective-permute-start | bytes 1179656 | tf_op jit(solution)/shard_map/ppermute | solution.py:35
  57.3 7.9 %collective-permute-start.12 = (bf16[1536,128]{1,0:T(8,128)(2,1)S(1)}, bf16[1536,128]{1,0:T(8,128)(2,1)S(1)}, u32[]{:S(2)}, u32[]{:S(2)}) collective-permute-start(bf16[1536,128]{1,0:T(8,128)(2,1)S(1)} %get-tuple-element.53), channel_id=1, source_target_pairs={{0,3},{1,0},{2,1},{3,2},{4,7},{5,4},{6,5},{7,6},{8,11},{9,8},{10,9... | collective-permute-start | bytes 1179656 | tf_op jit(solution)/shard_map/ppermute | solution.py:35
  59.0 7.2 %collective-permute-start.10 = (bf16[512,128]{1,0:T(8,128)(2,1)S(1)}, bf16[512,128]{1,0:T(8,128)(2,1)S(1)}, u32[]{:S(2)}, u32[]{:S(2)}) collective-permute-start(bf16[512,128]{1,0:T(8,128)(2,1)S(1)} %get-tuple-element.48), channel_id=1, source_target_pairs={{0,8},{1,9},{2,10},{3,11},{4,12},{5,13},{6,14},{7,15},{8,0},{9,1},... | collective-permute-start | bytes 393224 | tf_op jit(solution)/shard_map/ppermute | solution.py:31
  59.8 9.7 %collective-permute-start.13 = (bf16[512,128]{1,0:T(8,128)(2,1)S(1)}, bf16[512,128]{1,0:T(8,128)(2,1)S(1)}, u32[]{:S(2)}, u32[]{:S(2)}) collective-permute-start(bf16[512,128]{1,0:T(8,128)(2,1)S(1)} %get-tuple-element.54), channel_id=1, source_target_pairs={{0,2},{1,3},{2,0},{3,1},{4,6},{5,7},{6,4},{7,5},{8,10},{9,11},{10,... | collective-permute-start | bytes 393224 | tf_op jit(solution)/shard_map/ppermute | solution.py:35
  61.6 7.9 %copy-start = (f32[128,4096]{1,0:T(8,128)S(1)}, f32[128,4096]{1,0:T(8,128)}, u32[]{:S(2)}) copy-start(f32[128,4096]{1,0:T(8,128)} %w_ref.5) | copy-start | bytes 6291460
  61.9 7.6 %copy-start.2 = (bf16[1,128,4096]{2,1,0:T(8,128)(2,1)S(1)}, bf16[1,128,4096]{2,1,0:T(8,128)(2,1)}, u32[]{:S(2)}) copy-start(bf16[1,128,4096]{2,1,0:T(8,128)(2,1)} %param.11) | copy-start | bytes 3145732
  61.9 24.3 %collective-permute-start.16 = (bf16[128,2048]{1,0:T(8,128)(2,1)S(1)}, bf16[128,2048]{1,0:T(8,128)(2,1)S(1)}, u32[]{:S(2)}, u32[]{:S(2)}) collective-permute-start(bf16[128,2048]{1,0:T(8,128)(2,1)S(1)} %get-tuple-element.57), channel_id=1, source_target_pairs={{0,4},{1,5},{2,6},{3,7},{4,8},{5,9},{6,10},{7,11},{8,12},{9,13},{1... | collective-permute-start | bytes 1572872 | tf_op jit(solution)/shard_map/ppermute | solution.py:31
  64.7 21.5 %collective-permute-start.17 = (bf16[128,2048]{1,0:T(8,128)(2,1)S(1)}, bf16[128,2048]{1,0:T(8,128)(2,1)S(1)}, u32[]{:S(2)}, u32[]{:S(2)}) collective-permute-start(bf16[128,2048]{1,0:T(8,128)(2,1)S(1)} %get-tuple-element.58), channel_id=1, source_target_pairs={{0,12},{1,13},{2,14},{3,15},{4,0},{5,1},{6,2},{7,3},{8,4},{9,5},{1... | collective-permute-start | bytes 1572872 | tf_op jit(solution)/shard_map/ppermute | solution.py:31
  65.5 20.7 %collective-permute-start.18 = (bf16[128,2048]{1,0:T(8,128)(2,1)S(1)}, bf16[128,2048]{1,0:T(8,128)(2,1)S(1)}, u32[]{:S(2)}, u32[]{:S(2)}) collective-permute-start(bf16[128,2048]{1,0:T(8,128)(2,1)S(1)} %get-tuple-element.61), channel_id=1, source_target_pairs={{0,1},{1,2},{2,3},{3,0},{4,5},{5,6},{6,7},{7,4},{8,9},{9,10},{10,1... | collective-permute-start | bytes 1572872 | tf_op jit(solution)/shard_map/ppermute | solution.py:35
  66.2 20.0 %collective-permute-start.19 = (bf16[128,2048]{1,0:T(8,128)(2,1)S(1)}, bf16[128,2048]{1,0:T(8,128)(2,1)S(1)}, u32[]{:S(2)}, u32[]{:S(2)}) collective-permute-start(bf16[128,2048]{1,0:T(8,128)(2,1)S(1)} %get-tuple-element.62), channel_id=1, source_target_pairs={{0,3},{1,0},{2,1},{3,2},{4,7},{5,4},{6,5},{7,6},{8,11},{9,8},{10,9... | collective-permute-start | bytes 1572872 | tf_op jit(solution)/shard_map/ppermute | solution.py:35
  70.4 6.4 %collective-permute-start.14 = (bf16[528,128]{1,0:T(8,128)(2,1)S(1)}, bf16[528,128]{1,0:T(8,128)(2,1)S(1)}, u32[]{:S(2)}, u32[]{:S(2)}) collective-permute-start(bf16[528,128]{1,0:T(8,128)(2,1)S(1)} %sent_tiles.1.a.refs_0_), channel_id=1, source_target_pairs={{0,16},{16,0},{32,48},{48,32},{64,80},{80,64},{96,112},{112,96},{1... | collective-permute-start | bytes 405512 | tf_op jit(solution)/shard_map/ppermute | solution.py:44
  76.8 9.4 %collective-permute-start.15 = (bf16[1056,128]{1,0:T(8,128)(2,1)S(1)}, bf16[1056,128]{1,0:T(8,128)(2,1)S(1)}, u32[]{:S(2)}, u32[]{:S(2)}) collective-permute-start(bf16[1056,128]{1,0:T(8,128)(2,1)S(1)} %pair.1), channel_id=1, source_target_pairs={{0,32},{32,64},{64,96},{96,128},{128,160},{160,192},{192,224},{224... | collective-permute-start | bytes 811016 | tf_op jit(solution)/shard_map/ppermute | solution.py:40
  86.2 6.6 %collective-permute-start.20 = (bf16[1056,128]{1,0:T(8,128)(2,1)S(1)}, bf16[1056,128]{1,0:T(8,128)(2,1)S(1)}, u32[]{:S(2)}, u32[]{:S(2)}) collective-permute-start(bf16[1056,128]{1,0:T(8,128)(2,1)S(1)} %tied.1.refs_1_), channel_id=1, source_target_pairs={{0,32},{32,64},{64,96},{96,128},{128,160},{160,192},{192,224},{224... | collective-permute-start | bytes 811016 | tf_op jit(solution)/shard_map/ppermute | solution.py:40
  92.8 6.5 %collective-permute-start.21 = (bf16[1056,128]{1,0:T(8,128)(2,1)S(1)}, bf16[1056,128]{1,0:T(8,128)(2,1)S(1)}, u32[]{:S(2)}, u32[]{:S(2)}) collective-permute-start(bf16[1056,128]{1,0:T(8,128)(2,1)S(1)} %collective-permute-done.20.refs_2_), channel_id=1, source_target_pairs={{0,32},{32,64},{64,96},{96,128},{128,160},{160,192},{192,224},{224... | collective-permute-start | bytes 811016 | tf_op jit(solution)/shard_map/ppermute | solution.py:40
  99.3 5.6 %collective-permute-start.22 = (bf16[528,128]{1,0:T(8,128)(2,1)S(1)}, bf16[528,128]{1,0:T(8,128)(2,1)S(1)}, u32[]{:S(2)}, u32[]{:S(2)}) collective-permute-start(bf16[528,128]{1,0:T(8,128)(2,1)S(1)} %own_half.1), channel_id=1, source_target_pairs={{0,32},{32,64},{64,96},{96,128},{128,160},{160,192},{192,224},{224... | collective-permute-start | bytes 405512 | tf_op jit(solution)/shard_map/ppermute | solution.py:40
  104.9 7.9 %copy-start.6 = (bf16[128,4096]{1,0:T(8,128)(2,1)S(1)}, bf16[128,4096]{1,0:T(8,128)(2,1)}, u32[]{:S(2)}) copy-start(bf16[128,4096]{1,0:T(8,128)(2,1)} %v_ref.1) | copy-start | bytes 3145732
  105.6 7.2 %collective-permute-start.23 = (bf16[128,4096]{1,0:T(8,128)(2,1)S(1)}, bf16[128,4096]{1,0:T(8,128)(2,1)S(1)}, u32[]{:S(2)}, u32[]{:S(2)}) collective-permute-start(bf16[128,4096]{1,0:T(8,128)(2,1)S(1)} %add_tiles.1.m_ref), channel_id=1, source_target_pairs={{0,16},{16,0},{32,48},{48,32},{64,80},{80,64},{96,112},{112,96},{1... | collective-permute-start | bytes 3145736 | tf_op jit(solution)/shard_map/ppermute | solution.py:44

commit v3 on v2

--- a/solution.py
+++ b/solution.py
@@ -23,7 +23,6 @@
 BF = jnp.bfloat16
 F32 = jnp.float32
 SMALL_CAP = 8 * 1024 * 1024
-PACK_CAP = 50 * 1024 * 1024
 VMEM = pl.BlockSpec(memory_space=pltpu.VMEM)
 
 
@@ -35,8 +34,8 @@
     return lax.ppermute(v, "tp", [(N * a + b, N * a + (b + s) % N) for a in range(N) for b in range(N)])
 
 
-def onward(v):
-    pairs = [(2 * a, 2 * ((a + 1) % 8)) for a in range(8)] + [(2 * a + 1, 2 * ((a + 7) % 8) + 1) for a in range(8)]
+def onward(v, s):
+    pairs = [(2 * a, 2 * ((a + s) % 8)) for a in range(8)] + [(2 * a + 1, 2 * ((a + 8 - s) % 8) + 1) for a in range(8)]
     return lax.ppermute(v, "rep", pairs)
 
 
@@ -61,57 +60,31 @@
     return [((code >> (6 * k)) & 63) - 1 for k in range(SLOTS)]
 
 
-def pack(pos, lists, tokens, og4):
-    def kernel(pos_ref, ids_hbm, tok_hbm, og_hbm, *rest):
-        outs, (ids, tok, near, far, sems) = rest[:4], rest[4:]
-        x, y = pos_ref[0], pos_ref[1]
-        copies = [
-            pltpu.make_async_copy(ids_hbm, ids, sems.at[0]),
-            pltpu.make_async_copy(tok_hbm.at[:, pl.ds(0, HALF)], tok.at[0], sems.at[1]),
-            pltpu.make_async_copy(og_hbm.at[:, lax.rem(y + 1, N)], near.at[0], sems.at[2]),
-            pltpu.make_async_copy(og_hbm.at[:, lax.rem(y + 3, N)], near.at[1], sems.at[3]),
-            pltpu.make_async_copy(og_hbm.at[:, lax.rem(y + 2, N)], far.at[0], sems.at[4]),
-            pltpu.make_async_copy(tok_hbm.at[:, pl.ds(HALF, HALF)], tok.at[1], sems.at[5]),
-            pltpu.make_async_copy(og_hbm.at[lax.rem(x + 1, N)], near.at[2], sems.at[6]),
-            pltpu.make_async_copy(og_hbm.at[lax.rem(x + 3, N)], near.at[3], sems.at[7]),
-            pltpu.make_async_copy(og_hbm.at[lax.rem(x + 2, N)], far.at[1], sems.at[8]),
-        ]
-        for c in copies:
-            c.start()
-        copies[0].wait()
-        for out in outs:
-            put_ids(out, FIRST - IDS, lambda k: ids[0, k])
-        for part in range(2):
-            for c in copies[1 + 4 * part : 5 + 4 * part]:
-                c.wait()
-            for way in range(2):
-                out = outs[2 * part + way]
-                for j in range(HALF // TILE):
-                    out[ROWS * j : ROWS * (j + 1)] = tok[part, :, TILE * j : TILE * (j + 1)]
-                for i in range(N):
-                    row = T_ROWS + ROWS * i
-                    out[row : row + ROWS] = near[2 * part + way, i]
-                for i in range(2):
-                    row = T_ROWS + O_ROWS + ROWS * i
-                    out[row : row + ROWS] = far[part, 2 * way + i]
-
-    hbm = pl.BlockSpec(memory_space=pltpu.HBM)
+def pack(place, tokens, og4):
+    routes = [(0, 1), (0, 3), (1, 1), (1, 3)]
+
+    def kernel(place_ref, tok, og, *outs):
+        for out, (part, shift) in zip(outs, routes, strict=True):
+            here = place_ref[1 - part]
+            near, far = lax.rem(here + shift, N), lax.rem(here + 2, N)
+            lo = 0 if shift == 1 else 2
+            for j in range(HALF // TILE):
+                out[ROWS * j : ROWS * (j + 1)] = tok[:, HALF * part + TILE * j : HALF * part + TILE * (j + 1)]
+            for i in range(N + 2):
+                k, other = (i, near) if i < N else (lo + i - N, far)
+                row = T_ROWS + ROWS * i
+                out[row : row + ROWS] = og[k, other] if part == 0 else og[other, k]
+            put_ids(out, FIRST - IDS, lambda k: place_ref[2 + k])
+
     return pl.pallas_call(
         kernel,
         out_shape=[jax.ShapeDtypeStruct((FIRST, TILE), BF)] * 4,
-        in_specs=[pl.BlockSpec(memory_space=pltpu.SMEM), hbm, hbm, hbm],
+        in_specs=[pl.BlockSpec(memory_space=pltpu.SMEM), VMEM, VMEM],
         out_specs=[VMEM] * 4,
-        scratch_shapes=[
-            pltpu.SMEM((1, SLOTS), jnp.int32),
-            pltpu.VMEM((2, ROWS, HALF), BF),
-            pltpu.VMEM((4, N, ROWS, COLS), BF),
-            pltpu.VMEM((2, N, ROWS, COLS), BF),
-            pltpu.SemaphoreType.DMA((9,)),
-        ],
         cost_estimate=pl.CostEstimate(flops=0, bytes_accessed=16 * FIRST * TILE, transcendentals=0),
-        compiler_params=pltpu.CompilerParams(vmem_limit_bytes=PACK_CAP),
+        compiler_params=pltpu.CompilerParams(vmem_limit_bytes=SMALL_CAP),
         name="pack",
-    )(pos, lists, tokens, og4)
+    )(place, tokens, og4)
 
 
 def relay(message, shift):
@@ -480,13 +453,14 @@
 
 def per_device(tokens, out_grad, weights, moment_one, moment_two, error_buf, momentum, tile_lists):
     tp = lax.axis_index("tp")
-    pos = jnp.stack([tp // N, lax.rem(tp, N)]).astype(jnp.int32)
+    ids = tile_lists[0, 0]
+    place = jnp.concatenate([jnp.stack([tp // N, lax.rem(tp, N)]).astype(jnp.int32), ids])
+    pos = place[:2]
     tok = tokens[0]
     og4 = out_grad[0].reshape(N, N, ROWS, COLS)
-    ids = tile_lists[0, 0]
     state = (moment_one[0], moment_two[0], error_buf[0], weights)
 
-    m = pack(pos, tile_lists[0], tok, og4)
+    m = pack(place, tok, og4)
     yp, ym, xp, xm = along_y(m[0], 1), along_y(m[1], 3), along_x(m[2], 1), along_x(m[3], 3)
     y1, y2 = along_y(relay(yp, 1), 1), along_y(relay(ym, 3), 3)
     x1, x2 = along_x(relay(xp, 1), 1), along_x(relay(xm, 3), 3)
@@ -496,7 +470,8 @@
     pa = partials(pos, ra, x1, x2, y1, y2, 0, rb[1])
     sa = [pa[3], along_x(pa[5], 1), along_x(pa[4], 3), along_x(pa[6], 2)]
     pb = partials(pos, rb, y1, y2, x1, x2, 1, pa[3])
-    sb = [pb[3], along_y(pb[5], 1), along_y(pb[4], 3), along_y(pb[6], 2)]
+    (op_b,) = tied([pb[6]], sa[1:2])
+    sb = [pb[3], along_y(pb[5], 1), along_y(pb[4], 3), along_y(op_b, 2)]
     near_a, far_a = add_beyond(pa[1], pa[2], sa[1], sa[2])
     near_b, far_b = add_beyond(pb[1], pb[2], sb[1], sb[2])
     ga = [pa[0], along_x(far_a, 1), along_x(near_a, 3)]
@@ -504,11 +479,9 @@
 
     mine = sent_tiles(ids, sa + sb, *state)
     own = pair(mine, across(mine))
-    (z1,) = tied([onward(own)], ga[1:] + gb[1:])
-    z2 = onward(z1)
-    z3 = onward(z2)
+    z1, z2 = onward(own, 1), onward(own, 2)
+    z3, z4 = onward(z2, 1), onward(own_half(z2), 2)
     error_new, flag = keep_error(ids, ga, *state, 0)
-    z4 = onward(own_half(z3, flag))
     error_new, flag = keep_error(ids, gb, *state, 1, error_new)
     agg = add_tiles([mine, z1, z2, z3, z4], [flag])
     weights_new, momentum_new = outer(agg, across(agg), weights, momentum)

time: 115 us -> 104 us (0.904)
  starting transfers between devices: 51.7 us -> 42.3 us
  waiting for transfers between devices: 39.7 us -> 38 us
  Pallas kernels: 20.5 us -> 18.9 us
    ppermute x4, waiting for transfers between devices: 7.66 us -> 2.39 us  [onward(): return lax.ppermute(v, 'rep', pairs)]
    ppermute x2, starting transfers between devices: 10.2 us -> 5.17 us  [across(): lax.ppermute(v, 'rep', [(2 * a + c, 2 * a + 1 - c) for a in range(8) for...]
    ppermute x4, starting transfers between devices: 15.5 us -> 12.7 us  [onward(): return lax.ppermute(v, 'rep', pairs)]
    ppermute x9, waiting for transfers between devices: 21.4 us -> 23.7 us  [along_x(): lax.ppermute(v, 'tp', [(N * a + b, N * ((a + s) % N) + b) for a in range(...]
    pallas_call x1, Pallas kernels: 3.35 us -> 1.15 us  [pack(): pl.pallas_call(kernel, out_shape=[jax.ShapeDtypeStruct((FIRST, TILE), BF)...]
    ppermute x9, waiting for transfers between devices: 7.42 us -> 8.69 us  [along_y(): lax.ppermute(v, 'tp', [(N * a + b, N * a + (b + s) % N) for a in range(N)...]
    ppermute x9, starting transfers between devices: 15.7 us -> 14.5 us  [along_y(): lax.ppermute(v, 'tp', [(N * a + b, N * a + (b + s) % N) for a in range(N)...]
    unnamed x16 -> x20, local copies, waits for them, and re-layouts: 1.82 us -> 2.58 us
  transfers between devices with their start and end apart: 24 -> 24, of which waited for: 12 -> 12; matrix products, arithmetic and copies ran while one was open for 0% -> 0% of each run, Pallas kernels for 10% -> 12%
where the time goes in v3:
time: 104 us
  starting transfers between devices  42.3 us (41%)
  waiting for transfers between devices  38 us (37%)
  Pallas kernels  18.9 us (18%)
  local copies, waits for them, and re-layouts  2.58 us (2%)
  between operations  1.06 us (1%)
    ppermute x9, waiting for transfers between devices, along_x(): lax.ppermute(v, 'tp', [(N * a + b, N * ((a + s) % N) + b) for a in range(...  23.7 us
    ppermute x9, starting transfers between devices, along_y(): lax.ppermute(v, 'tp', [(N * a + b, N * a + (b + s) % N) for a in range(N)...  14.5 us
    ppermute x4, starting transfers between devices, onward(): return lax.ppermute(v, 'rep', pairs)  12.7 us
    ppermute x9, starting transfers between devices, along_x(): lax.ppermute(v, 'tp', [(N * a + b, N * ((a + s) % N) + b) for a in range(...  9.93 us
    ppermute x9, waiting for transfers between devices, along_y(): lax.ppermute(v, 'tp', [(N * a + b, N * a + (b + s) % N) for a in range(N)...  8.69 us
    pallas_call x2, Pallas kernels, keep_error(): pl.pallas_call(kernel, out_shape=[jax.ShapeDtypeStruct((COLS, FEATS), BF)...  5.48 us
    pallas_call x2, Pallas kernels, partials(): pl.pallas_call(kernel, out_shape=[shape(wide, F32), shape(wide, BF), shap...  5.43 us
    ppermute x2, starting transfers between devices, across(): lax.ppermute(v, 'rep', [(2 * a + c, 2 * a + 1 - c) for a in range(8) for...  5.17 us
  transfers between devices with their start and end apart: 24, of which 12 were waited for; matrix products, arithmetic and copies ran while one was open for 0% of the time, Pallas kernels for 12%

profile of v3, /device:TPU:1, one launch (start us, length us, event | category | flops | bytes accessed | tf_op | source)
XLA Modules:
  0.0 103.6 jit_solution(2422571315856199215)
XLA Ops:
  1.4 1.4 %copy-done.1 = bf16[1,192,4096]{2,1,0:T(8,128)(2,1)S(1)} copy-done((bf16[1,192,4096]{2,1,0:T(8,128)(2,1)S(1)}, bf16[1,192,4096]{2,1,0:T(8,128)(2,1)}, u32[]{:S(2)}) %copy-start.1) | copy-done | bytes 1572888
  3.9 1.2 %pack.1 = (bf16[4240,128]{1,0:T(8,128)(2,1)S(1)}, bf16[4240,128]{1,0:T(8,128)(2,1)S(1)}, bf16[4240,128]{1,0:T(8,128)(2,1)S(1)}, bf16[4240,128]{1,0:T(8,128)(2,1)S(1)}) custom-call(s32[6]{0:T(128)S(1)} %pad_add_fusion.1.place_ref, bf16[192,4096]{1,0:T(8,128)(2,1)S(1)} %bitcast.9, bf16[4,4,192,128]{3,2,1,0:T(8,128)(2,1)S(1)} %bitcast.21), custom_call_target="tpu_custom_call" | custom-call | bytes 8683520 | tf_op jit(solution)/shard_map/pack/pallas_call | solution.py:79
  5.1 2.1 %collective-permute-start = (bf16[4240,128]{1,0:T(8,128)(2,1)S(1)}, bf16[4240,128]{1,0:T(8,128)(2,1)S(1)}, u32[]{:S(2)}, u32[]{:S(2)}) collective-permute-start(bf16[4240,128]{1,0:T(8,128)(2,1)S(1)} %get-tuple-element.36), channel_id=1, source_target_pairs={{0,4},{1,5},{2,6},{3,7},{4,8},{5,9},{6,10},{7,11},{8,12},{9,13},{1... | collective-permute-start | bytes 3256328 | tf_op jit(solution)/shard_map/ppermute | solution.py:30
  7.2 1.4 %collective-permute-start.1 = (bf16[4240,128]{1,0:T(8,128)(2,1)S(1)}, bf16[4240,128]{1,0:T(8,128)(2,1)S(1)}, u32[]{:S(2)}, u32[]{:S(2)}) collective-permute-start(bf16[4240,128]{1,0:T(8,128)(2,1)S(1)} %get-tuple-element.37), channel_id=1, source_target_pairs={{0,12},{1,13},{2,14},{3,15},{4,0},{5,1},{6,2},{7,3},{8,4},{9,5},{1... | collective-permute-start | bytes 3256328 | tf_op jit(solution)/shard_map/ppermute | solution.py:30
  8.6 1.4 %collective-permute-start.2 = (bf16[4240,128]{1,0:T(8,128)(2,1)S(1)}, bf16[4240,128]{1,0:T(8,128)(2,1)S(1)}, u32[]{:S(2)}, u32[]{:S(2)}) collective-permute-start(bf16[4240,128]{1,0:T(8,128)(2,1)S(1)} %get-tuple-element.38), channel_id=1, source_target_pairs={{0,1},{1,2},{2,3},{3,0},{4,5},{5,6},{6,7},{7,4},{8,9},{9,10},{10,1... | collective-permute-start | bytes 3256328 | tf_op jit(solution)/shard_map/ppermute | solution.py:34
  10.0 1.4 %collective-permute-start.3 = (bf16[4240,128]{1,0:T(8,128)(2,1)S(1)}, bf16[4240,128]{1,0:T(8,128)(2,1)S(1)}, u32[]{:S(2)}, u32[]{:S(2)}) collective-permute-start(bf16[4240,128]{1,0:T(8,128)(2,1)S(1)} %get-tuple-element.39), channel_id=1, source_target_pairs={{0,3},{1,0},{2,1},{3,2},{4,7},{5,4},{6,5},{7,6},{8,11},{9,8},{10,9... | collective-permute-start | bytes 3256328 | tf_op jit(solution)/shard_map/ppermute | solution.py:34
  11.4 18.4 %collective-permute-done.n_o.ref.l = bf16[4240,128]{1,0:T(8,128)(2,1)S(1)} collective-permute-done((bf16[4240,128]{1,0:T(8,128)(2,1)S(1)}, bf16[4240,128]{1,0:T(8,128)(2,1)S(1)}, u32[]{:S(2)}, u32[]{:S(2)}) %collective-permute-start) | collective-permute-done | bytes 1085472 | tf_op jit(solution)/shard_map/ppermute | solution.py:30
  29.9 2.0 %collective-permute-start.4 = (bf16[1936,128]{1,0:T(8,128)(2,1)S(1)}, bf16[1936,128]{1,0:T(8,128)(2,1)S(1)}, u32[]{:S(2)}, u32[]{:S(2)}) collective-permute-start(bf16[1936,128]{1,0:T(8,128)(2,1)S(1)} %relay.4), channel_id=1, source_target_pairs={{0,4},{1,5},{2,6},{3,7},{4,8},{5,9},{6,10},{7,11},{8,12},{9,13},{1... | collective-permute-start | bytes 1486856 | tf_op jit(solution)/shard_map/ppermute | solution.py:30
  31.9 1.7 %collective-permute-start.5 = (bf16[1936,128]{1,0:T(8,128)(2,1)S(1)}, bf16[1936,128]{1,0:T(8,128)(2,1)S(1)}, u32[]{:S(2)}, u32[]{:S(2)}) collective-permute-start(bf16[1936,128]{1,0:T(8,128)(2,1)S(1)} %relay.5), channel_id=1, source_target_pairs={{0,12},{1,13},{2,14},{3,15},{4,0},{5,1},{6,2},{7,3},{8,4},{9,5},{1... | collective-permute-start | bytes 1486856 | tf_op jit(solution)/shard_map/ppermute | solution.py:30
  33.6 2.8 %collective-permute-start.6 = (bf16[1936,128]{1,0:T(8,128)(2,1)S(1)}, bf16[1936,128]{1,0:T(8,128)(2,1)S(1)}, u32[]{:S(2)}, u32[]{:S(2)}) collective-permute-start(bf16[1936,128]{1,0:T(8,128)(2,1)S(1)} %relay.6), channel_id=1, source_target_pairs={{0,1},{1,2},{2,3},{3,0},{4,5},{5,6},{6,7},{7,4},{8,9},{9,10},{10,1... | collective-permute-start | bytes 1486856 | tf_op jit(solution)/shard_map/ppermute | solution.py:34
  36.4 1.5 %collective-permute-start.7 = (bf16[1936,128]{1,0:T(8,128)(2,1)S(1)}, bf16[1936,128]{1,0:T(8,128)(2,1)S(1)}, u32[]{:S(2)}, u32[]{:S(2)}) collective-permute-start(bf16[1936,128]{1,0:T(8,128)(2,1)S(1)} %relay.7), channel_id=1, source_target_pairs={{0,3},{1,0},{2,1},{3,2},{4,7},{5,4},{6,5},{7,6},{8,11},{9,8},{10,9... | collective-permute-start | bytes 1486856 | tf_op jit(solution)/shard_map/ppermute | solution.py:34
  38.0 1.3 %gather.3 = (bf16[768,2048]{1,0:T(8,128)(2,1)S(1)}, bf16[512,768]{1,0:T(8,128)(2,1)S(1)}, s32[16]{0:T(128)S(1)}) custom-call(s32[2]{0:T(128)S(1)} %pad_add_fusion.pos_ref, s32[4]{0:T(128)S(1)} %bitcast.25, bf16[4,4,192,128]{3,2,1,0:T(8,128)(2,1)S(1)} %bitcast.22, bf16[4240,128]{1,0:T(8,128)(2,1)S(1)} %collective-permute-done.2.l.ref.n_o, ...), custom_call_target="tpu_custom_call" | custom-call | bytes 8388608 | tf_op jit(solution)/shard_map/gather/pallas_call | solution.py:136
  39.3 1.3 %gather.2 = (bf16[768,2048]{1,0:T(8,128)(2,1)S(1)}, bf16[512,768]{1,0:T(8,128)(2,1)S(1)}, s32[16]{0:T(128)S(1)}) custom-call(s32[2]{0:T(128)S(1)} %pad_add_fusion.pos_ref, s32[4]{0:T(128)S(1)} %bitcast.26, bf16[4,4,192,128]{3,2,1,0:T(8,128)(2,1)S(1)} %bitcast.23, bf16[4240,128]{1,0:T(8,128)(2,1)S(1)} %collective-permute-done.n_o.ref.l, ...), custom_call_target="tpu_custom_call" | custom-call | bytes 8388608 | tf_op jit(solution)/shard_map/gather/pallas_call | solution.py:136
  40.6 1.3 %collective-permute-done.4.lo.a = bf16[1936,128]{1,0:T(8,128)(2,1)S(1)} collective-permute-done((bf16[1936,128]{1,0:T(8,128)(2,1)S(1)}, bf16[1936,128]{1,0:T(8,128)(2,1)S(1)}, u32[]{:S(2)}, u32[]{:S(2)}) %collective-permute-start.4) | collective-permute-done | bytes 495648 | tf_op jit(solution)/shard_map/ppermute | solution.py:30
  42.7 4.6 %collective-permute-done.6.a.lo = bf16[1936,128]{1,0:T(8,128)(2,1)S(1)} collective-permute-done((bf16[1936,128]{1,0:T(8,128)(2,1)S(1)}, bf16[1936,128]{1,0:T(8,128)(2,1)S(1)}, u32[]{:S(2)}, u32[]{:S(2)}) %collective-permute-start.6) | collective-permute-done | bytes 495648 | tf_op jit(solution)/shard_map/ppermute | solution.py:34
  47.3 2.7 %partials.2 = (f32[128,2048]{1,0:T(8,128)S(1)}, bf16[128,2048]{1,0:T(8,128)(2,1)S(1)}, bf16[128,2048]{1,0:T(8,128)(2,1)S(1)}, f32[512,128]{1,0:T(8,128)S(1)}, bf...) custom-call(s32[2]{0:T(128)S(1)} %pad_add_fusion.pos_ref, ...), custom_call_target="tpu_custom_call", output_to_operand_aliasing={{7}: (6, {}), {8}: (7, {})} | custom-call | flops 1610612736 | bytes 8388608 | tf_op jit(solution)/shard_map/partials/pallas_call | solution.py:197
  50.1 2.7 %collective-permute-start.9 = (bf16[1536,128]{1,0:T(8,128)(2,1)S(1)}, bf16[1536,128]{1,0:T(8,128)(2,1)S(1)}, u32[]{:S(2)}, u32[]{:S(2)}) collective-permute-start(bf16[1536,128]{1,0:T(8,128)(2,1)S(1)} %get-tuple-element.46), channel_id=1, source_target_pairs={{0,12},{1,13},{2,14},{3,15},{4,0},{5,1},{6,2},{7,3},{8,4},{9,5},{1... | collective-permute-start | bytes 1179656 | tf_op jit(solution)/shard_map/ppermute | solution.py:30
  52.8 2.7 %partials.3 = (f32[128,2048]{1,0:T(8,128)S(1)}, bf16[128,2048]{1,0:T(8,128)(2,1)S(1)}, bf16[128,2048]{1,0:T(8,128)(2,1)S(1)}, f32[512,128]{1,0:T(8,128)S(1)}, bf...) custom-call(s32[2]{0:T(128)S(1)} %pad_add_fusion.pos_ref, ...), custom_call_target="tpu_custom_call", output_to_operand_aliasing={{7}: (6, {}), {8}: (7, {})} | custom-call | flops 1610612736 | bytes 8388608 | tf_op jit(solution)/shard_map/partials/pallas_call | solution.py:197
  56.5 1.7 %collective-permute-start.12 = (bf16[1536,128]{1,0:T(8,128)(2,1)S(1)}, bf16[1536,128]{1,0:T(8,128)(2,1)S(1)}, u32[]{:S(2)}, u32[]{:S(2)}) collective-permute-start(bf16[1536,128]{1,0:T(8,128)(2,1)S(1)} %get-tuple-element.52), channel_id=1, source_target_pairs={{0,3},{1,0},{2,1},{3,2},{4,7},{5,4},{6,5},{7,6},{8,11},{9,8},{10,9... | collective-permute-start | bytes 1179656 | tf_op jit(solution)/shard_map/ppermute | solution.py:34
  59.0 1.8 %collective-permute-start.13 = (bf16[512,128]{1,0:T(8,128)(2,1)S(1)}, bf16[512,128]{1,0:T(8,128)(2,1)S(1)}, u32[]{:S(2)}, u32[]{:S(2)}) collective-permute-start(bf16[512,128]{1,0:T(8,128)(2,1)S(1)} %tied.1), channel_id=1, source_target_pairs={{0,2},{1,3},{2,0},{3,1},{4,6},{5,7},{6,4},{7,5},{8,10},{9,11},{10,... | collective-permute-start | bytes 393224 | tf_op jit(solution)/shard_map/ppermute | solution.py:34
  61.2 2.4 %collective-permute-done.10.refs_3_ = bf16[512,128]{1,0:T(8,128)(2,1)S(1)} collective-permute-done((bf16[512,128]{1,0:T(8,128)(2,1)S(1)}, bf16[512,128]{1,0:T(8,128)(2,1)S(1)}, u32[]{:S(2)}, u32[]{:S(2)}) %collective-permute-start.10) | collective-permute-done | bytes 131104 | tf_op jit(solution)/shard_map/ppermute | solution.py:30
  64.3 3.4 %collective-permute-done.13.refs_7_ = bf16[512,128]{1,0:T(8,128)(2,1)S(1)} collective-permute-done((bf16[512,128]{1,0:T(8,128)(2,1)S(1)}, bf16[512,128]{1,0:T(8,128)(2,1)S(1)}, u32[]{:S(2)}, u32[]{:S(2)}) %collective-permute-start.13) | collective-permute-done | bytes 131104 | tf_op jit(solution)/shard_map/ppermute | solution.py:34
  68.6 4.6 %collective-permute-start.14 = (bf16[528,128]{1,0:T(8,128)(2,1)S(1)}, bf16[528,128]{1,0:T(8,128)(2,1)S(1)}, u32[]{:S(2)}, u32[]{:S(2)}) collective-permute-start(bf16[528,128]{1,0:T(8,128)(2,1)S(1)} %sent_tiles.1.a.refs_0_), channel_id=1, source_target_pairs={{0,16},{16,0},{32,48},{48,32},{64,80},{80,64},{96,112},{112,96},{1... | collective-permute-start | bytes 405512 | tf_op jit(solution)/shard_map/ppermute | solution.py:43
  74.2 5.7 %collective-permute-start.16 = (bf16[1056,128]{1,0:T(8,128)(2,1)S(1)}, bf16[1056,128]{1,0:T(8,128)(2,1)S(1)}, u32[]{:S(2)}, u32[]{:S(2)}) collective-permute-start(bf16[1056,128]{1,0:T(8,128)(2,1)S(1)} %pair.1), channel_id=1, source_target_pairs={{0,64},{32,96},{64,128},{96,160},{128,192},{160,224},{192,0},{224,... | collective-permute-start | bytes 811016 | tf_op jit(solution)/shard_map/ppermute | solution.py:39
  81.3 1.7 %collective-permute-start.20 = (bf16[128,2048]{1,0:T(8,128)(2,1)S(1)}, bf16[128,2048]{1,0:T(8,128)(2,1)S(1)}, u32[]{:S(2)}, u32[]{:S(2)}) collective-permute-start(bf16[128,2048]{1,0:T(8,128)(2,1)S(1)} %get-tuple-element.58), channel_id=1, source_target_pairs={{0,3},{1,0},{2,1},{3,2},{4,7},{5,4},{6,5},{7,6},{8,11},{9,8},{10,9... | collective-permute-start | bytes 1572872 | tf_op jit(solution)/shard_map/ppermute | solution.py:34
  83.9 2.4 %collective-permute-done.16.ref.refs_2_ = bf16[1056,128]{1,0:T(8,128)(2,1)S(1)} collective-permute-done((bf16[1056,128]{1,0:T(8,128)(2,1)S(1)}, bf16[1056,128]{1,0:T(8,128)(2,1)S(1)}, u32[]{:S(2)}, u32[]{:S(2)}) %collective-permute-start.16) | collective-permute-done | bytes 270368 | tf_op jit(solution)/shard_map/ppermute | solution.py:39
  86.3 2.2 %collective-permute-start.17 = (bf16[1056,128]{1,0:T(8,128)(2,1)S(1)}, bf16[1056,128]{1,0:T(8,128)(2,1)S(1)}, u32[]{:S(2)}, u32[]{:S(2)}) collective-permute-start(bf16[1056,128]{1,0:T(8,128)(2,1)S(1)} %collective-permute-done.16.ref.refs_2_), channel_id=1, source_target_pairs={{0,32},{32,64},{64,96},{96,128},{128,160},{160,192},{192,224},{224... | collective-permute-start | bytes 811016 | tf_op jit(solution)/shard_map/ppermute | solution.py:39
  88.5 3.8 %collective-permute-start.18 = (bf16[528,128]{1,0:T(8,128)(2,1)S(1)}, bf16[528,128]{1,0:T(8,128)(2,1)S(1)}, u32[]{:S(2)}, u32[]{:S(2)}) collective-permute-start(bf16[528,128]{1,0:T(8,128)(2,1)S(1)} %own_half.1), channel_id=1, source_target_pairs={{0,64},{32,96},{64,128},{96,160},{128,192},{160,224},{192,0},{224,... | collective-permute-start | bytes 405512 | tf_op jit(solution)/shard_map/ppermute | solution.py:39
  92.4 3.1 %keep_error.2 = (bf16[128,4096]{1,0:T(8,128)(2,1)}, f32[8,128]{1,0:T(8,128)}) custom-call(s32[4]{0:T(128)S(1)} %bitcast.28, f32[128,2048]{1,0:T(8,128)S(1)} %get-tuple-element.59.g0, bf16[128,2048]{1,0:T(8,128)(2,1)S(1)} %collective-permute-done.21.g1, bf16[128,2048]{1,0:T(8,128)(2,1)S(1)} %collective-permute-done.22.g2, bf16[128,4096]{1,0:T(8,128)(2,1)S(1)} %bitcast.13, ...), custom_call_target="tpu_custom_call" | custom-call | flops 5242880 | bytes 5242880 | tf_op jit(solution)/shard_map/keep_error/pallas_call | solution.py:374
  95.5 2.3 %keep_error.3 = (bf16[128,4096]{1,0:T(8,128)(2,1)}, f32[8,128]{1,0:T(8,128)S(1)}) custom-call(s32[4]{0:T(128)S(1)} %bitcast.29, f32[128,2048]{1,0:T(8,128)S(1)} %get-tuple-element.54.g0, bf16[128,2048]{1,0:T(8,128)(2,1)S(1)} %collective-permute-done.19.g1, bf16[128,2048]{1,0:T(8,128)(2,1)S(1)} %collective-permute-done.20.g2, ...), custom_call_target="tpu_custom_call", output_to_operand_aliasing={{0}: (8, {})} | custom-call | flops 5242880 | bytes 5242880 | tf_op jit(solution)/shard_map/keep_error/pallas_call | solution.py:374
  99.3 2.3 %collective-permute-done.23.o_ref = bf16[128,4096]{1,0:T(8,128)(2,1)S(1)} collective-permute-done((bf16[128,4096]{1,0:T(8,128)(2,1)S(1)}, bf16[128,4096]{1,0:T(8,128)(2,1)S(1)}, u32[]{:S(2)}, u32[]{:S(2)}) %collective-permute-start.23) | collective-permute-done | bytes 1048608 | tf_op jit(solution)/shard_map/ppermute | solution.py:43
  101.6 1.9 %outer.1 = (f32[128,4096]{1,0:T(8,128)}, bf16[128,4096]{1,0:T(8,128)(2,1)}) custom-call(bf16[128,4096]{1,0:T(8,128)(2,1)S(1)} %add_tiles.1.m_ref, bf16[128,4096]{1,0:T(8,128)(2,1)S(1)} %collective-permute-done.23.o_ref, f32[128,4096]{1,0:T(8,128)S(1)} %copy-done, bf16[128,4096]{1,0:T(8,128)(2,1)S(1)} %copy-done.8), custom_call_target="tpu_custom_call" | custom-call | flops 3145728 | bytes 8388608 | tf_op jit(solution)/shard_map/outer/pallas_call | solution.py:442
  (57 shorter events, 11.3 us)
Async XLA Ops:
  5.1 24.8 %collective-permute-start = (bf16[4240,128]{1,0:T(8,128)(2,1)S(1)}, bf16[4240,128]{1,0:T(8,128)(2,1)S(1)}, u32[]{:S(2)}, u32[]{:S(2)}) collective-permute-start(bf16[4240,128]{1,0:T(8,128)(2,1)S(1)} %get-tuple-element.36), channel_id=1, source_target_pairs={{0,4},{1,5},{2,6},{3,7},{4,8},{5,9},{6,10},{7,11},{8,12},{9,13},{1... | collective-permute-start | bytes 3256328 | tf_op jit(solution)/shard_map/ppermute | solution.py:30
  7.2 24.6 %collective-permute-start.1 = (bf16[4240,128]{1,0:T(8,128)(2,1)S(1)}, bf16[4240,128]{1,0:T(8,128)(2,1)S(1)}, u32[]{:S(2)}, u32[]{:S(2)}) collective-permute-start(bf16[4240,128]{1,0:T(8,128)(2,1)S(1)} %get-tuple-element.37), channel_id=1, source_target_pairs={{0,12},{1,13},{2,14},{3,15},{4,0},{5,1},{6,2},{7,3},{8,4},{9,5},{1... | collective-permute-start | bytes 3256328 | tf_op jit(solution)/shard_map/ppermute | solution.py:30
  8.6 25.0 %collective-permute-start.2 = (bf16[4240,128]{1,0:T(8,128)(2,1)S(1)}, bf16[4240,128]{1,0:T(8,128)(2,1)S(1)}, u32[]{:S(2)}, u32[]{:S(2)}) collective-permute-start(bf16[4240,128]{1,0:T(8,128)(2,1)S(1)} %get-tuple-element.38), channel_id=1, source_target_pairs={{0,1},{1,2},{2,3},{3,0},{4,5},{5,6},{6,7},{7,4},{8,9},{9,10},{10,1... | collective-permute-start | bytes 3256328 | tf_op jit(solution)/shard_map/ppermute | solution.py:34
  10.0 26.4 %collective-permute-start.3 = (bf16[4240,128]{1,0:T(8,128)(2,1)S(1)}, bf16[4240,128]{1,0:T(8,128)(2,1)S(1)}, u32[]{:S(2)}, u32[]{:S(2)}) collective-permute-start(bf16[4240,128]{1,0:T(8,128)(2,1)S(1)} %get-tuple-element.39), channel_id=1, source_target_pairs={{0,3},{1,0},{2,1},{3,2},{4,7},{5,4},{6,5},{7,6},{8,11},{9,8},{10,9... | collective-permute-start | bytes 3256328 | tf_op jit(solution)/shard_map/ppermute | solution.py:34
  29.9 12.1 %collective-permute-start.4 = (bf16[1936,128]{1,0:T(8,128)(2,1)S(1)}, bf16[1936,128]{1,0:T(8,128)(2,1)S(1)}, u32[]{:S(2)}, u32[]{:S(2)}) collective-permute-start(bf16[1936,128]{1,0:T(8,128)(2,1)S(1)} %relay.4), channel_id=1, source_target_pairs={{0,4},{1,5},{2,6},{3,7},{4,8},{5,9},{6,10},{7,11},{8,12},{9,13},{1... | collective-permute-start | bytes 1486856 | tf_op jit(solution)/shard_map/ppermute | solution.py:30
  31.9 10.8 %collective-permute-start.5 = (bf16[1936,128]{1,0:T(8,128)(2,1)S(1)}, bf16[1936,128]{1,0:T(8,128)(2,1)S(1)}, u32[]{:S(2)}, u32[]{:S(2)}) collective-permute-start(bf16[1936,128]{1,0:T(8,128)(2,1)S(1)} %relay.5), channel_id=1, source_target_pairs={{0,12},{1,13},{2,14},{3,15},{4,0},{5,1},{6,2},{7,3},{8,4},{9,5},{1... | collective-permute-start | bytes 1486856 | tf_op jit(solution)/shard_map/ppermute | solution.py:30
  33.5 4.5 %copy-start.7 = (bf16[1,3072,128]{2,1,0:T(8,128)(2,1)S(1)}, bf16[1,3072,128]{2,1,0:T(8,128)(2,1)}, u32[]{:S(2)}) copy-start(bf16[1,3072,128]{2,1,0:T(8,128)(2,1)} %param.9) | copy-start | bytes 2359300
  33.6 4.4 %copy-start.2 = (bf16[1,192,4096]{2,1,0:T(8,128)(2,1)S(1)}, bf16[1,192,4096]{2,1,0:T(8,128)(2,1)}, u32[]{:S(2)}) copy-start(bf16[1,192,4096]{2,1,0:T(8,128)(2,1)} %param.8) | copy-start | bytes 4718596
  33.6 4.4 %copy-start.9 = (s32[1,1,4]{2,1,0:T(1,128)S(1)}, s32[1,1,4]{2,1,0:T(1,128)}, u32[]{:S(2)}) copy-start(s32[1,1,4]{2,1,0:T(1,128)} %param.15) | copy-start | bytes 52
  33.6 13.7 %collective-permute-start.6 = (bf16[1936,128]{1,0:T(8,128)(2,1)S(1)}, bf16[1936,128]{1,0:T(8,128)(2,1)S(1)}, u32[]{:S(2)}, u32[]{:S(2)}) collective-permute-start(bf16[1936,128]{1,0:T(8,128)(2,1)S(1)} %relay.6), channel_id=1, source_target_pairs={{0,1},{1,2},{2,3},{3,0},{4,5},{5,6},{6,7},{7,4},{8,9},{9,10},{10,1... | collective-permute-start | bytes 1486856 | tf_op jit(solution)/shard_map/ppermute | solution.py:34
  36.4 10.9 %collective-permute-start.7 = (bf16[1936,128]{1,0:T(8,128)(2,1)S(1)}, bf16[1936,128]{1,0:T(8,128)(2,1)S(1)}, u32[]{:S(2)}, u32[]{:S(2)}) collective-permute-start(bf16[1936,128]{1,0:T(8,128)(2,1)S(1)} %relay.7), channel_id=1, source_target_pairs={{0,3},{1,0},{2,1},{3,2},{4,7},{5,4},{6,5},{7,6},{8,11},{9,8},{10,9... | collective-permute-start | bytes 1486856 | tf_op jit(solution)/shard_map/ppermute | solution.py:34
  50.0 9.0 %collective-permute-start.8 = (bf16[1536,128]{1,0:T(8,128)(2,1)S(1)}, bf16[1536,128]{1,0:T(8,128)(2,1)S(1)}, u32[]{:S(2)}, u32[]{:S(2)}) collective-permute-start(bf16[1536,128]{1,0:T(8,128)(2,1)S(1)} %get-tuple-element.45), channel_id=1, source_target_pairs={{0,4},{1,5},{2,6},{3,7},{4,8},{5,9},{6,10},{7,11},{8,12},{9,13},{1... | collective-permute-start | bytes 1179656 | tf_op jit(solution)/shard_map/ppermute | solution.py:30
  50.1 10.7 %collective-permute-start.9 = (bf16[1536,128]{1,0:T(8,128)(2,1)S(1)}, bf16[1536,128]{1,0:T(8,128)(2,1)S(1)}, u32[]{:S(2)}, u32[]{:S(2)}) collective-permute-start(bf16[1536,128]{1,0:T(8,128)(2,1)S(1)} %get-tuple-element.46), channel_id=1, source_target_pairs={{0,12},{1,13},{2,14},{3,15},{4,0},{5,1},{6,2},{7,3},{8,4},{9,5},{1... | collective-permute-start | bytes 1179656 | tf_op jit(solution)/shard_map/ppermute | solution.py:30
  52.8 14.9 %copy-start.3 = (bf16[1,128,4096]{2,1,0:T(8,128)(2,1)S(1)}, bf16[1,128,4096]{2,1,0:T(8,128)(2,1)}, u32[]{:S(2)}) copy-start(bf16[1,128,4096]{2,1,0:T(8,128)(2,1)} %param.11) | copy-start | bytes 3145732
  52.8 14.9 %copy-start.4 = (bf16[1,128,4096]{2,1,0:T(8,128)(2,1)S(1)}, bf16[1,128,4096]{2,1,0:T(8,128)(2,1)}, u32[]{:S(2)}) copy-start(bf16[1,128,4096]{2,1,0:T(8,128)(2,1)} %param.12) | copy-start | bytes 3145732
  52.8 14.9 %copy-start.5 = (bf16[1,128,4096]{2,1,0:T(8,128)(2,1)S(1)}, bf16[1,128,4096]{2,1,0:T(8,128)(2,1)}, u32[]{:S(2)}) copy-start(bf16[1,128,4096]{2,1,0:T(8,128)(2,1)} %param.13) | copy-start | bytes 3145732
  55.5 8.4 %collective-permute-start.11 = (bf16[1536,128]{1,0:T(8,128)(2,1)S(1)}, bf16[1536,128]{1,0:T(8,128)(2,1)S(1)}, u32[]{:S(2)}, u32[]{:S(2)}) collective-permute-start(bf16[1536,128]{1,0:T(8,128)(2,1)S(1)} %get-tuple-element.51), channel_id=1, source_target_pairs={{0,1},{1,2},{2,3},{3,0},{4,5},{5,6},{6,7},{7,4},{8,9},{9,10},{10,1... | collective-permute-start | bytes 1179656 | tf_op jit(solution)/shard_map/ppermute | solution.py:34
  56.5 7.8 %collective-permute-start.12 = (bf16[1536,128]{1,0:T(8,128)(2,1)S(1)}, bf16[1536,128]{1,0:T(8,128)(2,1)S(1)}, u32[]{:S(2)}, u32[]{:S(2)}) collective-permute-start(bf16[1536,128]{1,0:T(8,128)(2,1)S(1)} %get-tuple-element.52), channel_id=1, source_target_pairs={{0,3},{1,0},{2,1},{3,2},{4,7},{5,4},{6,5},{7,6},{8,11},{9,8},{10,9... | collective-permute-start | bytes 1179656 | tf_op jit(solution)/shard_map/ppermute | solution.py:34
  58.3 5.3 %collective-permute-start.10 = (bf16[512,128]{1,0:T(8,128)(2,1)S(1)}, bf16[512,128]{1,0:T(8,128)(2,1)S(1)}, u32[]{:S(2)}, u32[]{:S(2)}) collective-permute-start(bf16[512,128]{1,0:T(8,128)(2,1)S(1)} %get-tuple-element.47), channel_id=1, source_target_pairs={{0,8},{1,9},{2,10},{3,11},{4,12},{5,13},{6,14},{7,15},{8,0},{9,1},... | collective-permute-start | bytes 393224 | tf_op jit(solution)/shard_map/ppermute | solution.py:30
  59.0 8.7 %copy-start = (f32[128,4096]{1,0:T(8,128)S(1)}, f32[128,4096]{1,0:T(8,128)}, u32[]{:S(2)}) copy-start(f32[128,4096]{1,0:T(8,128)} %w_ref.5) | copy-start | bytes 6291460
  59.0 8.7 %collective-permute-start.13 = (bf16[512,128]{1,0:T(8,128)(2,1)S(1)}, bf16[512,128]{1,0:T(8,128)(2,1)S(1)}, u32[]{:S(2)}, u32[]{:S(2)}) collective-permute-start(bf16[512,128]{1,0:T(8,128)(2,1)S(1)} %tied.1), channel_id=1, source_target_pairs={{0,2},{1,3},{2,0},{3,1},{4,6},{5,7},{6,4},{7,5},{8,10},{9,11},{10,... | collective-permute-start | bytes 393224 | tf_op jit(solution)/shard_map/ppermute | solution.py:34
  61.1 21.9 %collective-permute-start.21 = (bf16[128,2048]{1,0:T(8,128)(2,1)S(1)}, bf16[128,2048]{1,0:T(8,128)(2,1)S(1)}, u32[]{:S(2)}, u32[]{:S(2)}) collective-permute-start(bf16[128,2048]{1,0:T(8,128)(2,1)S(1)} %get-tuple-element.62), channel_id=1, source_target_pairs={{0,4},{1,5},{2,6},{3,7},{4,8},{5,9},{6,10},{7,11},{8,12},{9,13},{1... | collective-permute-start | bytes 1572872 | tf_op jit(solution)/shard_map/ppermute | solution.py:30
  68.6 5.6 %collective-permute-start.14 = (bf16[528,128]{1,0:T(8,128)(2,1)S(1)}, bf16[528,128]{1,0:T(8,128)(2,1)S(1)}, u32[]{:S(2)}, u32[]{:S(2)}) collective-permute-start(bf16[528,128]{1,0:T(8,128)(2,1)S(1)} %sent_tiles.1.a.refs_0_), channel_id=1, source_target_pairs={{0,16},{16,0},{32,48},{48,32},{64,80},{80,64},{96,112},{112,96},{1... | collective-permute-start | bytes 405512 | tf_op jit(solution)/shard_map/ppermute | solution.py:43
  73.2 15.3 %collective-permute-start.22 = (bf16[128,2048]{1,0:T(8,128)(2,1)S(1)}, bf16[128,2048]{1,0:T(8,128)(2,1)S(1)}, u32[]{:S(2)}, u32[]{:S(2)}) collective-permute-start(bf16[128,2048]{1,0:T(8,128)(2,1)S(1)} %get-tuple-element.63), channel_id=1, source_target_pairs={{0,12},{1,13},{2,14},{3,15},{4,0},{5,1},{6,2},{7,3},{8,4},{9,5},{1... | collective-permute-start | bytes 1572872 | tf_op jit(solution)/shard_map/ppermute | solution.py:30
  74.2 12.0 %collective-permute-start.16 = (bf16[1056,128]{1,0:T(8,128)(2,1)S(1)}, bf16[1056,128]{1,0:T(8,128)(2,1)S(1)}, u32[]{:S(2)}, u32[]{:S(2)}) collective-permute-start(bf16[1056,128]{1,0:T(8,128)(2,1)S(1)} %pair.1), channel_id=1, source_target_pairs={{0,64},{32,96},{64,128},{96,160},{128,192},{160,224},{192,0},{224,... | collective-permute-start | bytes 811016 | tf_op jit(solution)/shard_map/ppermute | solution.py:39
  80.2 15.3 %collective-permute-start.19 = (bf16[128,2048]{1,0:T(8,128)(2,1)S(1)}, bf16[128,2048]{1,0:T(8,128)(2,1)S(1)}, u32[]{:S(2)}, u32[]{:S(2)}) collective-permute-start(bf16[128,2048]{1,0:T(8,128)(2,1)S(1)} %get-tuple-element.57), channel_id=1, source_target_pairs={{0,1},{1,2},{2,3},{3,0},{4,5},{5,6},{6,7},{7,4},{8,9},{9,10},{10,1... | collective-permute-start | bytes 1572872 | tf_op jit(solution)/shard_map/ppermute | solution.py:34
  81.3 14.2 %collective-permute-start.20 = (bf16[128,2048]{1,0:T(8,128)(2,1)S(1)}, bf16[128,2048]{1,0:T(8,128)(2,1)S(1)}, u32[]{:S(2)}, u32[]{:S(2)}) collective-permute-start(bf16[128,2048]{1,0:T(8,128)(2,1)S(1)} %get-tuple-element.58), channel_id=1, source_target_pairs={{0,3},{1,0},{2,1},{3,2},{4,7},{5,4},{6,5},{7,6},{8,11},{9,8},{10,9... | collective-permute-start | bytes 1572872 | tf_op jit(solution)/shard_map/ppermute | solution.py:34
  83.0 14.9 %collective-permute-start.15 = (bf16[1056,128]{1,0:T(8,128)(2,1)S(1)}, bf16[1056,128]{1,0:T(8,128)(2,1)S(1)}, u32[]{:S(2)}, u32[]{:S(2)}) collective-permute-start(bf16[1056,128]{1,0:T(8,128)(2,1)S(1)} %pair.1), channel_id=1, source_target_pairs={{0,32},{32,64},{64,96},{96,128},{128,160},{160,192},{192,224},{224... | collective-permute-start | bytes 811016 | tf_op jit(solution)/shard_map/ppermute | solution.py:39
  86.3 11.6 %collective-permute-start.17 = (bf16[1056,128]{1,0:T(8,128)(2,1)S(1)}, bf16[1056,128]{1,0:T(8,128)(2,1)S(1)}, u32[]{:S(2)}, u32[]{:S(2)}) collective-permute-start(bf16[1056,128]{1,0:T(8,128)(2,1)S(1)} %collective-permute-done.16.ref.refs_2_), channel_id=1, source_target_pairs={{0,32},{32,64},{64,96},{96,128},{128,160},{160,192},{192,224},{224... | collective-permute-start | bytes 811016 | tf_op jit(solution)/shard_map/ppermute | solution.py:39
  88.5 9.4 %collective-permute-start.18 = (bf16[528,128]{1,0:T(8,128)(2,1)S(1)}, bf16[528,128]{1,0:T(8,128)(2,1)S(1)}, u32[]{:S(2)}, u32[]{:S(2)}) collective-permute-start(bf16[528,128]{1,0:T(8,128)(2,1)S(1)} %own_half.1), channel_id=1, source_target_pairs={{0,64},{32,96},{64,128},{96,160},{128,192},{160,224},{192,0},{224,... | collective-permute-start | bytes 405512 | tf_op jit(solution)/shard_map/ppermute | solution.py:39
  97.9 3.7 %copy-start.8 = (bf16[128,4096]{1,0:T(8,128)(2,1)S(1)}, bf16[128,4096]{1,0:T(8,128)(2,1)}, u32[]{:S(2)}) copy-start(bf16[128,4096]{1,0:T(8,128)(2,1)} %v_ref.1) | copy-start | bytes 3145732
  98.7 2.9 %collective-permute-start.23 = (bf16[128,4096]{1,0:T(8,128)(2,1)S(1)}, bf16[128,4096]{1,0:T(8,128)(2,1)S(1)}, u32[]{:S(2)}, u32[]{:S(2)}) collective-permute-start(bf16[128,4096]{1,0:T(8,128)(2,1)S(1)} %add_tiles.1.m_ref), channel_id=1, source_target_pairs={{0,16},{16,0},{32,48},{48,32},{64,80},{80,64},{96,112},{112,96},{1... | collective-permute-start | bytes 3145736 | tf_op jit(solution)/shard_map/ppermute | solution.py:43
  (2 other events, 2.5 us)

commit v4 on v3

--- a/solution.py
+++ b/solution.py
@@ -23,6 +23,7 @@
 BF = jnp.bfloat16
 F32 = jnp.float32
 SMALL_CAP = 8 * 1024 * 1024
+PACK_CAP = 48 * 1024 * 1024
 VMEM = pl.BlockSpec(memory_space=pltpu.VMEM)
 
 
@@ -63,26 +64,38 @@
 def pack(place, tokens, og4):
     routes = [(0, 1), (0, 3), (1, 1), (1, 3)]
 
-    def kernel(place_ref, tok, og, *outs):
+    def kernel(place_ref, tok_hbm, og, *rest):
+        outs, (tok, sems) = rest[:4], rest[4:]
+        copies = []
+        for c in range(4):
+            lanes = pl.ds(HALF // 2 * c, HALF // 2)
+            copies.append(pltpu.make_async_copy(tok_hbm.at[:, lanes], tok.at[:, lanes], sems.at[c]))
+            copies[-1].start()
         for out, (part, shift) in zip(outs, routes, strict=True):
             here = place_ref[1 - part]
             near, far = lax.rem(here + shift, N), lax.rem(here + 2, N)
             lo = 0 if shift == 1 else 2
-            for j in range(HALF // TILE):
-                out[ROWS * j : ROWS * (j + 1)] = tok[:, HALF * part + TILE * j : HALF * part + TILE * (j + 1)]
             for i in range(N + 2):
                 k, other = (i, near) if i < N else (lo + i - N, far)
                 row = T_ROWS + ROWS * i
                 out[row : row + ROWS] = og[k, other] if part == 0 else og[other, k]
             put_ids(out, FIRST - IDS, lambda k: place_ref[2 + k])
+        tiles = HALF // TILE
+        for c in range(4):
+            copies[c].wait()
+            for out in outs[2 * (c // 2) : 2 * (c // 2) + 2]:
+                for j in range(tiles // 2 * (c % 2), tiles // 2 * (c % 2 + 1)):
+                    at = HALF * (c // 2) + TILE * j
+                    out[ROWS * j : ROWS * (j + 1)] = tok[:, at : at + TILE]
 
     return pl.pallas_call(
         kernel,
         out_shape=[jax.ShapeDtypeStruct((FIRST, TILE), BF)] * 4,
-        in_specs=[pl.BlockSpec(memory_space=pltpu.SMEM), VMEM, VMEM],
+        in_specs=[pl.BlockSpec(memory_space=pltpu.SMEM), pl.BlockSpec(memory_space=pltpu.HBM), VMEM],
         out_specs=[VMEM] * 4,
+        scratch_shapes=[pltpu.VMEM((ROWS, FEATS), BF), pltpu.SemaphoreType.DMA((4,))],
         cost_estimate=pl.CostEstimate(flops=0, bytes_accessed=16 * FIRST * TILE, transcendentals=0),
-        compiler_params=pltpu.CompilerParams(vmem_limit_bytes=SMALL_CAP),
+        compiler_params=pltpu.CompilerParams(vmem_limit_bytes=PACK_CAP),
         name="pack",
     )(place, tokens, og4)
 

time: 104 us -> 103 us (level)
  local copies, waits for them, and re-layouts: 2.58 us -> 1.17 us
    unnamed x20 -> x16, local copies, waits for them, and re-layouts: 2.58 us -> 1.17 us
where the time goes in v4:
time: 103 us
  starting transfers between devices  41.8 us (41%)
  waiting for transfers between devices  38.6 us (37%)
  Pallas kernels  19.7 us (19%)
  local copies, waits for them, and re-layouts  1.17 us (1%)
  between operations  1.05 us (1%)
    ppermute x9, waiting for transfers between devices, along_x(): lax.ppermute(v, 'tp', [(N * a + b, N * ((a + s) % N) + b) for a in range(...  23.7 us
    ppermute x9, starting transfers between devices, along_y(): lax.ppermute(v, 'tp', [(N * a + b, N * a + (b + s) % N) for a in range(N)...  14.4 us
    ppermute x4, starting transfers between devices, onward(): return lax.ppermute(v, 'rep', pairs)  12.5 us
    ppermute x9, starting transfers between devices, along_x(): lax.ppermute(v, 'tp', [(N * a + b, N * ((a + s) % N) + b) for a in range(...  9.95 us
    ppermute x9, waiting for transfers between devices, along_y(): lax.ppermute(v, 'tp', [(N * a + b, N * a + (b + s) % N) for a in range(N)...  8.69 us
    pallas_call x2, Pallas kernels, keep_error(): pl.pallas_call(kernel, out_shape=[jax.ShapeDtypeStruct((COLS, FEATS), BF)...  5.49 us
    pallas_call x2, Pallas kernels, partials(): pl.pallas_call(kernel, out_shape=[shape(wide, F32), shape(wide, BF), shap...  5.44 us
    ppermute x2, starting transfers between devices, across(): lax.ppermute(v, 'rep', [(2 * a + c, 2 * a + 1 - c) for a in range(8) for...  4.85 us
  transfers between devices with their start and end apart: 24, of which 12 were waited for; matrix products, arithmetic and copies ran while one was open for 0% of the time, Pallas kernels for 12%

profile of v4, /device:TPU:1, one launch (start us, length us, event | category | flops | bytes accessed | tf_op | source)
XLA Modules:
  0.0 103.1 jit_solution(6039918102434401272)
XLA Ops:
  1.4 1.1 %copy-done.5 = bf16[1,3072,128]{2,1,0:T(8,128)(2,1)S(1)} copy-done((bf16[1,3072,128]{2,1,0:T(8,128)(2,1)S(1)}, bf16[1,3072,128]{2,1,0:T(8,128)(2,1)}, u32[]{:S(2)}) %copy-start.5) | copy-done | bytes 786456
  2.5 2.0 %pack.1 = (bf16[4240,128]{1,0:T(8,128)(2,1)S(1)}, bf16[4240,128]{1,0:T(8,128)(2,1)S(1)}, bf16[4240,128]{1,0:T(8,128)(2,1)S(1)}, bf16[4240,128]{1,0:T(8,128)(2,1)S(1)}) custom-call(s32[6]{0:T(128)S(1)} %pad_add_fusion.1.place_ref, bf16[192,4096]{1,0:T(8,128)(2,1)} %bitcast.9, bf16[4,4,192,128]{3,2,1,0:T(8,128)(2,1)S(1)} %bitcast.21), custom_call_target="tpu_custom_call" | custom-call | bytes 8683520 | tf_op jit(solution)/shard_map/pack/pallas_call | solution.py:91
  4.6 2.1 %collective-permute-start = (bf16[4240,128]{1,0:T(8,128)(2,1)S(1)}, bf16[4240,128]{1,0:T(8,128)(2,1)S(1)}, u32[]{:S(2)}, u32[]{:S(2)}) collective-permute-start(bf16[4240,128]{1,0:T(8,128)(2,1)S(1)} %get-tuple-element.36), channel_id=1, source_target_pairs={{0,4},{1,5},{2,6},{3,7},{4,8},{5,9},{6,10},{7,11},{8,12},{9,13},{1... | collective-permute-start | bytes 3256328 | tf_op jit(solution)/shard_map/ppermute | solution.py:31
  6.7 1.4 %collective-permute-start.1 = (bf16[4240,128]{1,0:T(8,128)(2,1)S(1)}, bf16[4240,128]{1,0:T(8,128)(2,1)S(1)}, u32[]{:S(2)}, u32[]{:S(2)}) collective-permute-start(bf16[4240,128]{1,0:T(8,128)(2,1)S(1)} %get-tuple-element.37), channel_id=1, source_target_pairs={{0,12},{1,13},{2,14},{3,15},{4,0},{5,1},{6,2},{7,3},{8,4},{9,5},{1... | collective-permute-start | bytes 3256328 | tf_op jit(solution)/shard_map/ppermute | solution.py:31
  8.0 1.4 %collective-permute-start.2 = (bf16[4240,128]{1,0:T(8,128)(2,1)S(1)}, bf16[4240,128]{1,0:T(8,128)(2,1)S(1)}, u32[]{:S(2)}, u32[]{:S(2)}) collective-permute-start(bf16[4240,128]{1,0:T(8,128)(2,1)S(1)} %get-tuple-element.38), channel_id=1, source_target_pairs={{0,1},{1,2},{2,3},{3,0},{4,5},{5,6},{6,7},{7,4},{8,9},{9,10},{10,1... | collective-permute-start | bytes 3256328 | tf_op jit(solution)/shard_map/ppermute | solution.py:35
  9.4 1.4 %collective-permute-start.3 = (bf16[4240,128]{1,0:T(8,128)(2,1)S(1)}, bf16[4240,128]{1,0:T(8,128)(2,1)S(1)}, u32[]{:S(2)}, u32[]{:S(2)}) collective-permute-start(bf16[4240,128]{1,0:T(8,128)(2,1)S(1)} %get-tuple-element.39), channel_id=1, source_target_pairs={{0,3},{1,0},{2,1},{3,2},{4,7},{5,4},{6,5},{7,6},{8,11},{9,8},{10,9... | collective-permute-start | bytes 3256328 | tf_op jit(solution)/shard_map/ppermute | solution.py:35
  10.9 18.4 %collective-permute-done.n_o.ref.l = bf16[4240,128]{1,0:T(8,128)(2,1)S(1)} collective-permute-done((bf16[4240,128]{1,0:T(8,128)(2,1)S(1)}, bf16[4240,128]{1,0:T(8,128)(2,1)S(1)}, u32[]{:S(2)}, u32[]{:S(2)}) %collective-permute-start) | collective-permute-done | bytes 1085472 | tf_op jit(solution)/shard_map/ppermute | solution.py:31
  29.4 2.0 %collective-permute-start.4 = (bf16[1936,128]{1,0:T(8,128)(2,1)S(1)}, bf16[1936,128]{1,0:T(8,128)(2,1)S(1)}, u32[]{:S(2)}, u32[]{:S(2)}) collective-permute-start(bf16[1936,128]{1,0:T(8,128)(2,1)S(1)} %relay.4), channel_id=1, source_target_pairs={{0,4},{1,5},{2,6},{3,7},{4,8},{5,9},{6,10},{7,11},{8,12},{9,13},{1... | collective-permute-start | bytes 1486856 | tf_op jit(solution)/shard_map/ppermute | solution.py:31
  31.4 1.7 %collective-permute-start.5 = (bf16[1936,128]{1,0:T(8,128)(2,1)S(1)}, bf16[1936,128]{1,0:T(8,128)(2,1)S(1)}, u32[]{:S(2)}, u32[]{:S(2)}) collective-permute-start(bf16[1936,128]{1,0:T(8,128)(2,1)S(1)} %relay.5), channel_id=1, source_target_pairs={{0,12},{1,13},{2,14},{3,15},{4,0},{5,1},{6,2},{7,3},{8,4},{9,5},{1... | collective-permute-start | bytes 1486856 | tf_op jit(solution)/shard_map/ppermute | solution.py:31
  33.1 2.8 %collective-permute-start.6 = (bf16[1936,128]{1,0:T(8,128)(2,1)S(1)}, bf16[1936,128]{1,0:T(8,128)(2,1)S(1)}, u32[]{:S(2)}, u32[]{:S(2)}) collective-permute-start(bf16[1936,128]{1,0:T(8,128)(2,1)S(1)} %relay.6), channel_id=1, source_target_pairs={{0,1},{1,2},{2,3},{3,0},{4,5},{5,6},{6,7},{7,4},{8,9},{9,10},{10,1... | collective-permute-start | bytes 1486856 | tf_op jit(solution)/shard_map/ppermute | solution.py:35
  35.9 1.5 %collective-permute-start.7 = (bf16[1936,128]{1,0:T(8,128)(2,1)S(1)}, bf16[1936,128]{1,0:T(8,128)(2,1)S(1)}, u32[]{:S(2)}, u32[]{:S(2)}) collective-permute-start(bf16[1936,128]{1,0:T(8,128)(2,1)S(1)} %relay.7), channel_id=1, source_target_pairs={{0,3},{1,0},{2,1},{3,2},{4,7},{5,4},{6,5},{7,6},{8,11},{9,8},{10,9... | collective-permute-start | bytes 1486856 | tf_op jit(solution)/shard_map/ppermute | solution.py:35
  37.5 1.3 %gather.3 = (bf16[768,2048]{1,0:T(8,128)(2,1)S(1)}, bf16[512,768]{1,0:T(8,128)(2,1)S(1)}, s32[16]{0:T(128)S(1)}) custom-call(s32[2]{0:T(128)S(1)} %pad_add_fusion.pos_ref, s32[4]{0:T(128)S(1)} %bitcast.25, bf16[4,4,192,128]{3,2,1,0:T(8,128)(2,1)S(1)} %bitcast.22, bf16[4240,128]{1,0:T(8,128)(2,1)S(1)} %collective-permute-done.2.l.ref.n_o, ...), custom_call_target="tpu_custom_call" | custom-call | bytes 8388608 | tf_op jit(solution)/shard_map/gather/pallas_call | solution.py:149
  38.8 1.3 %gather.2 = (bf16[768,2048]{1,0:T(8,128)(2,1)S(1)}, bf16[512,768]{1,0:T(8,128)(2,1)S(1)}, s32[16]{0:T(128)S(1)}) custom-call(s32[2]{0:T(128)S(1)} %pad_add_fusion.pos_ref, s32[4]{0:T(128)S(1)} %bitcast.26, bf16[4,4,192,128]{3,2,1,0:T(8,128)(2,1)S(1)} %bitcast.23, bf16[4240,128]{1,0:T(8,128)(2,1)S(1)} %collective-permute-done.n_o.ref.l, ...), custom_call_target="tpu_custom_call" | custom-call | bytes 8388608 | tf_op jit(solution)/shard_map/gather/pallas_call | solution.py:149
  40.1 1.3 %collective-permute-done.4.lo.a = bf16[1936,128]{1,0:T(8,128)(2,1)S(1)} collective-permute-done((bf16[1936,128]{1,0:T(8,128)(2,1)S(1)}, bf16[1936,128]{1,0:T(8,128)(2,1)S(1)}, u32[]{:S(2)}, u32[]{:S(2)}) %collective-permute-start.4) | collective-permute-done | bytes 495648 | tf_op jit(solution)/shard_map/ppermute | solution.py:31
  42.2 4.6 %collective-permute-done.6.a.lo = bf16[1936,128]{1,0:T(8,128)(2,1)S(1)} collective-permute-done((bf16[1936,128]{1,0:T(8,128)(2,1)S(1)}, bf16[1936,128]{1,0:T(8,128)(2,1)S(1)}, u32[]{:S(2)}, u32[]{:S(2)}) %collective-permute-start.6) | collective-permute-done | bytes 495648 | tf_op jit(solution)/shard_map/ppermute | solution.py:35
  46.8 2.7 %partials.2 = (f32[128,2048]{1,0:T(8,128)S(1)}, bf16[128,2048]{1,0:T(8,128)(2,1)S(1)}, bf16[128,2048]{1,0:T(8,128)(2,1)S(1)}, f32[512,128]{1,0:T(8,128)S(1)}, bf...) custom-call(s32[2]{0:T(128)S(1)} %pad_add_fusion.pos_ref, ...), custom_call_target="tpu_custom_call", output_to_operand_aliasing={{7}: (6, {}), {8}: (7, {})} | custom-call | flops 1610612736 | bytes 8388608 | tf_op jit(solution)/shard_map/partials/pallas_call | solution.py:210
  49.6 2.7 %collective-permute-start.9 = (bf16[1536,128]{1,0:T(8,128)(2,1)S(1)}, bf16[1536,128]{1,0:T(8,128)(2,1)S(1)}, u32[]{:S(2)}, u32[]{:S(2)}) collective-permute-start(bf16[1536,128]{1,0:T(8,128)(2,1)S(1)} %get-tuple-element.46), channel_id=1, source_target_pairs={{0,12},{1,13},{2,14},{3,15},{4,0},{5,1},{6,2},{7,3},{8,4},{9,5},{1... | collective-permute-start | bytes 1179656 | tf_op jit(solution)/shard_map/ppermute | solution.py:31
  52.3 2.7 %partials.3 = (f32[128,2048]{1,0:T(8,128)S(1)}, bf16[128,2048]{1,0:T(8,128)(2,1)S(1)}, bf16[128,2048]{1,0:T(8,128)(2,1)S(1)}, f32[512,128]{1,0:T(8,128)S(1)}, bf...) custom-call(s32[2]{0:T(128)S(1)} %pad_add_fusion.pos_ref, ...), custom_call_target="tpu_custom_call", output_to_operand_aliasing={{7}: (6, {}), {8}: (7, {})} | custom-call | flops 1610612736 | bytes 8388608 | tf_op jit(solution)/shard_map/partials/pallas_call | solution.py:210
  55.9 1.8 %collective-permute-start.12 = (bf16[1536,128]{1,0:T(8,128)(2,1)S(1)}, bf16[1536,128]{1,0:T(8,128)(2,1)S(1)}, u32[]{:S(2)}, u32[]{:S(2)}) collective-permute-start(bf16[1536,128]{1,0:T(8,128)(2,1)S(1)} %get-tuple-element.52), channel_id=1, source_target_pairs={{0,3},{1,0},{2,1},{3,2},{4,7},{5,4},{6,5},{7,6},{8,11},{9,8},{10,9... | collective-permute-start | bytes 1179656 | tf_op jit(solution)/shard_map/ppermute | solution.py:35
  58.5 1.8 %collective-permute-start.13 = (bf16[512,128]{1,0:T(8,128)(2,1)S(1)}, bf16[512,128]{1,0:T(8,128)(2,1)S(1)}, u32[]{:S(2)}, u32[]{:S(2)}) collective-permute-start(bf16[512,128]{1,0:T(8,128)(2,1)S(1)} %tied.1), channel_id=1, source_target_pairs={{0,2},{1,3},{2,0},{3,1},{4,6},{5,7},{6,4},{7,5},{8,10},{9,11},{10,... | collective-permute-start | bytes 393224 | tf_op jit(solution)/shard_map/ppermute | solution.py:35
  60.6 2.4 %collective-permute-done.10.refs_3_ = bf16[512,128]{1,0:T(8,128)(2,1)S(1)} collective-permute-done((bf16[512,128]{1,0:T(8,128)(2,1)S(1)}, bf16[512,128]{1,0:T(8,128)(2,1)S(1)}, u32[]{:S(2)}, u32[]{:S(2)}) %collective-permute-start.10) | collective-permute-done | bytes 131104 | tf_op jit(solution)/shard_map/ppermute | solution.py:31
  64.0 3.2 %collective-permute-done.13.refs_7_ = bf16[512,128]{1,0:T(8,128)(2,1)S(1)} collective-permute-done((bf16[512,128]{1,0:T(8,128)(2,1)S(1)}, bf16[512,128]{1,0:T(8,128)(2,1)S(1)}, u32[]{:S(2)}, u32[]{:S(2)}) %collective-permute-start.13) | collective-permute-done | bytes 131104 | tf_op jit(solution)/shard_map/ppermute | solution.py:35
  68.0 4.7 %collective-permute-start.14 = (bf16[528,128]{1,0:T(8,128)(2,1)S(1)}, bf16[528,128]{1,0:T(8,128)(2,1)S(1)}, u32[]{:S(2)}, u32[]{:S(2)}) collective-permute-start(bf16[528,128]{1,0:T(8,128)(2,1)S(1)} %sent_tiles.1.a.refs_0_), channel_id=1, source_target_pairs={{0,16},{16,0},{32,48},{48,32},{64,80},{80,64},{96,112},{112,96},{1... | collective-permute-start | bytes 405512 | tf_op jit(solution)/shard_map/ppermute | solution.py:44
  73.7 5.9 %collective-permute-start.16 = (bf16[1056,128]{1,0:T(8,128)(2,1)S(1)}, bf16[1056,128]{1,0:T(8,128)(2,1)S(1)}, u32[]{:S(2)}, u32[]{:S(2)}) collective-permute-start(bf16[1056,128]{1,0:T(8,128)(2,1)S(1)} %pair.1), channel_id=1, source_target_pairs={{0,64},{32,96},{64,128},{96,160},{128,192},{160,224},{192,0},{224,... | collective-permute-start | bytes 811016 | tf_op jit(solution)/shard_map/ppermute | solution.py:40
  80.7 1.9 %collective-permute-start.20 = (bf16[128,2048]{1,0:T(8,128)(2,1)S(1)}, bf16[128,2048]{1,0:T(8,128)(2,1)S(1)}, u32[]{:S(2)}, u32[]{:S(2)}) collective-permute-start(bf16[128,2048]{1,0:T(8,128)(2,1)S(1)} %get-tuple-element.58), channel_id=1, source_target_pairs={{0,3},{1,0},{2,1},{3,2},{4,7},{5,4},{6,5},{7,6},{8,11},{9,8},{10,9... | collective-permute-start | bytes 1572872 | tf_op jit(solution)/shard_map/ppermute | solution.py:35
  83.2 2.7 %collective-permute-done.16.ref.refs_2_ = bf16[1056,128]{1,0:T(8,128)(2,1)S(1)} collective-permute-done((bf16[1056,128]{1,0:T(8,128)(2,1)S(1)}, bf16[1056,128]{1,0:T(8,128)(2,1)S(1)}, u32[]{:S(2)}, u32[]{:S(2)}) %collective-permute-start.16) | collective-permute-done | bytes 270368 | tf_op jit(solution)/shard_map/ppermute | solution.py:40
  85.9 2.0 %collective-permute-start.17 = (bf16[1056,128]{1,0:T(8,128)(2,1)S(1)}, bf16[1056,128]{1,0:T(8,128)(2,1)S(1)}, u32[]{:S(2)}, u32[]{:S(2)}) collective-permute-start(bf16[1056,128]{1,0:T(8,128)(2,1)S(1)} %collective-permute-done.16.ref.refs_2_), channel_id=1, source_target_pairs={{0,32},{32,64},{64,96},{96,128},{128,160},{160,192},{192,224},{224... | collective-permute-start | bytes 811016 | tf_op jit(solution)/shard_map/ppermute | solution.py:40
  87.9 4.1 %collective-permute-start.18 = (bf16[528,128]{1,0:T(8,128)(2,1)S(1)}, bf16[528,128]{1,0:T(8,128)(2,1)S(1)}, u32[]{:S(2)}, u32[]{:S(2)}) collective-permute-start(bf16[528,128]{1,0:T(8,128)(2,1)S(1)} %own_half.1), channel_id=1, source_target_pairs={{0,64},{32,96},{64,128},{96,160},{128,192},{160,224},{192,0},{224,... | collective-permute-start | bytes 405512 | tf_op jit(solution)/shard_map/ppermute | solution.py:40
  92.0 3.1 %keep_error.2 = (bf16[128,4096]{1,0:T(8,128)(2,1)}, f32[8,128]{1,0:T(8,128)}) custom-call(s32[4]{0:T(128)S(1)} %bitcast.28, f32[128,2048]{1,0:T(8,128)S(1)} %get-tuple-element.59.g0, bf16[128,2048]{1,0:T(8,128)(2,1)S(1)} %collective-permute-done.21.g1, bf16[128,2048]{1,0:T(8,128)(2,1)S(1)} %collective-permute-done.22.g2, bf16[128,4096]{1,0:T(8,128)(2,1)S(1)} %bitcast.13, ...), custom_call_target="tpu_custom_call" | custom-call | flops 5242880 | bytes 5242880 | tf_op jit(solution)/shard_map/keep_error/pallas_call | solution.py:387
  95.2 2.3 %keep_error.3 = (bf16[128,4096]{1,0:T(8,128)(2,1)}, f32[8,128]{1,0:T(8,128)S(1)}) custom-call(s32[4]{0:T(128)S(1)} %bitcast.29, f32[128,2048]{1,0:T(8,128)S(1)} %get-tuple-element.54.g0, bf16[128,2048]{1,0:T(8,128)(2,1)S(1)} %collective-permute-done.19.g1, bf16[128,2048]{1,0:T(8,128)(2,1)S(1)} %collective-permute-done.20.g2, ...), custom_call_target="tpu_custom_call", output_to_operand_aliasing={{0}: (8, {})} | custom-call | flops 5242880 | bytes 5242880 | tf_op jit(solution)/shard_map/keep_error/pallas_call | solution.py:387
  98.5 2.6 %collective-permute-done.23.o_ref = bf16[128,4096]{1,0:T(8,128)(2,1)S(1)} collective-permute-done((bf16[128,4096]{1,0:T(8,128)(2,1)S(1)}, bf16[128,4096]{1,0:T(8,128)(2,1)S(1)}, u32[]{:S(2)}, u32[]{:S(2)}) %collective-permute-start.23) | collective-permute-done | bytes 1048608 | tf_op jit(solution)/shard_map/ppermute | solution.py:44
  101.1 1.9 %outer.1 = (f32[128,4096]{1,0:T(8,128)}, bf16[128,4096]{1,0:T(8,128)(2,1)}) custom-call(bf16[128,4096]{1,0:T(8,128)(2,1)S(1)} %add_tiles.1.m_ref, bf16[128,4096]{1,0:T(8,128)(2,1)S(1)} %collective-permute-done.23.o_ref, f32[128,4096]{1,0:T(8,128)S(1)} %copy-done, bf16[128,4096]{1,0:T(8,128)(2,1)S(1)} %copy-done.6), custom_call_target="tpu_custom_call" | custom-call | flops 3145728 | bytes 8388608 | tf_op jit(solution)/shard_map/outer/pallas_call | solution.py:455
  (53 shorter events, 9.3 us)
Async XLA Ops:
  1.4 1.1 %copy-start.5 = (bf16[1,3072,128]{2,1,0:T(8,128)(2,1)S(1)}, bf16[1,3072,128]{2,1,0:T(8,128)(2,1)}, u32[]{:S(2)}) copy-start(bf16[1,3072,128]{2,1,0:T(8,128)(2,1)} %param.9) | copy-start | bytes 2359300
  4.6 24.8 %collective-permute-start = (bf16[4240,128]{1,0:T(8,128)(2,1)S(1)}, bf16[4240,128]{1,0:T(8,128)(2,1)S(1)}, u32[]{:S(2)}, u32[]{:S(2)}) collective-permute-start(bf16[4240,128]{1,0:T(8,128)(2,1)S(1)} %get-tuple-element.36), channel_id=1, source_target_pairs={{0,4},{1,5},{2,6},{3,7},{4,8},{5,9},{6,10},{7,11},{8,12},{9,13},{1... | collective-permute-start | bytes 3256328 | tf_op jit(solution)/shard_map/ppermute | solution.py:31
  6.7 24.6 %collective-permute-start.1 = (bf16[4240,128]{1,0:T(8,128)(2,1)S(1)}, bf16[4240,128]{1,0:T(8,128)(2,1)S(1)}, u32[]{:S(2)}, u32[]{:S(2)}) collective-permute-start(bf16[4240,128]{1,0:T(8,128)(2,1)S(1)} %get-tuple-element.37), channel_id=1, source_target_pairs={{0,12},{1,13},{2,14},{3,15},{4,0},{5,1},{6,2},{7,3},{8,4},{9,5},{1... | collective-permute-start | bytes 3256328 | tf_op jit(solution)/shard_map/ppermute | solution.py:31
  8.0 25.0 %collective-permute-start.2 = (bf16[4240,128]{1,0:T(8,128)(2,1)S(1)}, bf16[4240,128]{1,0:T(8,128)(2,1)S(1)}, u32[]{:S(2)}, u32[]{:S(2)}) collective-permute-start(bf16[4240,128]{1,0:T(8,128)(2,1)S(1)} %get-tuple-element.38), channel_id=1, source_target_pairs={{0,1},{1,2},{2,3},{3,0},{4,5},{5,6},{6,7},{7,4},{8,9},{9,10},{10,1... | collective-permute-start | bytes 3256328 | tf_op jit(solution)/shard_map/ppermute | solution.py:35
  9.4 26.4 %collective-permute-start.3 = (bf16[4240,128]{1,0:T(8,128)(2,1)S(1)}, bf16[4240,128]{1,0:T(8,128)(2,1)S(1)}, u32[]{:S(2)}, u32[]{:S(2)}) collective-permute-start(bf16[4240,128]{1,0:T(8,128)(2,1)S(1)} %get-tuple-element.39), channel_id=1, source_target_pairs={{0,3},{1,0},{2,1},{3,2},{4,7},{5,4},{6,5},{7,6},{8,11},{9,8},{10,9... | collective-permute-start | bytes 3256328 | tf_op jit(solution)/shard_map/ppermute | solution.py:35
  29.4 12.1 %collective-permute-start.4 = (bf16[1936,128]{1,0:T(8,128)(2,1)S(1)}, bf16[1936,128]{1,0:T(8,128)(2,1)S(1)}, u32[]{:S(2)}, u32[]{:S(2)}) collective-permute-start(bf16[1936,128]{1,0:T(8,128)(2,1)S(1)} %relay.4), channel_id=1, source_target_pairs={{0,4},{1,5},{2,6},{3,7},{4,8},{5,9},{6,10},{7,11},{8,12},{9,13},{1... | collective-permute-start | bytes 1486856 | tf_op jit(solution)/shard_map/ppermute | solution.py:31
  31.4 10.8 %collective-permute-start.5 = (bf16[1936,128]{1,0:T(8,128)(2,1)S(1)}, bf16[1936,128]{1,0:T(8,128)(2,1)S(1)}, u32[]{:S(2)}, u32[]{:S(2)}) collective-permute-start(bf16[1936,128]{1,0:T(8,128)(2,1)S(1)} %relay.5), channel_id=1, source_target_pairs={{0,12},{1,13},{2,14},{3,15},{4,0},{5,1},{6,2},{7,3},{8,4},{9,5},{1... | collective-permute-start | bytes 1486856 | tf_op jit(solution)/shard_map/ppermute | solution.py:31
  33.1 4.4 %copy-start.1 = (bf16[1,192,4096]{2,1,0:T(8,128)(2,1)S(1)}, bf16[1,192,4096]{2,1,0:T(8,128)(2,1)}, u32[]{:S(2)}) copy-start(bf16[1,192,4096]{2,1,0:T(8,128)(2,1)} %param.8) | copy-start | bytes 4718596
  33.1 4.4 %copy-start.7 = (s32[1,1,4]{2,1,0:T(1,128)S(1)}, s32[1,1,4]{2,1,0:T(1,128)}, u32[]{:S(2)}) copy-start(s32[1,1,4]{2,1,0:T(1,128)} %param.15) | copy-start | bytes 52
  33.1 13.7 %collective-permute-start.6 = (bf16[1936,128]{1,0:T(8,128)(2,1)S(1)}, bf16[1936,128]{1,0:T(8,128)(2,1)S(1)}, u32[]{:S(2)}, u32[]{:S(2)}) collective-permute-start(bf16[1936,128]{1,0:T(8,128)(2,1)S(1)} %relay.6), channel_id=1, source_target_pairs={{0,1},{1,2},{2,3},{3,0},{4,5},{5,6},{6,7},{7,4},{8,9},{9,10},{10,1... | collective-permute-start | bytes 1486856 | tf_op jit(solution)/shard_map/ppermute | solution.py:35
  35.9 10.9 %collective-permute-start.7 = (bf16[1936,128]{1,0:T(8,128)(2,1)S(1)}, bf16[1936,128]{1,0:T(8,128)(2,1)S(1)}, u32[]{:S(2)}, u32[]{:S(2)}) collective-permute-start(bf16[1936,128]{1,0:T(8,128)(2,1)S(1)} %relay.7), channel_id=1, source_target_pairs={{0,3},{1,0},{2,1},{3,2},{4,7},{5,4},{6,5},{7,6},{8,11},{9,8},{10,9... | collective-permute-start | bytes 1486856 | tf_op jit(solution)/shard_map/ppermute | solution.py:35
  49.5 9.0 %collective-permute-start.8 = (bf16[1536,128]{1,0:T(8,128)(2,1)S(1)}, bf16[1536,128]{1,0:T(8,128)(2,1)S(1)}, u32[]{:S(2)}, u32[]{:S(2)}) collective-permute-start(bf16[1536,128]{1,0:T(8,128)(2,1)S(1)} %get-tuple-element.45), channel_id=1, source_target_pairs={{0,4},{1,5},{2,6},{3,7},{4,8},{5,9},{6,10},{7,11},{8,12},{9,13},{1... | collective-permute-start | bytes 1179656 | tf_op jit(solution)/shard_map/ppermute | solution.py:31
  49.6 10.7 %collective-permute-start.9 = (bf16[1536,128]{1,0:T(8,128)(2,1)S(1)}, bf16[1536,128]{1,0:T(8,128)(2,1)S(1)}, u32[]{:S(2)}, u32[]{:S(2)}) collective-permute-start(bf16[1536,128]{1,0:T(8,128)(2,1)S(1)} %get-tuple-element.46), channel_id=1, source_target_pairs={{0,12},{1,13},{2,14},{3,15},{4,0},{5,1},{6,2},{7,3},{8,4},{9,5},{1... | collective-permute-start | bytes 1179656 | tf_op jit(solution)/shard_map/ppermute | solution.py:31
  52.3 14.9 %copy-start.2 = (bf16[1,128,4096]{2,1,0:T(8,128)(2,1)S(1)}, bf16[1,128,4096]{2,1,0:T(8,128)(2,1)}, u32[]{:S(2)}) copy-start(bf16[1,128,4096]{2,1,0:T(8,128)(2,1)} %param.11) | copy-start | bytes 3145732
  52.3 14.9 %copy-start.3 = (bf16[1,128,4096]{2,1,0:T(8,128)(2,1)S(1)}, bf16[1,128,4096]{2,1,0:T(8,128)(2,1)}, u32[]{:S(2)}) copy-start(bf16[1,128,4096]{2,1,0:T(8,128)(2,1)} %param.12) | copy-start | bytes 3145732
  52.3 14.9 %copy-start.4 = (bf16[1,128,4096]{2,1,0:T(8,128)(2,1)S(1)}, bf16[1,128,4096]{2,1,0:T(8,128)(2,1)}, u32[]{:S(2)}) copy-start(bf16[1,128,4096]{2,1,0:T(8,128)(2,1)} %param.13) | copy-start | bytes 3145732
  55.0 8.4 %collective-permute-start.11 = (bf16[1536,128]{1,0:T(8,128)(2,1)S(1)}, bf16[1536,128]{1,0:T(8,128)(2,1)S(1)}, u32[]{:S(2)}, u32[]{:S(2)}) collective-permute-start(bf16[1536,128]{1,0:T(8,128)(2,1)S(1)} %get-tuple-element.51), channel_id=1, source_target_pairs={{0,1},{1,2},{2,3},{3,0},{4,5},{5,6},{6,7},{7,4},{8,9},{9,10},{10,1... | collective-permute-start | bytes 1179656 | tf_op jit(solution)/shard_map/ppermute | solution.py:35
  55.9 8.0 %collective-permute-start.12 = (bf16[1536,128]{1,0:T(8,128)(2,1)S(1)}, bf16[1536,128]{1,0:T(8,128)(2,1)S(1)}, u32[]{:S(2)}, u32[]{:S(2)}) collective-permute-start(bf16[1536,128]{1,0:T(8,128)(2,1)S(1)} %get-tuple-element.52), channel_id=1, source_target_pairs={{0,3},{1,0},{2,1},{3,2},{4,7},{5,4},{6,5},{7,6},{8,11},{9,8},{10,9... | collective-permute-start | bytes 1179656 | tf_op jit(solution)/shard_map/ppermute | solution.py:35
  57.7 5.3 %collective-permute-start.10 = (bf16[512,128]{1,0:T(8,128)(2,1)S(1)}, bf16[512,128]{1,0:T(8,128)(2,1)S(1)}, u32[]{:S(2)}, u32[]{:S(2)}) collective-permute-start(bf16[512,128]{1,0:T(8,128)(2,1)S(1)} %get-tuple-element.47), channel_id=1, source_target_pairs={{0,8},{1,9},{2,10},{3,11},{4,12},{5,13},{6,14},{7,15},{8,0},{9,1},... | collective-permute-start | bytes 393224 | tf_op jit(solution)/shard_map/ppermute | solution.py:31
  58.5 8.7 %copy-start = (f32[128,4096]{1,0:T(8,128)S(1)}, f32[128,4096]{1,0:T(8,128)}, u32[]{:S(2)}) copy-start(f32[128,4096]{1,0:T(8,128)} %w_ref.5) | copy-start | bytes 6291460
  58.5 8.7 %collective-permute-start.13 = (bf16[512,128]{1,0:T(8,128)(2,1)S(1)}, bf16[512,128]{1,0:T(8,128)(2,1)S(1)}, u32[]{:S(2)}, u32[]{:S(2)}) collective-permute-start(bf16[512,128]{1,0:T(8,128)(2,1)S(1)} %tied.1), channel_id=1, source_target_pairs={{0,2},{1,3},{2,0},{3,1},{4,6},{5,7},{6,4},{7,5},{8,10},{9,11},{10,... | collective-permute-start | bytes 393224 | tf_op jit(solution)/shard_map/ppermute | solution.py:35
  60.6 22.1 %collective-permute-start.21 = (bf16[128,2048]{1,0:T(8,128)(2,1)S(1)}, bf16[128,2048]{1,0:T(8,128)(2,1)S(1)}, u32[]{:S(2)}, u32[]{:S(2)}) collective-permute-start(bf16[128,2048]{1,0:T(8,128)(2,1)S(1)} %get-tuple-element.62), channel_id=1, source_target_pairs={{0,4},{1,5},{2,6},{3,7},{4,8},{5,9},{6,10},{7,11},{8,12},{9,13},{1... | collective-permute-start | bytes 1572872 | tf_op jit(solution)/shard_map/ppermute | solution.py:31
  68.0 5.7 %collective-permute-start.14 = (bf16[528,128]{1,0:T(8,128)(2,1)S(1)}, bf16[528,128]{1,0:T(8,128)(2,1)S(1)}, u32[]{:S(2)}, u32[]{:S(2)}) collective-permute-start(bf16[528,128]{1,0:T(8,128)(2,1)S(1)} %sent_tiles.1.a.refs_0_), channel_id=1, source_target_pairs={{0,16},{16,0},{32,48},{48,32},{64,80},{80,64},{96,112},{112,96},{1... | collective-permute-start | bytes 405512 | tf_op jit(solution)/shard_map/ppermute | solution.py:44
  72.7 15.2 %collective-permute-start.22 = (bf16[128,2048]{1,0:T(8,128)(2,1)S(1)}, bf16[128,2048]{1,0:T(8,128)(2,1)S(1)}, u32[]{:S(2)}, u32[]{:S(2)}) collective-permute-start(bf16[128,2048]{1,0:T(8,128)(2,1)S(1)} %get-tuple-element.63), channel_id=1, source_target_pairs={{0,12},{1,13},{2,14},{3,15},{4,0},{5,1},{6,2},{7,3},{8,4},{9,5},{1... | collective-permute-start | bytes 1572872 | tf_op jit(solution)/shard_map/ppermute | solution.py:31
  73.7 12.2 %collective-permute-start.16 = (bf16[1056,128]{1,0:T(8,128)(2,1)S(1)}, bf16[1056,128]{1,0:T(8,128)(2,1)S(1)}, u32[]{:S(2)}, u32[]{:S(2)}) collective-permute-start(bf16[1056,128]{1,0:T(8,128)(2,1)S(1)} %pair.1), channel_id=1, source_target_pairs={{0,64},{32,96},{64,128},{96,160},{128,192},{160,224},{192,0},{224,... | collective-permute-start | bytes 811016 | tf_op jit(solution)/shard_map/ppermute | solution.py:40
  79.9 15.3 %collective-permute-start.19 = (bf16[128,2048]{1,0:T(8,128)(2,1)S(1)}, bf16[128,2048]{1,0:T(8,128)(2,1)S(1)}, u32[]{:S(2)}, u32[]{:S(2)}) collective-permute-start(bf16[128,2048]{1,0:T(8,128)(2,1)S(1)} %get-tuple-element.57), channel_id=1, source_target_pairs={{0,1},{1,2},{2,3},{3,0},{4,5},{5,6},{6,7},{7,4},{8,9},{9,10},{10,1... | collective-permute-start | bytes 1572872 | tf_op jit(solution)/shard_map/ppermute | solution.py:35
  80.7 14.4 %collective-permute-start.20 = (bf16[128,2048]{1,0:T(8,128)(2,1)S(1)}, bf16[128,2048]{1,0:T(8,128)(2,1)S(1)}, u32[]{:S(2)}, u32[]{:S(2)}) collective-permute-start(bf16[128,2048]{1,0:T(8,128)(2,1)S(1)} %get-tuple-element.58), channel_id=1, source_target_pairs={{0,3},{1,0},{2,1},{3,2},{4,7},{5,4},{6,5},{7,6},{8,11},{9,8},{10,9... | collective-permute-start | bytes 1572872 | tf_op jit(solution)/shard_map/ppermute | solution.py:35
  82.6 14.9 %collective-permute-start.15 = (bf16[1056,128]{1,0:T(8,128)(2,1)S(1)}, bf16[1056,128]{1,0:T(8,128)(2,1)S(1)}, u32[]{:S(2)}, u32[]{:S(2)}) collective-permute-start(bf16[1056,128]{1,0:T(8,128)(2,1)S(1)} %pair.1), channel_id=1, source_target_pairs={{0,32},{32,64},{64,96},{96,128},{128,160},{160,192},{192,224},{224... | collective-permute-start | bytes 811016 | tf_op jit(solution)/shard_map/ppermute | solution.py:40
  85.9 11.7 %collective-permute-start.17 = (bf16[1056,128]{1,0:T(8,128)(2,1)S(1)}, bf16[1056,128]{1,0:T(8,128)(2,1)S(1)}, u32[]{:S(2)}, u32[]{:S(2)}) collective-permute-start(bf16[1056,128]{1,0:T(8,128)(2,1)S(1)} %collective-permute-done.16.ref.refs_2_), channel_id=1, source_target_pairs={{0,32},{32,64},{64,96},{96,128},{128,160},{160,192},{192,224},{224... | collective-permute-start | bytes 811016 | tf_op jit(solution)/shard_map/ppermute | solution.py:40
  87.9 9.6 %collective-permute-start.18 = (bf16[528,128]{1,0:T(8,128)(2,1)S(1)}, bf16[528,128]{1,0:T(8,128)(2,1)S(1)}, u32[]{:S(2)}, u32[]{:S(2)}) collective-permute-start(bf16[528,128]{1,0:T(8,128)(2,1)S(1)} %own_half.1), channel_id=1, source_target_pairs={{0,64},{32,96},{64,128},{96,160},{128,192},{160,224},{192,0},{224,... | collective-permute-start | bytes 405512 | tf_op jit(solution)/shard_map/ppermute | solution.py:40
  97.5 3.6 %copy-start.6 = (bf16[128,4096]{1,0:T(8,128)(2,1)S(1)}, bf16[128,4096]{1,0:T(8,128)(2,1)}, u32[]{:S(2)}) copy-start(bf16[128,4096]{1,0:T(8,128)(2,1)} %v_ref.1) | copy-start | bytes 3145732
  98.3 2.7 %collective-permute-start.23 = (bf16[128,4096]{1,0:T(8,128)(2,1)S(1)}, bf16[128,4096]{1,0:T(8,128)(2,1)S(1)}, u32[]{:S(2)}, u32[]{:S(2)}) collective-permute-start(bf16[128,4096]{1,0:T(8,128)(2,1)S(1)} %add_tiles.1.m_ref), channel_id=1, source_target_pairs={{0,16},{16,0},{32,48},{48,32},{64,80},{80,64},{96,112},{112,96},{1... | collective-permute-start | bytes 3145736 | tf_op jit(solution)/shard_map/ppermute | solution.py:44

commit v5 on v4

--- a/solution.py
+++ b/solution.py
@@ -494,8 +494,8 @@
     own = pair(mine, across(mine))
     z1, z2 = onward(own, 1), onward(own, 2)
     z3, z4 = onward(z2, 1), onward(own_half(z2), 2)
-    error_new, flag = keep_error(ids, ga, *state, 0)
-    error_new, flag = keep_error(ids, gb, *state, 1, error_new)
+    error_new, flag = keep_error(ids, gb, *state, 1)
+    error_new, flag = keep_error(ids, ga, *state, 0, error_new)
     agg = add_tiles([mine, z1, z2, z3, z4], [flag])
     weights_new, momentum_new = outer(agg, across(agg), weights, momentum)
 

time: 103 us -> 103 us (level)
  waiting for transfers between devices: 38.6 us -> 35.2 us
  starting transfers between devices: 41.8 us -> 44.9 us
    ppermute x9, starting transfers between devices: 9.95 us -> 12.5 us  [along_x(): lax.ppermute(v, 'tp', [(N * a + b, N * ((a + s) % N) + b) for a in range(...]
    ppermute x9, waiting for transfers between devices: 8.69 us -> 6.71 us  [along_y(): lax.ppermute(v, 'tp', [(N * a + b, N * a + (b + s) % N) for a in range(N)...]
    ppermute x2, starting transfers between devices: 4.85 us -> 6.71 us  [across(): lax.ppermute(v, 'rep', [(2 * a + c, 2 * a + 1 - c) for a in range(8) for...]
    ppermute x2, waiting for transfers between devices: 3.56 us -> 2.29 us  [across(): lax.ppermute(v, 'rep', [(2 * a + c, 2 * a + 1 - c) for a in range(8) for...]
  transfers between devices with their start and end apart: 24 -> 24, of which waited for: 12 -> 11; matrix products, arithmetic and copies ran while one was open for 0% -> 0% of each run, Pallas kernels for 12% -> 12%
where the time goes in v5:
time: 103 us
  starting transfers between devices  44.9 us (44%)
  waiting for transfers between devices  35.2 us (34%)
  Pallas kernels  19.8 us (19%)
  local copies, waits for them, and re-layouts  1.18 us (1%)
  between operations  1.06 us (1%)
    ppermute x9, waiting for transfers between devices, along_x(): lax.ppermute(v, 'tp', [(N * a + b, N * ((a + s) % N) + b) for a in range(...  23.5 us
    ppermute x9, starting transfers between devices, along_y(): lax.ppermute(v, 'tp', [(N * a + b, N * a + (b + s) % N) for a in range(N)...  13.5 us
    ppermute x9, starting transfers between devices, along_x(): lax.ppermute(v, 'tp', [(N * a + b, N * ((a + s) % N) + b) for a in range(...  12.5 us
    ppermute x4, starting transfers between devices, onward(): return lax.ppermute(v, 'rep', pairs)  12.1 us
    ppermute x9, waiting for transfers between devices, along_y(): lax.ppermute(v, 'tp', [(N * a + b, N * a + (b + s) % N) for a in range(N)...  6.71 us
    ppermute x2, starting transfers between devices, across(): lax.ppermute(v, 'rep', [(2 * a + c, 2 * a + 1 - c) for a in range(8) for...  6.71 us
    pallas_call x2, Pallas kernels, keep_error(): pl.pallas_call(kernel, out_shape=[jax.ShapeDtypeStruct((COLS, FEATS), BF)...  5.49 us
    pallas_call x2, Pallas kernels, partials(): pl.pallas_call(kernel, out_shape=[shape(wide, F32), shape(wide, BF), shap...  5.45 us
  transfers between devices with their start and end apart: 24, of which 11 were waited for; matrix products, arithmetic and copies ran while one was open for 0% of the time, Pallas kernels for 12%

profile of v5, /device:TPU:1, one launch (start us, length us, event | category | flops | bytes accessed | tf_op | source)
XLA Modules:
  0.0 103.0 jit_solution(10348342572404828230)
XLA Ops:
  2.5 2.0 %pack.1 = (bf16[4240,128]{1,0:T(8,128)(2,1)S(1)}, bf16[4240,128]{1,0:T(8,128)(2,1)S(1)}, bf16[4240,128]{1,0:T(8,128)(2,1)S(1)}, bf16[4240,128]{1,0:T(8,128)(2,1)S(1)}) custom-call(s32[6]{0:T(128)S(1)} %pad_add_fusion.1.place_ref, bf16[192,4096]{1,0:T(8,128)(2,1)} %bitcast.9, bf16[4,4,192,128]{3,2,1,0:T(8,128)(2,1)S(1)} %bitcast.21), custom_call_target="tpu_custom_call" | custom-call | bytes 8683520 | tf_op jit(solution)/shard_map/pack/pallas_call | solution.py:91
  4.6 2.1 %collective-permute-start = (bf16[4240,128]{1,0:T(8,128)(2,1)S(1)}, bf16[4240,128]{1,0:T(8,128)(2,1)S(1)}, u32[]{:S(2)}, u32[]{:S(2)}) collective-permute-start(bf16[4240,128]{1,0:T(8,128)(2,1)S(1)} %get-tuple-element.36), channel_id=1, source_target_pairs={{0,4},{1,5},{2,6},{3,7},{4,8},{5,9},{6,10},{7,11},{8,12},{9,13},{1... | collective-permute-start | bytes 3256328 | tf_op jit(solution)/shard_map/ppermute | solution.py:31
  6.7 1.4 %collective-permute-start.1 = (bf16[4240,128]{1,0:T(8,128)(2,1)S(1)}, bf16[4240,128]{1,0:T(8,128)(2,1)S(1)}, u32[]{:S(2)}, u32[]{:S(2)}) collective-permute-start(bf16[4240,128]{1,0:T(8,128)(2,1)S(1)} %get-tuple-element.37), channel_id=1, source_target_pairs={{0,12},{1,13},{2,14},{3,15},{4,0},{5,1},{6,2},{7,3},{8,4},{9,5},{1... | collective-permute-start | bytes 3256328 | tf_op jit(solution)/shard_map/ppermute | solution.py:31
  8.0 1.4 %collective-permute-start.2 = (bf16[4240,128]{1,0:T(8,128)(2,1)S(1)}, bf16[4240,128]{1,0:T(8,128)(2,1)S(1)}, u32[]{:S(2)}, u32[]{:S(2)}) collective-permute-start(bf16[4240,128]{1,0:T(8,128)(2,1)S(1)} %get-tuple-element.38), channel_id=1, source_target_pairs={{0,1},{1,2},{2,3},{3,0},{4,5},{5,6},{6,7},{7,4},{8,9},{9,10},{10,1... | collective-permute-start | bytes 3256328 | tf_op jit(solution)/shard_map/ppermute | solution.py:35
  9.4 1.4 %collective-permute-start.3 = (bf16[4240,128]{1,0:T(8,128)(2,1)S(1)}, bf16[4240,128]{1,0:T(8,128)(2,1)S(1)}, u32[]{:S(2)}, u32[]{:S(2)}) collective-permute-start(bf16[4240,128]{1,0:T(8,128)(2,1)S(1)} %get-tuple-element.39), channel_id=1, source_target_pairs={{0,3},{1,0},{2,1},{3,2},{4,7},{5,4},{6,5},{7,6},{8,11},{9,8},{10,9... | collective-permute-start | bytes 3256328 | tf_op jit(solution)/shard_map/ppermute | solution.py:35
  10.9 18.4 %collective-permute-done.n_o.ref.l = bf16[4240,128]{1,0:T(8,128)(2,1)S(1)} collective-permute-done((bf16[4240,128]{1,0:T(8,128)(2,1)S(1)}, bf16[4240,128]{1,0:T(8,128)(2,1)S(1)}, u32[]{:S(2)}, u32[]{:S(2)}) %collective-permute-start) | collective-permute-done | bytes 1085472 | tf_op jit(solution)/shard_map/ppermute | solution.py:31
  29.4 2.0 %collective-permute-start.4 = (bf16[1936,128]{1,0:T(8,128)(2,1)S(1)}, bf16[1936,128]{1,0:T(8,128)(2,1)S(1)}, u32[]{:S(2)}, u32[]{:S(2)}) collective-permute-start(bf16[1936,128]{1,0:T(8,128)(2,1)S(1)} %relay.4), channel_id=1, source_target_pairs={{0,4},{1,5},{2,6},{3,7},{4,8},{5,9},{6,10},{7,11},{8,12},{9,13},{1... | collective-permute-start | bytes 1486856 | tf_op jit(solution)/shard_map/ppermute | solution.py:31
  31.4 1.7 %collective-permute-start.5 = (bf16[1936,128]{1,0:T(8,128)(2,1)S(1)}, bf16[1936,128]{1,0:T(8,128)(2,1)S(1)}, u32[]{:S(2)}, u32[]{:S(2)}) collective-permute-start(bf16[1936,128]{1,0:T(8,128)(2,1)S(1)} %relay.5), channel_id=1, source_target_pairs={{0,12},{1,13},{2,14},{3,15},{4,0},{5,1},{6,2},{7,3},{8,4},{9,5},{1... | collective-permute-start | bytes 1486856 | tf_op jit(solution)/shard_map/ppermute | solution.py:31
  33.1 2.8 %collective-permute-start.6 = (bf16[1936,128]{1,0:T(8,128)(2,1)S(1)}, bf16[1936,128]{1,0:T(8,128)(2,1)S(1)}, u32[]{:S(2)}, u32[]{:S(2)}) collective-permute-start(bf16[1936,128]{1,0:T(8,128)(2,1)S(1)} %relay.6), channel_id=1, source_target_pairs={{0,1},{1,2},{2,3},{3,0},{4,5},{5,6},{6,7},{7,4},{8,9},{9,10},{10,1... | collective-permute-start | bytes 1486856 | tf_op jit(solution)/shard_map/ppermute | solution.py:35
  35.9 1.5 %collective-permute-start.7 = (bf16[1936,128]{1,0:T(8,128)(2,1)S(1)}, bf16[1936,128]{1,0:T(8,128)(2,1)S(1)}, u32[]{:S(2)}, u32[]{:S(2)}) collective-permute-start(bf16[1936,128]{1,0:T(8,128)(2,1)S(1)} %relay.7), channel_id=1, source_target_pairs={{0,3},{1,0},{2,1},{3,2},{4,7},{5,4},{6,5},{7,6},{8,11},{9,8},{10,9... | collective-permute-start | bytes 1486856 | tf_op jit(solution)/shard_map/ppermute | solution.py:35
  37.5 1.3 %gather.3 = (bf16[768,2048]{1,0:T(8,128)(2,1)S(1)}, bf16[512,768]{1,0:T(8,128)(2,1)S(1)}, s32[16]{0:T(128)S(1)}) custom-call(s32[2]{0:T(128)S(1)} %pad_add_fusion.pos_ref, s32[4]{0:T(128)S(1)} %bitcast.25, bf16[4,4,192,128]{3,2,1,0:T(8,128)(2,1)S(1)} %bitcast.22, bf16[4240,128]{1,0:T(8,128)(2,1)S(1)} %collective-permute-done.2.l.ref.n_o, ...), custom_call_target="tpu_custom_call" | custom-call | bytes 8388608 | tf_op jit(solution)/shard_map/gather/pallas_call | solution.py:149
  38.8 1.3 %gather.2 = (bf16[768,2048]{1,0:T(8,128)(2,1)S(1)}, bf16[512,768]{1,0:T(8,128)(2,1)S(1)}, s32[16]{0:T(128)S(1)}) custom-call(s32[2]{0:T(128)S(1)} %pad_add_fusion.pos_ref, s32[4]{0:T(128)S(1)} %bitcast.26, bf16[4,4,192,128]{3,2,1,0:T(8,128)(2,1)S(1)} %bitcast.23, bf16[4240,128]{1,0:T(8,128)(2,1)S(1)} %collective-permute-done.n_o.ref.l, ...), custom_call_target="tpu_custom_call" | custom-call | bytes 8388608 | tf_op jit(solution)/shard_map/gather/pallas_call | solution.py:149
  40.1 1.3 %collective-permute-done.4.lo.a = bf16[1936,128]{1,0:T(8,128)(2,1)S(1)} collective-permute-done((bf16[1936,128]{1,0:T(8,128)(2,1)S(1)}, bf16[1936,128]{1,0:T(8,128)(2,1)S(1)}, u32[]{:S(2)}, u32[]{:S(2)}) %collective-permute-start.4) | collective-permute-done | bytes 495648 | tf_op jit(solution)/shard_map/ppermute | solution.py:31
  42.2 4.6 %collective-permute-done.6.a.lo = bf16[1936,128]{1,0:T(8,128)(2,1)S(1)} collective-permute-done((bf16[1936,128]{1,0:T(8,128)(2,1)S(1)}, bf16[1936,128]{1,0:T(8,128)(2,1)S(1)}, u32[]{:S(2)}, u32[]{:S(2)}) %collective-permute-start.6) | collective-permute-done | bytes 495648 | tf_op jit(solution)/shard_map/ppermute | solution.py:35
  46.8 2.7 %partials.2 = (f32[128,2048]{1,0:T(8,128)S(1)}, bf16[128,2048]{1,0:T(8,128)(2,1)S(1)}, bf16[128,2048]{1,0:T(8,128)(2,1)S(1)}, f32[512,128]{1,0:T(8,128)S(1)}, bf...) custom-call(s32[2]{0:T(128)S(1)} %pad_add_fusion.pos_ref, ...), custom_call_target="tpu_custom_call", output_to_operand_aliasing={{7}: (6, {}), {8}: (7, {})} | custom-call | flops 1610612736 | bytes 8388608 | tf_op jit(solution)/shard_map/partials/pallas_call | solution.py:210
  49.6 2.7 %partials.3 = (f32[128,2048]{1,0:T(8,128)S(1)}, bf16[128,2048]{1,0:T(8,128)(2,1)S(1)}, bf16[128,2048]{1,0:T(8,128)(2,1)S(1)}, f32[512,128]{1,0:T(8,128)S(1)}, bf...) custom-call(s32[2]{0:T(128)S(1)} %pad_add_fusion.pos_ref, ...), custom_call_target="tpu_custom_call", output_to_operand_aliasing={{7}: (6, {}), {8}: (7, {})} | custom-call | flops 1610612736 | bytes 8388608 | tf_op jit(solution)/shard_map/partials/pallas_call | solution.py:210
  53.5 1.7 %collective-permute-start.12 = (bf16[1536,128]{1,0:T(8,128)(2,1)S(1)}, bf16[1536,128]{1,0:T(8,128)(2,1)S(1)}, u32[]{:S(2)}, u32[]{:S(2)}) collective-permute-start(bf16[1536,128]{1,0:T(8,128)(2,1)S(1)} %get-tuple-element.52), channel_id=1, source_target_pairs={{0,3},{1,0},{2,1},{3,2},{4,7},{5,4},{6,5},{7,6},{8,11},{9,8},{10,9... | collective-permute-start | bytes 1179656 | tf_op jit(solution)/shard_map/ppermute | solution.py:35
  55.3 2.6 %collective-permute-start.9 = (bf16[1536,128]{1,0:T(8,128)(2,1)S(1)}, bf16[1536,128]{1,0:T(8,128)(2,1)S(1)}, u32[]{:S(2)}, u32[]{:S(2)}) collective-permute-start(bf16[1536,128]{1,0:T(8,128)(2,1)S(1)} %get-tuple-element.46), channel_id=1, source_target_pairs={{0,12},{1,13},{2,14},{3,15},{4,0},{5,1},{6,2},{7,3},{8,4},{9,5},{1... | collective-permute-start | bytes 1179656 | tf_op jit(solution)/shard_map/ppermute | solution.py:31
  58.5 1.8 %collective-permute-start.13 = (bf16[512,128]{1,0:T(8,128)(2,1)S(1)}, bf16[512,128]{1,0:T(8,128)(2,1)S(1)}, u32[]{:S(2)}, u32[]{:S(2)}) collective-permute-start(bf16[512,128]{1,0:T(8,128)(2,1)S(1)} %tied.1), channel_id=1, source_target_pairs={{0,2},{1,3},{2,0},{3,1},{4,6},{5,7},{6,4},{7,5},{8,10},{9,11},{10,... | collective-permute-start | bytes 393224 | tf_op jit(solution)/shard_map/ppermute | solution.py:35
  60.3 1.2 %collective-permute-done.11.refs_5_.a = bf16[1536,128]{1,0:T(8,128)(2,1)S(1)} collective-permute-done((bf16[1536,128]{1,0:T(8,128)(2,1)S(1)}, bf16[1536,128]{1,0:T(8,128)(2,1)S(1)}, u32[]{:S(2)}, u32[]{:S(2)}) %collective-permute-start.11) | collective-permute-done | bytes 393248 | tf_op jit(solution)/shard_map/ppermute | solution.py:35
  62.0 1.2 %collective-permute-done.10.refs_3_ = bf16[512,128]{1,0:T(8,128)(2,1)S(1)} collective-permute-done((bf16[512,128]{1,0:T(8,128)(2,1)S(1)}, bf16[512,128]{1,0:T(8,128)(2,1)S(1)}, u32[]{:S(2)}, u32[]{:S(2)}) %collective-permute-start.10) | collective-permute-done | bytes 131104 | tf_op jit(solution)/shard_map/ppermute | solution.py:31
  66.2 6.1 %collective-permute-start.14 = (bf16[528,128]{1,0:T(8,128)(2,1)S(1)}, bf16[528,128]{1,0:T(8,128)(2,1)S(1)}, u32[]{:S(2)}, u32[]{:S(2)}) collective-permute-start(bf16[528,128]{1,0:T(8,128)(2,1)S(1)} %sent_tiles.1.a.refs_0_), channel_id=1, source_target_pairs={{0,16},{16,0},{32,48},{48,32},{64,80},{80,64},{96,112},{112,96},{1... | collective-permute-start | bytes 405512 | tf_op jit(solution)/shard_map/ppermute | solution.py:44
  72.3 1.4 %collective-permute-start.22 = (bf16[128,2048]{1,0:T(8,128)(2,1)S(1)}, bf16[128,2048]{1,0:T(8,128)(2,1)S(1)}, u32[]{:S(2)}, u32[]{:S(2)}) collective-permute-start(bf16[128,2048]{1,0:T(8,128)(2,1)S(1)} %get-tuple-element.63), channel_id=1, source_target_pairs={{0,3},{1,0},{2,1},{3,2},{4,7},{5,4},{6,5},{7,6},{8,11},{9,8},{10,9... | collective-permute-start | bytes 1572872 | tf_op jit(solution)/shard_map/ppermute | solution.py:35
  73.8 5.9 %collective-permute-start.16 = (bf16[1056,128]{1,0:T(8,128)(2,1)S(1)}, bf16[1056,128]{1,0:T(8,128)(2,1)S(1)}, u32[]{:S(2)}, u32[]{:S(2)}) collective-permute-start(bf16[1056,128]{1,0:T(8,128)(2,1)S(1)} %pair.1), channel_id=1, source_target_pairs={{0,64},{32,96},{64,128},{96,160},{128,192},{160,224},{192,0},{224,... | collective-permute-start | bytes 811016 | tf_op jit(solution)/shard_map/ppermute | solution.py:40
  80.2 2.6 %collective-permute-start.20 = (bf16[128,2048]{1,0:T(8,128)(2,1)S(1)}, bf16[128,2048]{1,0:T(8,128)(2,1)S(1)}, u32[]{:S(2)}, u32[]{:S(2)}) collective-permute-start(bf16[128,2048]{1,0:T(8,128)(2,1)S(1)} %get-tuple-element.58), channel_id=1, source_target_pairs={{0,12},{1,13},{2,14},{3,15},{4,0},{5,1},{6,2},{7,3},{8,4},{9,5},{1... | collective-permute-start | bytes 1572872 | tf_op jit(solution)/shard_map/ppermute | solution.py:31
  83.3 2.7 %collective-permute-done.16.ref.refs_2_ = bf16[1056,128]{1,0:T(8,128)(2,1)S(1)} collective-permute-done((bf16[1056,128]{1,0:T(8,128)(2,1)S(1)}, bf16[1056,128]{1,0:T(8,128)(2,1)S(1)}, u32[]{:S(2)}, u32[]{:S(2)}) %collective-permute-start.16) | collective-permute-done | bytes 270368 | tf_op jit(solution)/shard_map/ppermute | solution.py:40
  86.0 2.2 %collective-permute-start.17 = (bf16[1056,128]{1,0:T(8,128)(2,1)S(1)}, bf16[1056,128]{1,0:T(8,128)(2,1)S(1)}, u32[]{:S(2)}, u32[]{:S(2)}) collective-permute-start(bf16[1056,128]{1,0:T(8,128)(2,1)S(1)} %collective-permute-done.16.ref.refs_2_), channel_id=1, source_target_pairs={{0,32},{32,64},{64,96},{96,128},{128,160},{160,192},{192,224},{224... | collective-permute-start | bytes 811016 | tf_op jit(solution)/shard_map/ppermute | solution.py:40
  88.2 3.5 %collective-permute-start.18 = (bf16[528,128]{1,0:T(8,128)(2,1)S(1)}, bf16[528,128]{1,0:T(8,128)(2,1)S(1)}, u32[]{:S(2)}, u32[]{:S(2)}) collective-permute-start(bf16[528,128]{1,0:T(8,128)(2,1)S(1)} %own_half.1), channel_id=1, source_target_pairs={{0,64},{32,96},{64,128},{96,160},{128,192},{160,224},{192,0},{224,... | collective-permute-start | bytes 405512 | tf_op jit(solution)/shard_map/ppermute | solution.py:40
  91.7 2.9 %keep_error.2 = (bf16[128,4096]{1,0:T(8,128)(2,1)}, f32[8,128]{1,0:T(8,128)}) custom-call(s32[4]{0:T(128)S(1)} %bitcast.28, f32[128,2048]{1,0:T(8,128)S(1)} %get-tuple-element.59.g0, bf16[128,2048]{1,0:T(8,128)(2,1)S(1)} %collective-permute-done.21.g1, bf16[128,2048]{1,0:T(8,128)(2,1)S(1)} %collective-permute-done.22.g2, bf16[128,4096]{1,0:T(8,128)(2,1)S(1)} %bitcast.13, ...), custom_call_target="tpu_custom_call" | custom-call | flops 5242880 | bytes 5242880 | tf_op jit(solution)/shard_map/keep_error/pallas_call | solution.py:387
  94.7 2.6 %keep_error.3 = (bf16[128,4096]{1,0:T(8,128)(2,1)}, f32[8,128]{1,0:T(8,128)S(1)}) custom-call(s32[4]{0:T(128)S(1)} %bitcast.29, f32[128,2048]{1,0:T(8,128)S(1)} %get-tuple-element.54.g0, bf16[128,2048]{1,0:T(8,128)(2,1)S(1)} %collective-permute-done.19.g1, bf16[128,2048]{1,0:T(8,128)(2,1)S(1)} %collective-permute-done.20.g2, ...), custom_call_target="tpu_custom_call", output_to_operand_aliasing={{0}: (8, {})} | custom-call | flops 5242880 | bytes 5242880 | tf_op jit(solution)/shard_map/keep_error/pallas_call | solution.py:387
  98.6 2.3 %collective-permute-done.23.o_ref = bf16[128,4096]{1,0:T(8,128)(2,1)S(1)} collective-permute-done((bf16[128,4096]{1,0:T(8,128)(2,1)S(1)}, bf16[128,4096]{1,0:T(8,128)(2,1)S(1)}, u32[]{:S(2)}, u32[]{:S(2)}) %collective-permute-start.23) | collective-permute-done | bytes 1048608 | tf_op jit(solution)/shard_map/ppermute | solution.py:44
  100.9 1.9 %outer.1 = (f32[128,4096]{1,0:T(8,128)}, bf16[128,4096]{1,0:T(8,128)(2,1)}) custom-call(bf16[128,4096]{1,0:T(8,128)(2,1)S(1)} %add_tiles.1.m_ref, bf16[128,4096]{1,0:T(8,128)(2,1)S(1)} %collective-permute-done.23.o_ref, f32[128,4096]{1,0:T(8,128)S(1)} %copy-done, bf16[128,4096]{1,0:T(8,128)(2,1)S(1)} %copy-done.6), custom_call_target="tpu_custom_call" | custom-call | flops 3145728 | bytes 8388608 | tf_op jit(solution)/shard_map/outer/pallas_call | solution.py:455
  (53 shorter events, 10.6 us)
Async XLA Ops:
  1.4 1.1 %copy-start.5 = (bf16[1,3072,128]{2,1,0:T(8,128)(2,1)S(1)}, bf16[1,3072,128]{2,1,0:T(8,128)(2,1)}, u32[]{:S(2)}) copy-start(bf16[1,3072,128]{2,1,0:T(8,128)(2,1)} %param.9) | copy-start | bytes 2359300
  4.6 24.8 %collective-permute-start = (bf16[4240,128]{1,0:T(8,128)(2,1)S(1)}, bf16[4240,128]{1,0:T(8,128)(2,1)S(1)}, u32[]{:S(2)}, u32[]{:S(2)}) collective-permute-start(bf16[4240,128]{1,0:T(8,128)(2,1)S(1)} %get-tuple-element.36), channel_id=1, source_target_pairs={{0,4},{1,5},{2,6},{3,7},{4,8},{5,9},{6,10},{7,11},{8,12},{9,13},{1... | collective-permute-start | bytes 3256328 | tf_op jit(solution)/shard_map/ppermute | solution.py:31
  6.7 24.6 %collective-permute-start.1 = (bf16[4240,128]{1,0:T(8,128)(2,1)S(1)}, bf16[4240,128]{1,0:T(8,128)(2,1)S(1)}, u32[]{:S(2)}, u32[]{:S(2)}) collective-permute-start(bf16[4240,128]{1,0:T(8,128)(2,1)S(1)} %get-tuple-element.37), channel_id=1, source_target_pairs={{0,12},{1,13},{2,14},{3,15},{4,0},{5,1},{6,2},{7,3},{8,4},{9,5},{1... | collective-permute-start | bytes 3256328 | tf_op jit(solution)/shard_map/ppermute | solution.py:31
  8.0 25.0 %collective-permute-start.2 = (bf16[4240,128]{1,0:T(8,128)(2,1)S(1)}, bf16[4240,128]{1,0:T(8,128)(2,1)S(1)}, u32[]{:S(2)}, u32[]{:S(2)}) collective-permute-start(bf16[4240,128]{1,0:T(8,128)(2,1)S(1)} %get-tuple-element.38), channel_id=1, source_target_pairs={{0,1},{1,2},{2,3},{3,0},{4,5},{5,6},{6,7},{7,4},{8,9},{9,10},{10,1... | collective-permute-start | bytes 3256328 | tf_op jit(solution)/shard_map/ppermute | solution.py:35
  9.4 26.4 %collective-permute-start.3 = (bf16[4240,128]{1,0:T(8,128)(2,1)S(1)}, bf16[4240,128]{1,0:T(8,128)(2,1)S(1)}, u32[]{:S(2)}, u32[]{:S(2)}) collective-permute-start(bf16[4240,128]{1,0:T(8,128)(2,1)S(1)} %get-tuple-element.39), channel_id=1, source_target_pairs={{0,3},{1,0},{2,1},{3,2},{4,7},{5,4},{6,5},{7,6},{8,11},{9,8},{10,9... | collective-permute-start | bytes 3256328 | tf_op jit(solution)/shard_map/ppermute | solution.py:35
  29.4 12.1 %collective-permute-start.4 = (bf16[1936,128]{1,0:T(8,128)(2,1)S(1)}, bf16[1936,128]{1,0:T(8,128)(2,1)S(1)}, u32[]{:S(2)}, u32[]{:S(2)}) collective-permute-start(bf16[1936,128]{1,0:T(8,128)(2,1)S(1)} %relay.4), channel_id=1, source_target_pairs={{0,4},{1,5},{2,6},{3,7},{4,8},{5,9},{6,10},{7,11},{8,12},{9,13},{1... | collective-permute-start | bytes 1486856 | tf_op jit(solution)/shard_map/ppermute | solution.py:31
  31.4 10.8 %collective-permute-start.5 = (bf16[1936,128]{1,0:T(8,128)(2,1)S(1)}, bf16[1936,128]{1,0:T(8,128)(2,1)S(1)}, u32[]{:S(2)}, u32[]{:S(2)}) collective-permute-start(bf16[1936,128]{1,0:T(8,128)(2,1)S(1)} %relay.5), channel_id=1, source_target_pairs={{0,12},{1,13},{2,14},{3,15},{4,0},{5,1},{6,2},{7,3},{8,4},{9,5},{1... | collective-permute-start | bytes 1486856 | tf_op jit(solution)/shard_map/ppermute | solution.py:31
  33.1 4.4 %copy-start.1 = (bf16[1,192,4096]{2,1,0:T(8,128)(2,1)S(1)}, bf16[1,192,4096]{2,1,0:T(8,128)(2,1)}, u32[]{:S(2)}) copy-start(bf16[1,192,4096]{2,1,0:T(8,128)(2,1)} %param.8) | copy-start | bytes 4718596
  33.1 4.4 %copy-start.7 = (s32[1,1,4]{2,1,0:T(1,128)S(1)}, s32[1,1,4]{2,1,0:T(1,128)}, u32[]{:S(2)}) copy-start(s32[1,1,4]{2,1,0:T(1,128)} %param.15) | copy-start | bytes 52
  33.1 13.7 %collective-permute-start.6 = (bf16[1936,128]{1,0:T(8,128)(2,1)S(1)}, bf16[1936,128]{1,0:T(8,128)(2,1)S(1)}, u32[]{:S(2)}, u32[]{:S(2)}) collective-permute-start(bf16[1936,128]{1,0:T(8,128)(2,1)S(1)} %relay.6), channel_id=1, source_target_pairs={{0,1},{1,2},{2,3},{3,0},{4,5},{5,6},{6,7},{7,4},{8,9},{9,10},{10,1... | collective-permute-start | bytes 1486856 | tf_op jit(solution)/shard_map/ppermute | solution.py:35
  35.9 10.9 %collective-permute-start.7 = (bf16[1936,128]{1,0:T(8,128)(2,1)S(1)}, bf16[1936,128]{1,0:T(8,128)(2,1)S(1)}, u32[]{:S(2)}, u32[]{:S(2)}) collective-permute-start(bf16[1936,128]{1,0:T(8,128)(2,1)S(1)} %relay.7), channel_id=1, source_target_pairs={{0,3},{1,0},{2,1},{3,2},{4,7},{5,4},{6,5},{7,6},{8,11},{9,8},{10,9... | collective-permute-start | bytes 1486856 | tf_op jit(solution)/shard_map/ppermute | solution.py:35
  49.5 9.0 %collective-permute-start.8 = (bf16[1536,128]{1,0:T(8,128)(2,1)S(1)}, bf16[1536,128]{1,0:T(8,128)(2,1)S(1)}, u32[]{:S(2)}, u32[]{:S(2)}) collective-permute-start(bf16[1536,128]{1,0:T(8,128)(2,1)S(1)} %get-tuple-element.45), channel_id=1, source_target_pairs={{0,4},{1,5},{2,6},{3,7},{4,8},{5,9},{6,10},{7,11},{8,12},{9,13},{1... | collective-permute-start | bytes 1179656 | tf_op jit(solution)/shard_map/ppermute | solution.py:31
  49.6 15.7 %copy-start.2 = (bf16[1,128,4096]{2,1,0:T(8,128)(2,1)S(1)}, bf16[1,128,4096]{2,1,0:T(8,128)(2,1)}, u32[]{:S(2)}) copy-start(bf16[1,128,4096]{2,1,0:T(8,128)(2,1)} %param.11) | copy-start | bytes 3145732
  49.6 15.7 %copy-start.3 = (bf16[1,128,4096]{2,1,0:T(8,128)(2,1)S(1)}, bf16[1,128,4096]{2,1,0:T(8,128)(2,1)}, u32[]{:S(2)}) copy-start(bf16[1,128,4096]{2,1,0:T(8,128)(2,1)} %param.12) | copy-start | bytes 3145732
  49.6 15.7 %copy-start.4 = (bf16[1,128,4096]{2,1,0:T(8,128)(2,1)S(1)}, bf16[1,128,4096]{2,1,0:T(8,128)(2,1)}, u32[]{:S(2)}) copy-start(bf16[1,128,4096]{2,1,0:T(8,128)(2,1)} %param.13) | copy-start | bytes 3145732
  52.4 9.2 %collective-permute-start.11 = (bf16[1536,128]{1,0:T(8,128)(2,1)S(1)}, bf16[1536,128]{1,0:T(8,128)(2,1)S(1)}, u32[]{:S(2)}, u32[]{:S(2)}) collective-permute-start(bf16[1536,128]{1,0:T(8,128)(2,1)S(1)} %get-tuple-element.51), channel_id=1, source_target_pairs={{0,1},{1,2},{2,3},{3,0},{4,5},{5,6},{6,7},{7,4},{8,9},{9,10},{10,1... | collective-permute-start | bytes 1179656 | tf_op jit(solution)/shard_map/ppermute | solution.py:35
  53.5 8.0 %collective-permute-start.12 = (bf16[1536,128]{1,0:T(8,128)(2,1)S(1)}, bf16[1536,128]{1,0:T(8,128)(2,1)S(1)}, u32[]{:S(2)}, u32[]{:S(2)}) collective-permute-start(bf16[1536,128]{1,0:T(8,128)(2,1)S(1)} %get-tuple-element.52), channel_id=1, source_target_pairs={{0,3},{1,0},{2,1},{3,2},{4,7},{5,4},{6,5},{7,6},{8,11},{9,8},{10,9... | collective-permute-start | bytes 1179656 | tf_op jit(solution)/shard_map/ppermute | solution.py:35
  55.3 9.1 %collective-permute-start.9 = (bf16[1536,128]{1,0:T(8,128)(2,1)S(1)}, bf16[1536,128]{1,0:T(8,128)(2,1)S(1)}, u32[]{:S(2)}, u32[]{:S(2)}) collective-permute-start(bf16[1536,128]{1,0:T(8,128)(2,1)S(1)} %get-tuple-element.46), channel_id=1, source_target_pairs={{0,12},{1,13},{2,14},{3,15},{4,0},{5,1},{6,2},{7,3},{8,4},{9,5},{1... | collective-permute-start | bytes 1179656 | tf_op jit(solution)/shard_map/ppermute | solution.py:31
  57.9 5.3 %collective-permute-start.10 = (bf16[512,128]{1,0:T(8,128)(2,1)S(1)}, bf16[512,128]{1,0:T(8,128)(2,1)S(1)}, u32[]{:S(2)}, u32[]{:S(2)}) collective-permute-start(bf16[512,128]{1,0:T(8,128)(2,1)S(1)} %get-tuple-element.47), channel_id=1, source_target_pairs={{0,8},{1,9},{2,10},{3,11},{4,12},{5,13},{6,14},{7,15},{8,0},{9,1},... | collective-permute-start | bytes 393224 | tf_op jit(solution)/shard_map/ppermute | solution.py:31
  58.5 6.8 %copy-start = (f32[128,4096]{1,0:T(8,128)S(1)}, f32[128,4096]{1,0:T(8,128)}, u32[]{:S(2)}) copy-start(f32[128,4096]{1,0:T(8,128)} %w_ref.5) | copy-start | bytes 6291460
  58.5 6.8 %collective-permute-start.13 = (bf16[512,128]{1,0:T(8,128)(2,1)S(1)}, bf16[512,128]{1,0:T(8,128)(2,1)S(1)}, u32[]{:S(2)}, u32[]{:S(2)}) collective-permute-start(bf16[512,128]{1,0:T(8,128)(2,1)S(1)} %tied.1), channel_id=1, source_target_pairs={{0,2},{1,3},{2,0},{3,1},{4,6},{5,7},{6,4},{7,5},{8,10},{9,11},{10,... | collective-permute-start | bytes 393224 | tf_op jit(solution)/shard_map/ppermute | solution.py:35
  61.8 20.9 %collective-permute-start.21 = (bf16[128,2048]{1,0:T(8,128)(2,1)S(1)}, bf16[128,2048]{1,0:T(8,128)(2,1)S(1)}, u32[]{:S(2)}, u32[]{:S(2)}) collective-permute-start(bf16[128,2048]{1,0:T(8,128)(2,1)S(1)} %get-tuple-element.62), channel_id=1, source_target_pairs={{0,1},{1,2},{2,3},{3,0},{4,5},{5,6},{6,7},{7,4},{8,9},{9,10},{10,1... | collective-permute-start | bytes 1572872 | tf_op jit(solution)/shard_map/ppermute | solution.py:35
  66.2 7.6 %collective-permute-start.14 = (bf16[528,128]{1,0:T(8,128)(2,1)S(1)}, bf16[528,128]{1,0:T(8,128)(2,1)S(1)}, u32[]{:S(2)}, u32[]{:S(2)}) collective-permute-start(bf16[528,128]{1,0:T(8,128)(2,1)S(1)} %sent_tiles.1.a.refs_0_), channel_id=1, source_target_pairs={{0,16},{16,0},{32,48},{48,32},{64,80},{80,64},{96,112},{112,96},{1... | collective-permute-start | bytes 405512 | tf_op jit(solution)/shard_map/ppermute | solution.py:44
  72.3 15.8 %collective-permute-start.22 = (bf16[128,2048]{1,0:T(8,128)(2,1)S(1)}, bf16[128,2048]{1,0:T(8,128)(2,1)S(1)}, u32[]{:S(2)}, u32[]{:S(2)}) collective-permute-start(bf16[128,2048]{1,0:T(8,128)(2,1)S(1)} %get-tuple-element.63), channel_id=1, source_target_pairs={{0,3},{1,0},{2,1},{3,2},{4,7},{5,4},{6,5},{7,6},{8,11},{9,8},{10,9... | collective-permute-start | bytes 1572872 | tf_op jit(solution)/shard_map/ppermute | solution.py:35
  73.8 12.2 %collective-permute-start.16 = (bf16[1056,128]{1,0:T(8,128)(2,1)S(1)}, bf16[1056,128]{1,0:T(8,128)(2,1)S(1)}, u32[]{:S(2)}, u32[]{:S(2)}) collective-permute-start(bf16[1056,128]{1,0:T(8,128)(2,1)S(1)} %pair.1), channel_id=1, source_target_pairs={{0,64},{32,96},{64,128},{96,160},{128,192},{160,224},{192,0},{224,... | collective-permute-start | bytes 811016 | tf_op jit(solution)/shard_map/ppermute | solution.py:40
  80.0 14.7 %collective-permute-start.19 = (bf16[128,2048]{1,0:T(8,128)(2,1)S(1)}, bf16[128,2048]{1,0:T(8,128)(2,1)S(1)}, u32[]{:S(2)}, u32[]{:S(2)}) collective-permute-start(bf16[128,2048]{1,0:T(8,128)(2,1)S(1)} %get-tuple-element.57), channel_id=1, source_target_pairs={{0,4},{1,5},{2,6},{3,7},{4,8},{5,9},{6,10},{7,11},{8,12},{9,13},{1... | collective-permute-start | bytes 1572872 | tf_op jit(solution)/shard_map/ppermute | solution.py:31
  80.2 14.5 %collective-permute-start.20 = (bf16[128,2048]{1,0:T(8,128)(2,1)S(1)}, bf16[128,2048]{1,0:T(8,128)(2,1)S(1)}, u32[]{:S(2)}, u32[]{:S(2)}) collective-permute-start(bf16[128,2048]{1,0:T(8,128)(2,1)S(1)} %get-tuple-element.58), channel_id=1, source_target_pairs={{0,12},{1,13},{2,14},{3,15},{4,0},{5,1},{6,2},{7,3},{8,4},{9,5},{1... | collective-permute-start | bytes 1572872 | tf_op jit(solution)/shard_map/ppermute | solution.py:31
  82.7 14.5 %collective-permute-start.15 = (bf16[1056,128]{1,0:T(8,128)(2,1)S(1)}, bf16[1056,128]{1,0:T(8,128)(2,1)S(1)}, u32[]{:S(2)}, u32[]{:S(2)}) collective-permute-start(bf16[1056,128]{1,0:T(8,128)(2,1)S(1)} %pair.1), channel_id=1, source_target_pairs={{0,32},{32,64},{64,96},{96,128},{128,160},{160,192},{192,224},{224... | collective-permute-start | bytes 811016 | tf_op jit(solution)/shard_map/ppermute | solution.py:40
  86.0 11.3 %collective-permute-start.17 = (bf16[1056,128]{1,0:T(8,128)(2,1)S(1)}, bf16[1056,128]{1,0:T(8,128)(2,1)S(1)}, u32[]{:S(2)}, u32[]{:S(2)}) collective-permute-start(bf16[1056,128]{1,0:T(8,128)(2,1)S(1)} %collective-permute-done.16.ref.refs_2_), channel_id=1, source_target_pairs={{0,32},{32,64},{64,96},{96,128},{128,160},{160,192},{192,224},{224... | collective-permute-start | bytes 811016 | tf_op jit(solution)/shard_map/ppermute | solution.py:40
  88.2 9.1 %collective-permute-start.18 = (bf16[528,128]{1,0:T(8,128)(2,1)S(1)}, bf16[528,128]{1,0:T(8,128)(2,1)S(1)}, u32[]{:S(2)}, u32[]{:S(2)}) collective-permute-start(bf16[528,128]{1,0:T(8,128)(2,1)S(1)} %own_half.1), channel_id=1, source_target_pairs={{0,64},{32,96},{64,128},{96,160},{128,192},{160,224},{192,0},{224,... | collective-permute-start | bytes 405512 | tf_op jit(solution)/shard_map/ppermute | solution.py:40
  97.2 3.7 %copy-start.6 = (bf16[128,4096]{1,0:T(8,128)(2,1)S(1)}, bf16[128,4096]{1,0:T(8,128)(2,1)}, u32[]{:S(2)}) copy-start(bf16[128,4096]{1,0:T(8,128)(2,1)} %v_ref.1) | copy-start | bytes 3145732
  98.1 2.9 %collective-permute-start.23 = (bf16[128,4096]{1,0:T(8,128)(2,1)S(1)}, bf16[128,4096]{1,0:T(8,128)(2,1)S(1)}, u32[]{:S(2)}, u32[]{:S(2)}) collective-permute-start(bf16[128,4096]{1,0:T(8,128)(2,1)S(1)} %add_tiles.1.m_ref), channel_id=1, source_target_pairs={{0,16},{16,0},{32,48},{48,32},{64,80},{80,64},{96,112},{112,96},{1... | collective-permute-start | bytes 3145736 | tf_op jit(solution)/shard_map/ppermute | solution.py:44
